TPU v7x, 1024 devices: a whole 4x8x16 slice. The times are simulated.
1024 devices in a mesh: gx: 8 (over y), gy: 16 (over z), gz: 8 (over x, core).
Axes of the slice: x: 4, y: 8, z: 16, core: 2. Of those that a mesh axis runs over, the one named last changes fastest.
Arguments:
- right_side: float32 [32, 32, 4096], P('gx', 'gy', 'gz'), may hold values from -24 to 24
- element_class: int32 [32, 32, 64], P('gx', 'gy', 'gz'), may hold values from 0 to 15
- class_blocks: float32 [16, 64, 64], replicated, may hold values from -0.05 to 11, as said below
- class_shift: float32 [16], replicated, may hold values from 0.5 to 4
- face_weights: float32 [3], replicated, may hold values from 0.4 to 0.9
Outputs:
- solution_field: float32 [32, 32, 4096], P('gx', 'gy', 'gz')
- residual: float32 [32, 32, 4096], P('gx', 'gy', 'gz')
Inputs may be any that keep to these rules, and one draw needn't show every extreme that they name: `class_blocks`: each block is symmetric, and each diagonal entry exceeds the sum of magnitudes of the other entries of its row by 3 or more.
All inputs are finite; a program needn't handle non-finite values.
Results may differ from a plain program's by a relative error of at most 0.00027.
Values sent between devices are 32-bit elements; how exact they have to be, the bound alone decides.
No kernel may reach another device: no remote copies, remote signals or barrier semaphores. Data moves between devices by JAX's collectives and lax.ppermute only.
A program may use at most 32 MiB of HBM per device.

v0:
```python
import jax
import jax.numpy as jnp
import numpy as np
from jax import lax
from jax.sharding import PartitionSpec as P

P_SIZE = 64
SWEEPS = 4


highest = lax.Precision.HIGHEST
relax_weight = 0.6


def with_halo(x, sides, width):
    for axis, dim in sides:
        size, length = (lax.axis_size(axis), x.shape[dim])
        up = [(i, (i + 1) % size) for i in range(size - 1)]
        down = [(j, i) for i, j in up]
        last = lax.slice_in_dim(x, length - width, length, axis=dim)
        first = lax.slice_in_dim(x, 0, width, axis=dim)
        before = lax.ppermute(last, axis, up)
        after = lax.ppermute(first, axis, down)
        x = jnp.concatenate([before, x, after], axis=dim)
    return x


def partner_2(x, axis, bit):
    return lax.ppermute(x, axis, [(i, i ^ 1 << bit) for i in range(lax.axis_size(axis))])


def face_tables():
    node_ids = np.arange(P_SIZE)
    digits = (node_ids // 16, node_ids // 4 % 4, node_ids % 4)
    strides = (48, 12, 3)
    lower_sets = [node_ids[digits[axis_dim] == 0] for axis_dim in range(3)]
    return (lower_sets, strides)


def full_matrix(face_weights):
    lower_sets, strides = face_tables()
    pieces = []
    for axis_dim in range(3):
        lower_ids = lower_sets[axis_dim]
        upper_ids = lower_ids + strides[axis_dim]
        from_next = np.zeros((P_SIZE, P_SIZE), np.float32)
        from_next[lower_ids, upper_ids] = 1.0
        from_prev = np.zeros((P_SIZE, P_SIZE), np.float32)
        from_prev[upper_ids, lower_ids] = 1.0
        pieces.append(face_weights[axis_dim] * jnp.asarray(from_next))
        pieces.append(face_weights[axis_dim] * jnp.asarray(from_prev))
    return jnp.concatenate(pieces, axis=0)


def couple_full(cubes, face_weights):
    count = cubes.shape[0] * cubes.shape[1] * cubes.shape[2]
    padded = with_halo(cubes, (("gx", 0), ("gy", 1), ("gz", 2)), 1)
    views = [
        padded[2:, 1:-1, 1:-1],
        padded[:-2, 1:-1, 1:-1],
        padded[1:-1, 2:, 1:-1],
        padded[1:-1, :-2, 1:-1],
        padded[1:-1, 1:-1, 2:],
        padded[1:-1, 1:-1, :-2],
    ]
    stacked = jnp.concatenate(views, axis=3).reshape(count, 6 * P_SIZE)
    return jnp.dot(stacked, full_matrix(face_weights), precision=highest)


def coarsen(values):
    size_x, size_y, size_z = values.shape
    return values.reshape(size_x // 2, 2, size_y // 2, 2, size_z // 2, 2).sum(axis=(1, 3, 5))


def refine(values):
    return jnp.repeat(jnp.repeat(jnp.repeat(values, 2, axis=0), 2, axis=1), 2, axis=2)


def section_apply(values, shift):
    padded = jnp.pad(values, ((1, 1), (1, 1), (1, 1)))
    beside = padded[2:, 1:-1, 1:-1] + padded[:-2, 1:-1, 1:-1]
    beside = beside + padded[1:-1, 2:, 1:-1] + padded[1:-1, :-2, 1:-1]
    beside = beside + padded[1:-1, 1:-1, 2:] + padded[1:-1, 1:-1, :-2]
    return (6.0 + shift) * values - beside


def assemble(stacked, depth, layout):
    undo_list = []
    for axis_dim, axis_count, bit_offset, my_index in layout:
        partner = partner_2(stacked, ("gx", "gy", "gz"), bit_offset + depth - 1)
        upper_half = my_index >> depth - 1 & 1 == 1
        half_size = stacked.shape[axis_dim + 1]
        low_first = jnp.concatenate([stacked, partner], axis_dim + 1)
        high_first = jnp.concatenate([partner, stacked], axis_dim + 1)
        stacked = jnp.where(upper_half, high_first, low_first)
        undo_list.append((axis_dim, upper_half, half_size))
    return (stacked, undo_list)


def unpick(values, undo_list):
    for axis_dim, upper_half, half_size in reversed(undo_list):
        values = lax.dynamic_slice_in_dim(
            values, upper_half.astype(jnp.int32) * half_size, half_size, axis_dim
        )
    return values


def fine_apply(field, operator):
    onehot, wide_blocks, face_weights = operator
    size_x, size_y, width = field.shape
    size_z = width // P_SIZE
    count = size_x * size_y * size_z
    classes = onehot.shape[1]
    flat = field.reshape(count, P_SIZE)
    products = jnp.dot(flat, wide_blocks, precision=highest).reshape(count, classes, P_SIZE)
    local_part = jnp.einsum("ekn,ek->en", products, onehot, precision=highest)
    cubes = field.reshape(size_x, size_y, size_z, P_SIZE)
    nearby = couple_full(cubes, face_weights)
    return (local_part - nearby).reshape(size_x, size_y, width)


def section_cycle(source, shift, depth, layout):
    diagonal = 6.0 + shift
    if depth == 3:
        iterate = jnp.zeros_like(source)
        for sweep_index in range(SWEEPS):
            iterate = iterate + relax_weight * (source - section_apply(iterate, shift)) / diagonal
        return iterate
    iterate = relax_weight * source / diagonal
    remainder = source - section_apply(iterate, shift)
    gathered, undo_list = assemble(
        jnp.stack([0.25 * coarsen(remainder), 0.125 * coarsen(shift)]), depth + 1, layout
    )
    coarse = section_cycle(gathered[0], gathered[1], depth + 1, layout)
    iterate = iterate + refine(unpick(coarse, undo_list))
    return iterate + relax_weight * (source - section_apply(iterate, shift)) / diagonal


def precondition(source, context):
    operator, fine_diagonal, shift_cells, row_totals, layout = context
    iterate = relax_weight * source / fine_diagonal
    remainder = source - fine_apply(iterate, operator)
    size_x, size_y, width = source.shape
    sums = remainder.reshape(size_x, size_y, width // P_SIZE, P_SIZE).sum(axis=3)
    gathered, undo_list = assemble(
        jnp.stack([coarsen(sums) / float(P_SIZE), 0.125 * coarsen(shift_cells)]), 1, layout
    )
    coarse = section_cycle(gathered[0], gathered[1], 1, layout)
    correction = refine(unpick(coarse, undo_list))
    iterate = iterate + jnp.repeat(correction, P_SIZE, axis=2)
    update = source - fine_apply(iterate, operator)
    return iterate + relax_weight * update / fine_diagonal


def total(terms):
    return lax.psum(terms, ("gx", "gy", "gz"))


def per_device(right_side, element_class, class_blocks, class_shift, face_weights):
    size_x, size_y, width = right_side.shape
    size_z = width // P_SIZE
    classes = class_blocks.shape[0]
    element_count = size_x * size_y * size_z
    onehot = (
        element_class.reshape(element_count, 1) == jnp.arange(classes, dtype=jnp.int32)[None, :]
    ).astype(jnp.float32)
    wide_blocks = jnp.transpose(class_blocks, (2, 0, 1)).reshape(P_SIZE, classes * P_SIZE)
    operator = (onehot, wide_blocks, face_weights)
    diag_table = jnp.diagonal(class_blocks, axis1=1, axis2=2)
    fine_diagonal = jnp.dot(onehot, diag_table, precision=highest).reshape(size_x, size_y, width)
    shift_cells = jnp.dot(onehot, class_shift[:, None], precision=highest).reshape(
        size_x, size_y, size_z
    )
    row_totals = None
    bits_z = lax.axis_size("gz").bit_length() - 1
    bits_y = lax.axis_size("gy").bit_length() - 1
    layout = (
        (0, lax.axis_size("gx"), bits_z + bits_y, lax.axis_index("gx")),
        (1, lax.axis_size("gy"), bits_z, lax.axis_index("gy")),
        (2, lax.axis_size("gz"), 0, lax.axis_index("gz")),
    )
    context = (operator, fine_diagonal, shift_cells, row_totals, layout)
    residual = right_side
    smoothed = precondition(residual, context)
    gamma_now = total((jnp.sum(residual * smoothed),))[0]
    direction = smoothed
    image = fine_apply(direction, operator)
    step_size = gamma_now / total((jnp.sum(direction * image),))[0]
    solution_field = step_size * direction
    residual = residual - step_size * image
    smoothed = precondition(residual, context)
    gamma_next = total((jnp.sum(residual * smoothed),))[0]
    direction = smoothed + gamma_next / gamma_now * direction
    image = fine_apply(direction, operator)
    step_size = gamma_next / total((jnp.sum(direction * image),))[0]
    solution_field = solution_field + step_size * direction
    residual = residual - step_size * image
    return (solution_field, residual)


def solution(mesh):
    in_specs = (P("gx", "gy", "gz"), P("gx", "gy", "gz"), P(), P(), P())
    out_specs = (P("gx", "gy", "gz"), P("gx", "gy", "gz"))
    return jax.shard_map(
        per_device, mesh=mesh, in_specs=in_specs, out_specs=out_specs, check_vma=False
    )
```

profile of v0, /device:TPU:1, one launch (start us, length us, event | category | flops | bytes accessed | tf_op | source)
XLA Modules:
  0.0 670.3 jit_solution(3606315168053110778)
XLA Ops:
  4.0 4.0 collective-permute-start.1
  18.0 4.6 collective-permute-start.3
  23.9 4.5 collective-permute-start.5
  28.4 10.3 %collective-permute-start.4 = (f32[6,4,1,64]{3,2,1,0:T(1,128)S(1)}, f32[6,4,1,64]{3,2,1,0:T(1,128)S(1)}, u32[]{:S(2)}, u32[]{:S(2)}) collective-permute-start(f32[6,4,1,64]{3,2,1,0:T(1,128)S(1)} %get-tuple-element.33), channel_id=1, source_target_pairs={{1,0},{2,1},{3,2},{4,3},{5,4},{6,5},{7,6},{9,8},{10,9},{11,10},{12... | collective-permute-start | bytes 18440 | tf_op jit(solution)/shard_map/ppermute | solution.py:23
  40.4 4.3 collective-permute-start.6
  45.7 3.9 collective-permute-start.7
  50.6 4.0 collective-permute-start.8
  57.9 3.3 collective-permute-done.9
  61.2 3.1 collective-permute-start.10
  68.4 2.4 collective-permute-done.11
  71.4 4.2 collective-permute-start.12
  75.6 4.0 collective-permute-done.12
  79.7 7.5 %collective-permute-start.13 = (f32[2,4,1,4]{3,1,2,0:T(4,128)S(1)}, f32[2,4,1,4]{3,1,2,0:T(4,128)S(1)}, u32[]{:S(2)}, u32[]{:S(2)}) collective-permute-start(f32[2,4,1,4]{3,1,2,0:T(4,128)S(1)} %maximum_select_fusion.13), channel_id=1, source_target_pairs={{0,32},{1,33},{2,34},{3,35},{4,36},{5,37},{6,38},{7,39},{8,40},{9,... | collective-permute-start | bytes 392 | tf_op jit(solution)/shard_map/ppermute | solution.py:29
  88.2 4.9 collective-permute-start.14
  95.9 3.3 collective-permute-start.16
  100.8 3.1 collective-permute-done.15
  105.2 4.3 collective-permute-start.18
  111.1 10.5 %collective-permute-start.20 = (f32[6,4,1,64]{3,2,1,0:T(1,128)S(1)}, f32[6,4,1,64]{3,2,1,0:T(1,128)S(1)}, u32[]{:S(2)}, u32[]{:S(2)}) collective-permute-start(f32[6,4,1,64]{3,2,1,0:T(1,128)S(1)} %get-tuple-element.28), channel_id=1, source_target_pairs={{0,1},{1,2},{2,3},{3,4},{4,5},{5,6},{6,7},{8,9},{9,10},{10,11},{11... | collective-permute-start | bytes 18440 | tf_op jit(solution)/shard_map/ppermute | solution.py:22
  124.3 2.4 collective-permute-done.19
  127.3 3.1 collective-permute-start.22
  132.0 4.5 collective-permute-done.21
  137.8 4.4 collective-permute-start.24
  143.9 3.4 collective-permute-start.26
  149.9 2.4 collective-permute-done.25
  153.4 128.5 %all-reduce.15 = (f32[]{:T(128)}, f32[]{:T(128)}) all-reduce(f32[]{:T(128)} %get-tuple-element.3, f32[]{:T(128)} %get-tuple-element.2), channel_id=1, replica_groups=mesh['gx'=8,'gy'=16,'gz'=8] {'gx','gy','gz'}, use_global_device_ids=true, to_apply=%region_13.14 | all-reduce | flops 2 | bytes 16 | tf_op jit(solution)/shard_map/psum | solution.py:156
  286.2 4.8 collective-permute-done.27
  292.4 4.4 collective-permute-start.30
  298.4 4.7 collective-permute-start.32
  309.0 5.1 collective-permute-start.33
  315.1 3.6 collective-permute-start.34
  323.4 8.7 %collective-permute-start.36 = (f32[2,2,1,4]{3,1,2,0:T(2,128)S(1)}, f32[2,2,1,4]{3,1,2,0:T(2,128)S(1)}, u32[]{:S(2)}, u32[]{:S(2)}) collective-permute-start(f32[2,2,1,4]{3,1,2,0:T(2,128)S(1)} %pad_maximum_fusion.86), channel_id=1, source_target_pairs={{0,256},{1,257},{2,258},{3,259},{4,260},{5,261},{6,262},{7,263},{8... | collective-permute-start | bytes 200 | tf_op jit(solution)/shard_map/ppermute | solution.py:29
  333.1 4.8 collective-permute-start.37
  338.9 3.7 collective-permute-start.38
  344.2 4.9 collective-permute-start.39
  349.1 3.3 collective-permute-done.39
  352.5 6.4 collective-permute-start.40
  360.7 3.1 collective-permute-start.41
  363.9 2.8 collective-permute-done.41
  368.4 3.6 collective-permute-start.43
  373.5 3.1 collective-permute-done.42
  378.0 4.0 collective-permute-start.45
  383.6 11.9 %collective-permute-start.47 = (f32[6,4,1,64]{3,2,1,0:T(1,128)S(1)}, f32[6,4,1,64]{3,2,1,0:T(1,128)S(1)}, u32[]{:S(2)}, u32[]{:S(2)}) collective-permute-start(f32[6,4,1,64]{3,2,1,0:T(1,128)S(1)} %get-tuple-element.16), channel_id=1, source_target_pairs={{0,1},{1,2},{2,3},{3,4},{4,5},{5,6},{6,7},{8,9},{9,10},{10,11},{11... | collective-permute-start | bytes 18440 | tf_op jit(solution)/shard_map/ppermute | solution.py:22
  398.2 2.4 collective-permute-done.46
  401.7 120.3 %psum.30 = f32[]{:T(128)} all-reduce(f32[]{:T(128)} %get-tuple-element.6), channel_id=1, replica_groups=mesh['gx'=8,'gy'=16,'gz'=8] {'gx','gy','gz'}, use_global_device_ids=true, to_apply=%region_28.29 | all-reduce | flops 1 | bytes 8 | tf_op jit(solution)/shard_map/psum | solution.py:156
  526.3 3.1 collective-permute-done.48
  530.7 4.0 collective-permute-start.51
  536.3 5.9 collective-permute-start.53
  548.4 119.3 %psum.31 = f32[]{:T(128)} all-reduce(f32[]{:T(128)} %multiply_reduce_fusion), channel_id=1, replica_groups=mesh['gx'=8,'gy'=16,'gz'=8] {'gx','gy','gz'}, use_global_device_ids=true, to_apply=%region_30.31 | all-reduce | flops 1 | bytes 8 | tf_op jit(solution)/shard_map/psum | solution.py:156
  (347 shorter events, 91.0 us)
Async XLA Ops:
  4.0 12.7 %collective-permute-start.1 = (f32[1,2,8,64]{3,2,1,0:T(8,128)S(1)}, f32[1,2,8,64]{3,2,1,0:T(8,128)S(1)}, u32[]{:S(2)}, u32[]{:S(2)}) collective-permute-start(f32[1,2,8,64]{3,2,1,0:T(8,128)S(1)} %slice.646), channel_id=1, source_target_pairs={{0,128},{128,256},{256,384},{384,512},{512,640},{640,768},{768,896... | collective-permute-start | bytes 12296 | tf_op jit(solution)/shard_map/ppermute | solution.py:22
  8.1 8.6 %collective-permute-start = (f32[1,2,8,64]{3,2,1,0:T(8,128)S(1)}, f32[1,2,8,64]{3,2,1,0:T(8,128)S(1)}, u32[]{:S(2)}, u32[]{:S(2)}) collective-permute-start(f32[1,2,8,64]{3,2,1,0:T(8,128)S(1)} %slice.643), channel_id=1, source_target_pairs={{128,0},{256,128},{384,256},{512,384},{640,512},{768,640},{896,768... | collective-permute-start | bytes 12296 | tf_op jit(solution)/shard_map/ppermute | solution.py:23
  16.7 7.1 %collective-permute-start.2 = (f32[6,1,8,64]{3,2,1,0:T(8,128)S(1)}, f32[6,1,8,64]{3,2,1,0:T(8,128)S(1)}, u32[]{:S(2)}, u32[]{:S(2)}) collective-permute-start(f32[6,1,8,64]{3,2,1,0:T(8,128)S(1)} %get-tuple-element.57), channel_id=1, source_target_pairs={{8,0},{16,8},{24,16},{32,24},{40,32},{48,40},{56,48},{64,56},{72,6... | collective-permute-start | bytes 36872 | tf_op jit(solution)/shard_map/ppermute | solution.py:23
  18.0 5.8 collective-permute-start.3
  23.9 14.9 %collective-permute-start.5 = (f32[6,4,1,64]{3,2,1,0:T(1,128)S(1)}, f32[6,4,1,64]{3,2,1,0:T(1,128)S(1)}, u32[]{:S(2)}, u32[]{:S(2)}) collective-permute-start(f32[6,4,1,64]{3,2,1,0:T(1,128)S(1)} %get-tuple-element.32), channel_id=1, source_target_pairs={{0,1},{1,2},{2,3},{3,4},{4,5},{5,6},{6,7},{8,9},{9,10},{10,11},{11... | collective-permute-start | bytes 18440 | tf_op jit(solution)/shard_map/ppermute | solution.py:22
  28.4 11.1 %collective-permute-start.4 = (f32[6,4,1,64]{3,2,1,0:T(1,128)S(1)}, f32[6,4,1,64]{3,2,1,0:T(1,128)S(1)}, u32[]{:S(2)}, u32[]{:S(2)}) collective-permute-start(f32[6,4,1,64]{3,2,1,0:T(1,128)S(1)} %get-tuple-element.33), channel_id=1, source_target_pairs={{1,0},{2,1},{3,2},{4,3},{5,4},{6,5},{7,6},{9,8},{10,9},{11,10},{12... | collective-permute-start | bytes 18440 | tf_op jit(solution)/shard_map/ppermute | solution.py:23
  40.4 5.2 collective-permute-start.6
  45.7 4.9 collective-permute-start.7
  50.6 4.8 collective-permute-start.8
  56.0 5.2 collective-permute-start.9
  61.2 5.3 collective-permute-start.10
  71.4 8.2 %collective-permute-start.12 = (f32[2,2,1,4]{3,1,2,0:T(2,128)S(1)}, f32[2,2,1,4]{3,1,2,0:T(2,128)S(1)}, u32[]{:S(2)}, u32[]{:S(2)}) collective-permute-start(f32[2,2,1,4]{3,1,2,0:T(2,128)S(1)} %pad_maximum_fusion.85), channel_id=1, source_target_pairs={{0,512},{1,513},{2,514},{3,515},{4,516},{5,517},{6,518},{7,519},{8... | collective-permute-start | bytes 200 | tf_op jit(solution)/shard_map/ppermute | solution.py:29
  79.7 8.5 %collective-permute-start.13 = (f32[2,4,1,4]{3,1,2,0:T(4,128)S(1)}, f32[2,4,1,4]{3,1,2,0:T(4,128)S(1)}, u32[]{:S(2)}, u32[]{:S(2)}) collective-permute-start(f32[2,4,1,4]{3,1,2,0:T(4,128)S(1)} %maximum_select_fusion.13), channel_id=1, source_target_pairs={{0,32},{1,33},{2,34},{3,35},{4,36},{5,37},{6,38},{7,39},{8,40},{9,... | collective-permute-start | bytes 392 | tf_op jit(solution)/shard_map/ppermute | solution.py:29
  88.2 5.9 collective-permute-start.14
  95.9 4.9 collective-permute-start.16
  103.9 7.2 %collective-permute-start.17 = (f32[6,1,8,64]{3,2,1,0:T(8,128)S(1)}, f32[6,1,8,64]{3,2,1,0:T(8,128)S(1)}, u32[]{:S(2)}, u32[]{:S(2)}) collective-permute-start(f32[6,1,8,64]{3,2,1,0:T(8,128)S(1)} %get-tuple-element.55), channel_id=1, source_target_pairs={{8,0},{16,8},{24,16},{32,24},{40,32},{48,40},{56,48},{64,56},{72,6... | collective-permute-start | bytes 36872 | tf_op jit(solution)/shard_map/ppermute | solution.py:23
  105.2 5.9 collective-permute-start.18
  111.1 13.2 %collective-permute-start.20 = (f32[6,4,1,64]{3,2,1,0:T(1,128)S(1)}, f32[6,4,1,64]{3,2,1,0:T(1,128)S(1)}, u32[]{:S(2)}, u32[]{:S(2)}) collective-permute-start(f32[6,4,1,64]{3,2,1,0:T(1,128)S(1)} %get-tuple-element.28), channel_id=1, source_target_pairs={{0,1},{1,2},{2,3},{3,4},{4,5},{5,6},{6,7},{8,9},{9,10},{10,11},{11... | collective-permute-start | bytes 18440 | tf_op jit(solution)/shard_map/ppermute | solution.py:22
  121.7 5.0 collective-permute-start.19
  127.3 4.7 collective-permute-start.22
  130.7 5.8 collective-permute-start.21
  136.5 7.3 %collective-permute-start.23 = (f32[6,1,8,64]{3,2,1,0:T(8,128)S(1)}, f32[6,1,8,64]{3,2,1,0:T(8,128)S(1)}, u32[]{:S(2)}, u32[]{:S(2)}) collective-permute-start(f32[6,1,8,64]{3,2,1,0:T(8,128)S(1)} %get-tuple-element.53), channel_id=1, source_target_pairs={{8,0},{16,8},{24,16},{32,24},{40,32},{48,40},{56,48},{64,56},{72,6... | collective-permute-start | bytes 36872 | tf_op jit(solution)/shard_map/ppermute | solution.py:23
  137.8 6.1 collective-permute-start.24
  143.9 6.0 collective-permute-start.26
  147.3 5.0 collective-permute-start.25
  284.9 6.1 collective-permute-start.27
  291.1 7.4 %collective-permute-start.29 = (f32[6,1,8,64]{3,2,1,0:T(8,128)S(1)}, f32[6,1,8,64]{3,2,1,0:T(8,128)S(1)}, u32[]{:S(2)}, u32[]{:S(2)}) collective-permute-start(f32[6,1,8,64]{3,2,1,0:T(8,128)S(1)} %get-tuple-element.51), channel_id=1, source_target_pairs={{8,0},{16,8},{24,16},{32,24},{40,32},{48,40},{56,48},{64,56},{72,6... | collective-permute-start | bytes 36872 | tf_op jit(solution)/shard_map/ppermute | solution.py:23
  292.4 6.1 collective-permute-start.30
  298.4 7.3 %collective-permute-start.32 = (f32[6,4,1,64]{3,2,1,0:T(1,128)S(1)}, f32[6,4,1,64]{3,2,1,0:T(1,128)S(1)}, u32[]{:S(2)}, u32[]{:S(2)}) collective-permute-start(f32[6,4,1,64]{3,2,1,0:T(1,128)S(1)} %get-tuple-element.20), channel_id=1, source_target_pairs={{0,1},{1,2},{2,3},{3,4},{4,5},{5,6},{6,7},{8,9},{9,10},{10,11},{11... | collective-permute-start | bytes 18440 | tf_op jit(solution)/shard_map/ppermute | solution.py:22
  303.1 5.0 collective-permute-start.31
  309.0 6.1 collective-permute-start.33
  315.1 4.6 collective-permute-start.34
  323.4 9.7 %collective-permute-start.36 = (f32[2,2,1,4]{3,1,2,0:T(2,128)S(1)}, f32[2,2,1,4]{3,1,2,0:T(2,128)S(1)}, u32[]{:S(2)}, u32[]{:S(2)}) collective-permute-start(f32[2,2,1,4]{3,1,2,0:T(2,128)S(1)} %pad_maximum_fusion.86), channel_id=1, source_target_pairs={{0,256},{1,257},{2,258},{3,259},{4,260},{5,261},{6,262},{7,263},{8... | collective-permute-start | bytes 200 | tf_op jit(solution)/shard_map/ppermute | solution.py:29
  333.1 5.8 collective-permute-start.37
  338.9 4.8 collective-permute-start.38
  344.2 8.2 %collective-permute-start.39 = (f32[2,2,1,4]{3,1,2,0:T(2,128)S(1)}, f32[2,2,1,4]{3,1,2,0:T(2,128)S(1)}, u32[]{:S(2)}, u32[]{:S(2)}) collective-permute-start(f32[2,2,1,4]{3,1,2,0:T(2,128)S(1)} %pad_maximum_fusion.87), channel_id=1, source_target_pairs={{0,512},{1,513},{2,514},{3,515},{4,516},{5,517},{6,518},{7,519},{8... | collective-permute-start | bytes 200 | tf_op jit(solution)/shard_map/ppermute | solution.py:29
  352.5 8.3 %collective-permute-start.40 = (f32[2,4,1,4]{3,1,2,0:T(4,128)S(1)}, f32[2,4,1,4]{3,1,2,0:T(4,128)S(1)}, u32[]{:S(2)}, u32[]{:S(2)}) collective-permute-start(f32[2,4,1,4]{3,1,2,0:T(4,128)S(1)} %maximum_select_fusion.15), channel_id=1, source_target_pairs={{0,32},{1,33},{2,34},{3,35},{4,36},{5,37},{6,38},{7,39},{8,40},{9,... | collective-permute-start | bytes 392 | tf_op jit(solution)/shard_map/ppermute | solution.py:29
  360.7 5.9 collective-permute-start.41
  368.4 5.2 collective-permute-start.43
  376.7 6.9 %collective-permute-start.44 = (f32[6,1,8,64]{3,2,1,0:T(8,128)S(1)}, f32[6,1,8,64]{3,2,1,0:T(8,128)S(1)}, u32[]{:S(2)}, u32[]{:S(2)}) collective-permute-start(f32[6,1,8,64]{3,2,1,0:T(8,128)S(1)} %get-tuple-element.49), channel_id=1, source_target_pairs={{8,0},{16,8},{24,16},{32,24},{40,32},{48,40},{56,48},{64,56},{72,6... | collective-permute-start | bytes 36872 | tf_op jit(solution)/shard_map/ppermute | solution.py:23
  378.0 5.6 collective-permute-start.45
  383.6 14.5 %collective-permute-start.47 = (f32[6,4,1,64]{3,2,1,0:T(1,128)S(1)}, f32[6,4,1,64]{3,2,1,0:T(1,128)S(1)}, u32[]{:S(2)}, u32[]{:S(2)}) collective-permute-start(f32[6,4,1,64]{3,2,1,0:T(1,128)S(1)} %get-tuple-element.16), channel_id=1, source_target_pairs={{0,1},{1,2},{2,3},{3,4},{4,5},{5,6},{6,7},{8,9},{9,10},{10,11},{11... | collective-permute-start | bytes 18440 | tf_op jit(solution)/shard_map/ppermute | solution.py:22
  395.5 5.0 collective-permute-start.46
  525.0 4.4 collective-permute-start.48
  529.4 6.9 %collective-permute-start.50 = (f32[6,1,8,64]{3,2,1,0:T(8,128)S(1)}, f32[6,1,8,64]{3,2,1,0:T(8,128)S(1)}, u32[]{:S(2)}, u32[]{:S(2)}) collective-permute-start(f32[6,1,8,64]{3,2,1,0:T(8,128)S(1)} %get-tuple-element.47), channel_id=1, source_target_pairs={{8,0},{16,8},{24,16},{32,24},{40,32},{48,40},{56,48},{64,56},{72,6... | collective-permute-start | bytes 36872 | tf_op jit(solution)/shard_map/ppermute | solution.py:23
  530.7 5.6 collective-permute-start.51
  536.3 8.5 %collective-permute-start.53 = (f32[6,4,1,64]{3,2,1,0:T(1,128)S(1)}, f32[6,4,1,64]{3,2,1,0:T(1,128)S(1)}, u32[]{:S(2)}, u32[]{:S(2)}) collective-permute-start(f32[6,4,1,64]{3,2,1,0:T(1,128)S(1)} %get-tuple-element.12), channel_id=1, source_target_pairs={{0,1},{1,2},{2,3},{3,4},{4,5},{5,6},{6,7},{8,9},{9,10},{10,11},{11... | collective-permute-start | bytes 18440 | tf_op jit(solution)/shard_map/ppermute | solution.py:22
  542.3 5.0 collective-permute-start.52
  (17 other events, 149.0 us)
where the time goes:
time: 678 us; the launch traced here: 670 us
  blocking collectives  368 us (54%)
  starting transfers between devices  197 us (29%)
  waiting for transfers between devices  61.9 us (9%)
  matrix products  16.5 us (2%)
  other arithmetic  11.4 us (2%)
  local copies, waits for them, and re-layouts  9.4 us (1%)
    psum x3, blocking collectives, total(): return lax.psum(terms, ('gx', 'gy', 'gz'))  368 us
    ppermute x18, starting transfers between devices, with_halo(): before = lax.ppermute(last, axis, up)  83.3 us
    ppermute x18, starting transfers between devices, partner_2(): lax.ppermute(x, axis, [(i, i ^ 1 << bit) for i in range(lax.axis_size(axi...  77.9 us
    ppermute x18, starting transfers between devices, with_halo(): after = lax.ppermute(first, axis, down)  35.3 us
    ppermute x18, waiting for transfers between devices, with_halo(): after = lax.ppermute(first, axis, down)  31.3 us
    ppermute x18, waiting for transfers between devices, partner_2(): lax.ppermute(x, axis, [(i, i ^ 1 << bit) for i in range(lax.axis_size(axi...  30.6 us
  transfers between devices with their start and end apart: 54, of which 29 were waited for; matrix products, arithmetic and copies ran while one was open for 3% of the time, Pallas kernels for 0%

commit v1 on v0

v1 whole, which is shorter than its diff:
```python
import functools

import jax
import jax.numpy as jnp
from jax import lax
from jax.experimental import pallas as pl
from jax.experimental.pallas import tpu as pltpu
from jax.sharding import PartitionSpec as P

NODES = 64
CLASSES = 16
SLABS = 16
RELAX = 0.6
F32 = jnp.float32
HIGHEST = lax.Precision.HIGHEST
AXES = ("gx", "gy", "gz")


def dot(left, right):
    return jnp.dot(left, right, precision=HIGHEST, preferred_element_type=F32)


def iota(shape, dim):
    return lax.broadcasted_iota(jnp.int32, shape, dim)


def roll(values, shift, axis):
    return pltpu.roll(values, shift % values.shape[axis], axis)


def lane_places(shape):
    lane = iota(shape, len(shape) - 1)
    yd = (lane * 171) >> 12
    rest = lane - 24 * yd
    return rest >> 1, yd, rest & 1


def beside_1(v, lane, sub):
    a, b, gy = lane >> 6, (lane >> 4) & 3, lane & 15
    swapped = [roll(x, 64, 1) for x in v]
    result = []
    for gx in range(8):
        x = v[gx]
        total = swapped[gx] + jnp.where((gy & 1) == 0, roll(x, -1, 1), roll(x, 1, 1))
        if gx % 2 == 0:
            total = total + jnp.where(a == 1, swapped[gx + 1], 0.0)
        else:
            total = total + jnp.where(a == 0, swapped[gx - 1], 0.0)
        after = jnp.where((sub & 1) == 0, roll(roll(x, -1, 0), 48, 1), 0.0)
        before = jnp.where((sub & 1) == 1, roll(roll(x, 1, 0), -48, 1), 0.0)
        total = total + jnp.where(b < 3, roll(x, -16, 1), after)
        total = total + jnp.where(b > 0, roll(x, 16, 1), before)
        result.append(total)
    return result


def beside_2(v, lane, sub):
    b, gy = (lane >> 4) & 3, lane & 15
    result = []
    for gx in range(8):
        x = v[gx]
        total = jnp.where((gy & 2) == 0, roll(x, -2, 1), roll(x, 2, 1))
        if gx % 4 < 3:
            total = total + v[gx + 1]
        if gx % 4 > 0:
            total = total + v[gx - 1]
        after = jnp.where((sub & 3) < 3, roll(roll(x, -1, 0), 32, 1), 0.0)
        before = jnp.where((sub & 3) > 0, roll(roll(x, 1, 0), -32, 1), 0.0)
        total = total + jnp.where(b < 2, roll(x, -32, 1), after)
        total = total + jnp.where(b >= 2, roll(x, 32, 1), before)
        result.append(total)
    return result


def beside_3(v, lane, sub):
    gy = lane & 15
    result = []
    for gx in range(8):
        x = v[gx]
        total = jnp.where((gy & 4) == 0, roll(x, -4, 1), roll(x, 4, 1))
        if gx + 2 < 8:
            total = total + v[gx + 2]
        if gx - 2 >= 0:
            total = total + v[gx - 2]
        total = total + jnp.where(sub < 7, roll(x, -1, 0), 0.0)
        total = total + jnp.where(sub > 0, roll(x, 1, 0), 0.0)
        result.append(total)
    return result


def coarsen_1(v, lane):
    b, gy = (lane >> 4) & 3, lane & 15
    result = []
    for x in v:
        x = x + roll(x, 64, 1)
        x = x + jnp.where((b & 1) == 0, roll(x, -16, 1), roll(x, 16, 1))
        x = x + jnp.where((gy & 1) == 0, roll(x, -1, 1), roll(x, 1, 1))
        result.append(x)
    return result


def coarsen_2(v, lane):
    b, gy = (lane >> 4) & 3, lane & 15
    result = []
    for gx in range(8):
        x = v[gx] + v[gx ^ 1]
        x = x + jnp.where(b < 2, roll(x, -32, 1), roll(x, 32, 1))
        x = x + jnp.where((gy & 2) == 0, roll(x, -2, 1), roll(x, 2, 1))
        result.append(x)
    return result


def coarse_cycle(source, shift):
    lane, sub = iota((8, 128), 1), iota((8, 128), 0)
    eight = range(8)

    def remainder(beside, q, d, x):
        around = beside(x, lane, sub)
        return [q[i] - (d[i] * x[i] - around[i]) for i in eight]

    d1 = [6.0 + s for s in shift]
    shift2 = [0.125 * s for s in coarsen_1(shift, lane)]
    d2 = [6.0 + s for s in shift2]
    d3 = [6.0 + 0.125 * s for s in coarsen_2(shift2, lane)]
    w1 = [RELAX / d for d in d1]
    w2 = [RELAX / d for d in d2]
    w3 = [RELAX / d for d in d3]
    x1 = [w1[i] * source[i] for i in eight]
    q2 = [0.25 * t for t in coarsen_1(remainder(beside_1, source, d1, x1), lane)]
    x2 = [w2[i] * q2[i] for i in eight]
    q3 = [0.25 * t for t in coarsen_2(remainder(beside_2, q2, d2, x2), lane)]
    x3 = [w3[i] * q3[i] for i in eight]
    for _ in range(3):
        t3 = remainder(beside_3, q3, d3, x3)
        x3 = [x3[i] + w3[i] * t3[i] for i in eight]
    x2 = [x2[i] + x3[i] for i in eight]
    t2 = remainder(beside_2, q2, d2, x2)
    x2 = [x2[i] + w2[i] * t2[i] for i in eight]
    x1 = [x1[i] + x2[i] for i in eight]
    t1 = remainder(beside_1, source, d1, x1)
    return [x1[i] + w1[i] * t1[i] for i in eight]


def place_correction(coarse, place_ref, pad_ref, rows_ref, out_ref):
    gx0, gy0, gz0 = place_ref[0], place_ref[1], place_ref[2]
    pad_ref[...] = jnp.zeros_like(pad_ref)
    for gx in range(8):
        pad_ref[gx + 1, 8:16, :] = coarse[gx]
    rows_ref[...] = jnp.zeros_like(rows_ref)
    for e in range(3):
        for d in range(3):
            rows_ref[3 * e + d : 3 * e + d + 1, :] = pad_ref[gx0 + d, pl.ds(gz0 + 7 + e, 1), :]
    shape = (128, 512)
    source = iota(shape, 0)
    column = iota(shape, 1)
    target = column & 127
    yd = (target * 171) >> 12
    x = (target - 24 * yd) >> 1
    hit = ((source >> 4) & 3) == (column >> 7)
    hit = hit & ((source >> 6) == ((x >> 1) & 1))
    hit = hit & ((source & 15) == gy0 - 2 + yd) & (target < 120)
    spread = dot(rows_ref[...], jnp.where(hit, 1.0, 0.0))
    lane_x, _, _ = lane_places((1, 128))
    part = lane_x >> 2
    for t in range(8):
        e, b = (t + 2) // 4, (t + 2) % 4
        pieces = [spread[3 * e + d : 3 * e + d + 1, 128 * b : 128 * b + 128] for d in range(3)]
        row = jnp.where(part == 0, pieces[0], jnp.where(part == 1, pieces[1], pieces[2]))
        out_ref[2 * t : 2 * t + 1, :] = row
        out_ref[2 * t + 1 : 2 * t + 2, :] = row


def groups(values):
    return [values[8 * g : 8 * g + 8] for g in range(8)]


def next_y(values, yi):
    return jnp.where(yi == 0, roll(values, -1, 1), roll(values, -23, 1))


def previous_y(values, yi):
    return jnp.where(yi == 1, roll(values, 1, 1), roll(values, 23, 1))


def coupling(before, here, after, weights_ref):
    sub = iota((8, 128), 0)
    _, _, yi = lane_places((8, 128))
    wx, wy, wz = weights_ref[0], weights_ref[1], weights_ref[2]
    own, low, high = groups(here), groups(before), groups(after)
    wz_top = jnp.where((sub & 3) == 3, wz, 0.0)
    wz_bottom = jnp.where((sub & 3) == 0, wz, 0.0)
    wy_top = jnp.where(sub >= 4, wy, 0.0)
    wy_bottom = jnp.where(sub < 4, wy, 0.0)
    result = []
    for g in range(8):
        term = wz_top * roll(high[g], 3, 0) + wz_bottom * roll(low[g], -3, 0)
        if g % 2 == 1:
            term = term + wy_top * next_y(roll(own[g - 1], 4, 0), yi)
        else:
            term = term + wy_bottom * previous_y(roll(own[g + 1], 4, 0), yi)
        if g >= 6:
            term = term + wx * roll(own[g - 6], -2, 1)
        if g < 2:
            term = term + wx * roll(own[g + 6], 2, 1)
        result.append(term)
    return result


def apply_pair(field_ref, slab, packed_ref, class_ref, weights_ref, write):
    planes = [field_ref[slab + i] for i in (-1, 0, 1, 2)]
    u = jnp.concatenate([planes[1], planes[2]], axis=1)
    first = u.astype(jnp.bfloat16)
    rest = u - first.astype(F32)
    second = rest.astype(jnp.bfloat16)
    third = (rest - second.astype(F32)).astype(jnp.bfloat16)
    packed = jnp.concatenate([first, second, third, first, second, first], axis=0)
    products = jnp.dot(packed_ref[...], packed, preferred_element_type=F32)
    for half in range(2):
        marks = jnp.broadcast_to(class_ref[pl.ds(slab + half, 1), :], (8, 128))
        columns = slice(128 * half, 128 * half + 128)
        chosen = [products[8 * g : 8 * g + 8, columns] for g in range(8)]
        for k in range(1, CLASSES):
            hit = marks == k
            for g in range(8):
                row = 64 * k + 8 * g
                chosen[g] = jnp.where(hit, products[row : row + 8, columns], chosen[g])
        faces = coupling(planes[half], planes[half + 1], planes[half + 2], weights_ref)
        for g in range(8):
            write(slab + half, g, chosen[g] - faces[g])


def restrict(source_ref, inverse_ref, sums_ref, weights_ref, total_ref, all_ref, out_ref):
    sub = iota((8, 128), 0)
    _, _, yi = lane_places((8, 128))
    wx, wy, wz = weights_ref[0], weights_ref[1], weights_ref[2]

    def collect(s, carry):
        r, inv, cols = source_ref[s], inverse_ref[s], sums_ref[s]
        x = inv * r
        d = groups(r - cols * x)
        xs = groups(x)
        even = (xs[0] + xs[2]) + (xs[4] + xs[6])
        odd = (xs[1] + xs[3]) + (xs[5] + xs[7])
        local = ((d[0] + d[1]) + (d[2] + d[3])) + ((d[4] + d[5]) + (d[6] + d[7]))
        local = local + wx * (roll(xs[0] + xs[1], -2, 1) + roll(xs[6] + xs[7], 2, 1))
        local = local + jnp.where(sub < 4, wy, 0.0) * next_y(even, yi)
        local = local + jnp.where(sub >= 4, wy, 0.0) * previous_y(odd, yi)
        total_ref[s] = local
        all_ref[s] = even + odd
        return carry

    lax.fori_loop(3, 13, collect, 0)
    bottom = jnp.where((sub & 3) == 0, wz, 0.0)
    top = jnp.where((sub & 3) == 3, wz, 0.0)
    for z in range(8):
        s = z + 4
        value = total_ref[s] + bottom * all_ref[s + 1] + top * all_ref[s - 1]
        out_ref[z : z + 1, :] = jnp.sum(value, axis=0, keepdims=True)


def payload(cells, place_ref, scale):
    shape = (128, 128)
    source, target = iota(shape, 0), iota(shape, 1)
    hit = (source >= 56) & (source < 64) & (((source - 56) >> 2) == (target >> 6))
    hit = hit & ((target & 15) == place_ref[1])
    spread = dot(cells, jnp.where(hit, scale, 0.0))
    z, lane = iota((8, 128), 0), iota((8, 128), 1)
    return jnp.sum(jnp.where((z >> 1) == ((lane >> 4) & 3), spread, 0.0), axis=0, keepdims=True)


def compact(ref, out_ref):
    for pair in range(4):
        both = jnp.concatenate([ref[4 + 2 * pair], ref[5 + 2 * pair]], axis=0)
        out_ref[:, 128 * pair : 128 * pair + 128] = both.T[56:64]


def pack_kernel(blocks_ref, out_ref):
    w = blocks_ref[...]
    first = w.astype(jnp.bfloat16).astype(F32)
    rest = w - first
    second = rest.astype(jnp.bfloat16).astype(F32)
    third = rest - second
    column = iota(w.shape, 1)
    out_ref[...] = jnp.where(column < 192, first, jnp.where(column < 320, second, third)).astype(jnp.bfloat16)


def start_kernel(
    place_ref, weights_ref, class_shift_ref, middle_ref, low_ref, high_ref, table_ref,
    field_ref, class_ref, inverse_ref, sums_ref, payload_ref,
    total_ref, all_ref, cells_ref,
):
    rows = jnp.zeros((8, 128), F32)

    def turned(ref, block):
        return jnp.concatenate([ref[:, 128 * block : 128 * block + 128], rows], axis=0).T

    blocks = [turned(low_ref, 1), turned(low_ref, 2), turned(middle_ref, 0), turned(middle_ref, 1)]
    blocks += [turned(middle_ref, 3), turned(middle_ref, 4), turned(high_ref, 0), turned(high_ref, 1)]
    for pair, block in enumerate(blocks):
        field_ref[2 * pair] = block[:64]
        field_ref[2 * pair + 1] = block[64:]
    marks = jnp.concatenate(
        [turned(low_ref, 0)[0:8], turned(middle_ref, 2)[0:8], turned(high_ref, 2)[0:8]], axis=0
    )
    class_ref[...] = jnp.concatenate([marks[4:16], marks[16:20]], axis=0).astype(jnp.int32)

    gx0, gy0, gz0 = place_ref[0], place_ref[1], place_ref[2]
    x, yd, _ = lane_places((1, 128))
    gx, gy = gx0 - 1 + (x >> 2), gy0 - 2 + yd
    inside = (gx >= 0) & (gx < 8) & (gy >= 0) & (gy < 16) & (yd < 5)
    relax = jnp.where(inside, RELAX, 0.0)

    def coefficients(s, carry):
        row = class_ref[pl.ds(s, 1), :]
        onehot = jnp.where(jnp.broadcast_to(row, (CLASSES, 128)) == iota((CLASSES, 128), 0), 1.0, 0.0)
        both = dot(table_ref[...], onehot)
        gz = gz0 - 1 + ((s + 4) >> 3)
        valid = jnp.where((gz >= 0) & (gz < 8), 1.0, 0.0)
        inverse_ref[s] = (relax * valid) / both[:64]
        sums_ref[s] = both[64:]
        return carry

    lax.fori_loop(0, SLABS, coefficients, 0)
    restrict(field_ref, inverse_ref, sums_ref, weights_ref, total_ref, all_ref, cells_ref)
    own_marks = class_ref[4:12, :]
    shifts = jnp.zeros((8, 128), F32)
    for k in range(CLASSES):
        shifts = jnp.where(own_marks == k, class_shift_ref[k], shifts)
    payload_ref[:, 0:128] = payload(cells_ref[...], place_ref, 1.0 / NODES)
    payload_ref[:, 128:256] = payload(shifts, place_ref, 0.125)


def first_kernel(
    place_ref, weights_ref, gathered_ref, field_ref, class_ref, inverse_ref, sums_ref, packed_ref, right_ref,
    image_ref, own_direction_ref, own_image_ref, payload_ref,
    iterate_ref, smooth_ref, pad_ref, rows_ref, shift_ref, total_ref, all_ref, cells_ref,
):
    coarse = coarse_cycle(
        [gathered_ref[g, :, 0:128] for g in range(8)], [gathered_ref[g, :, 128:256] for g in range(8)]
    )
    place_correction(coarse, place_ref, pad_ref, rows_ref, shift_ref)

    def correct(s, carry):
        iterate_ref[s] = inverse_ref[s] * field_ref[s] + shift_ref[pl.ds(s, 1), :]
        return carry

    lax.fori_loop(0, SLABS, correct, 0)

    def smooth(s, g, value):
        at = (s, pl.ds(8 * g, 8))
        smooth_ref[at] = iterate_ref[at] + inverse_ref[at] * (field_ref[at] - value)

    def smooth_pair(i, carry):
        apply_pair(iterate_ref, 2 * i + 1, packed_ref, class_ref, weights_ref, smooth)
        return carry

    lax.fori_loop(0, 7, smooth_pair, 0)

    def store(s, g, value):
        image_ref[s, pl.ds(8 * g, 8)] = value

    def image_pair(i, carry):
        apply_pair(smooth_ref, 2 * i + 2, packed_ref, class_ref, weights_ref, store)
        return carry

    lax.fori_loop(0, 6, image_pair, 0)
    for s in (0, 1, 14, 15):
        image_ref[s] = jnp.zeros((64, 128), F32)
    restrict(image_ref, inverse_ref, sums_ref, weights_ref, total_ref, all_ref, cells_ref)
    payload_ref[:, 0:128] = payload(cells_ref[...], place_ref, 1.0 / NODES)
    compact(smooth_ref, own_direction_ref)
    compact(image_ref, own_image_ref)
    direction = own_direction_ref[...]
    gamma = jnp.sum(jnp.sum(right_ref[...] * direction, axis=0, keepdims=True), axis=1, keepdims=True)
    delta = jnp.sum(jnp.sum(direction * own_image_ref[...], axis=0, keepdims=True), axis=1, keepdims=True)
    lane = iota((1, 128), 1)
    payload_ref[:, 128:256] = jnp.where(lane == 0, gamma, jnp.where(lane == 1, delta, 0.0))


def second_kernel(
    place_ref, weights_ref, gathered_ref, shifts_ref, image_ref, class_ref, inverse_ref, packed_ref, right_ref,
    own_direction_ref, own_image_ref,
    residual_ref, smoothed_ref, applied_ref, known_ref, payload_ref,
    iterate_ref, smooth_ref, second_ref, pad_ref, rows_ref, shift_ref, turned_ref,
):
    coarse = coarse_cycle(
        [gathered_ref[g, :, 0:128] for g in range(8)], [shifts_ref[g, :, 128:256] for g in range(8)]
    )
    place_correction(coarse, place_ref, pad_ref, rows_ref, shift_ref)

    def correct(s, carry):
        iterate_ref[s] = inverse_ref[s] * image_ref[s] + shift_ref[pl.ds(s, 1), :]
        return carry

    lax.fori_loop(2, 14, correct, 0)

    def smooth(s, g, value):
        at = (s, pl.ds(8 * g, 8))
        smooth_ref[at] = iterate_ref[at] + inverse_ref[at] * (image_ref[at] - value)

    def smooth_pair(i, carry):
        apply_pair(iterate_ref, 2 * i + 3, packed_ref, class_ref, weights_ref, smooth)
        return carry

    lax.fori_loop(0, 5, smooth_pair, 0)

    def store(s, g, value):
        second_ref[s, pl.ds(8 * g, 8)] = value

    def second_pair(i, carry):
        apply_pair(smooth_ref, 2 * i + 4, packed_ref, class_ref, weights_ref, store)
        return carry

    lax.fori_loop(0, 4, second_pair, 0)

    sums = gathered_ref[0, :, 128:256]
    for g in range(1, 8):
        sums = sums + gathered_ref[g, :, 128:256]
    sums = jnp.sum(sums, axis=0, keepdims=True)
    known_ref[...] = sums
    step = sums[:, 0:1] / sums[:, 1:2]
    compact(smooth_ref, turned_ref)
    smoothed = own_direction_ref[...] - step * turned_ref[...]
    smoothed_ref[...] = smoothed
    compact(second_ref, turned_ref)
    applied = own_image_ref[...] - step * turned_ref[...]
    applied_ref[...] = applied
    residual = right_ref[...] - step * own_image_ref[...]
    residual_ref[...] = residual

    def total(values):
        return jnp.sum(jnp.sum(values, axis=0, keepdims=True), axis=1, keepdims=True)

    lane = iota((1, 128), 1)
    cross = own_direction_ref[...] * applied + own_image_ref[...] * smoothed
    row = jnp.where(lane == 0, total(residual * smoothed), 0.0)
    row = jnp.where(lane == 1, total(smoothed * applied), row)
    payload_ref[...] = jnp.where(lane == 2, total(cross), row)


VMEM = pl.BlockSpec(memory_space=pltpu.VMEM)
SMEM = pl.BlockSpec(memory_space=pltpu.SMEM)


def call(body, scalars, out_shape, scratch, *args):
    specs = [SMEM] * scalars + [VMEM] * (len(args) - scalars)
    shapes = [jax.ShapeDtypeStruct(shape, dtype) for shape, dtype in out_shape]
    return pl.pallas_call(
        body,
        out_shape=shapes,
        in_specs=specs,
        out_specs=[VMEM] * len(shapes),
        scratch_shapes=[pltpu.VMEM(shape, F32) for shape in scratch],
        compiler_params=pltpu.CompilerParams(vmem_limit_bytes=40 * 1024 * 1024),
    )(*args)


FIELD = (SLABS, NODES, 128)
COARSE_SCRATCH = [(10, 24, 128), (16, 128), (16, 128)]
SUM_SCRATCH = [(SLABS, 8, 128), (SLABS, 8, 128), (8, 128)]
OWN = (8, 512)


def start_call(*args):
    shapes = [(FIELD, F32), ((SLABS, 128), jnp.int32), (FIELD, F32), (FIELD, F32), ((1, 256), F32)]
    return call(start_kernel, 3, shapes, SUM_SCRATCH, *args)


def first_call(*args):
    shapes = [(FIELD, F32), (OWN, F32), (OWN, F32), ((1, 256), F32)]
    return call(first_kernel, 2, shapes, [FIELD, FIELD] + COARSE_SCRATCH + SUM_SCRATCH, *args)


def second_call(*args):
    shapes = [(OWN, F32), (OWN, F32), (OWN, F32), ((1, 128), F32), ((1, 128), F32)]
    return call(second_kernel, 2, shapes, [FIELD, FIELD, FIELD] + COARSE_SCRATCH + [OWN], *args)


def shifted(x, axis, step):
    size = lax.axis_size(axis)
    pairs = [(i, i + step) for i in range(size) if 0 <= i + step < size]
    return lax.ppermute(x, axis, pairs)


def extend(own):
    wide = jnp.concatenate([shifted(own, "gx", 1), own, shifted(own, "gx", -1)], axis=0)
    middle = jnp.concatenate(
        [
            shifted(wide, "gy", 2), shifted(wide, "gy", 1), wide, shifted(wide, "gy", -1), shifted(wide, "gy", -2),
        ],
        axis=0,
    )
    low = shifted(middle[:, 256:640], "gz", 1)
    high = shifted(middle[:, 0:384], "gz", -1)
    return middle, low, high


def gather_cells(row):
    parts = lax.all_to_all(jnp.broadcast_to(row[None], (128, 1, 256)), ("gy", "gz"), 0, 0, tiled=True)
    plane = parts.reshape(16, 8, 256).sum(axis=0)
    return lax.all_to_all(jnp.broadcast_to(plane[None], (8, 8, 256)), "gx", 0, 0, tiled=True)


def gather_sum(row):
    parts = lax.all_to_all(jnp.broadcast_to(row[None], (128, 1, 128)), ("gy", "gz"), 0, 0, tiled=True)
    part = parts.reshape(128, 128).sum(axis=0)
    parts = lax.all_to_all(jnp.broadcast_to(part[None, None], (8, 1, 128)), "gx", 0, 0, tiled=True)
    return parts.reshape(8, 128).sum(axis=0)


def per_device(right_side, element_class, class_blocks, class_shift, face_weights):
    place = jnp.stack([lax.axis_index(axis) for axis in AXES]).astype(jnp.int32)
    right = right_side.reshape(OWN)
    marks = jnp.pad(element_class.reshape(8, 8).astype(F32), ((0, 0), (0, 120)))
    own = jnp.concatenate([right[:, 0:256], marks, right[:, 256:512]], axis=1)
    middle, low, high = extend(own)

    blocks = class_blocks.reshape(CLASSES * NODES, NODES)
    packed = call(
        pack_kernel, 0, [((CLASSES * NODES, 384), jnp.bfloat16)], [], jnp.concatenate([blocks] * 6, axis=1)
    )[0]
    table = jnp.concatenate(
        [jnp.diagonal(class_blocks, axis1=1, axis2=2), class_blocks.sum(axis=1)], axis=1
    ).T

    field, classes, inverse, sums, row = start_call(place, face_weights, class_shift, middle, low, high, table)
    gathered = gather_cells(row)
    image, direction, own_image, row = first_call(
        place, face_weights, gathered, field, classes, inverse, sums, packed, right
    )
    again = gather_cells(row)
    residual, smoothed, applied, known, row = second_call(
        place, face_weights, again, gathered, image, classes, inverse, packed, right, direction, own_image
    )
    totals = gather_sum(row)
    gamma, delta = known[0, 0], known[0, 1]
    beta = totals[0] / gamma
    step = totals[0] / (totals[1] + beta * (totals[2] + beta * delta))
    solution_field = (gamma / delta) * direction + step * (smoothed + beta * direction)
    residual = residual - step * (applied + beta * own_image)
    return (solution_field.reshape(right_side.shape), residual.reshape(right_side.shape))


def solution(mesh):
    in_specs = (P("gx", "gy", "gz"), P("gx", "gy", "gz"), P(), P(), P())
    out_specs = (P("gx", "gy", "gz"), P("gx", "gy", "gz"))
    return jax.shard_map(
        per_device, mesh=mesh, in_specs=in_specs, out_specs=out_specs, check_vma=False
    )
```

time: 678 us -> 189 us (0.28)
  blocking collectives: 368 us -> 92.3 us
  starting transfers between devices: 197 us -> 43.4 us
  waiting for transfers between devices: 61.9 us -> 12.2 us
  Pallas kernels: 0 us -> 19.8 us
  matrix products: 16.5 us -> 0 us
  other arithmetic: 11.4 us -> 2 us
    psum x3 -> x0, blocking collectives: 368 us -> none  [total(): return lax.psum(terms, ('gx', 'gy', 'gz'))]
    ppermute x54 -> x8, starting transfers between devices: 197 us -> 32.9 us  [shifted(): return lax.ppermute(x, axis, pairs)]
    all_to_all x0 -> x4, blocking collectives: none -> 92.3 us  [the longest x2 60 us: gather_cells(): lax.all_to_all(jnp.broadcast_to(row[None], (128, 1, 256)), ('gy', 'gz'),...]
    ppermute x54 -> x8, waiting for transfers between devices: 61.9 us -> 3.67 us  [shifted(): return lax.ppermute(x, axis, pairs)]
    pallas_call x0 -> x4, Pallas kernels: none -> 19.8 us  [call(): pl.pallas_call(body, out_shape=shapes, in_specs=specs, out_specs=[VMEM] *...]
    dot_general x20 -> x0, matrix products: 16.5 us -> none  [the longest x6 9.65 us: fine_apply(): jnp.dot(flat, wide_blocks, precision=highest)]
    all_to_all x0 -> x2, starting transfers between devices: none -> 10.4 us  [the longest x1 7.14 us: gather_cells(): lax.all_to_all(jnp.broadcast_to(plane[None], (8, 8, 256)), 'gx', 0, 0, ti...]
    all_to_all x0 -> x2, waiting for transfers between devices: none -> 8.57 us  [the longest x1 4.42 us: gather_sum(): lax.all_to_all(jnp.broadcast_to(part[None, None], (8, 1, 128)), 'gx', 0,...]
  transfers between devices with their start and end apart: 54 -> 10, of which waited for: 29 -> 5; matrix products, arithmetic and copies ran while one was open for 3% -> 4% of each run, Pallas kernels for 0% -> 0%
where the time goes in v1:
time: 189 us; the launch traced here: 188 us
  blocking collectives  92.3 us (49%)
  starting transfers between devices  43.4 us (23%)
  Pallas kernels  19.8 us (10%)
  waiting for transfers between devices  12.2 us (6%)
  local copies, waits for them, and re-layouts  12.1 us (6%)
  between operations  6.1 us (3%)
  other arithmetic  2 us (1%)
    all_to_all x2, blocking collectives, gather_cells(): lax.all_to_all(jnp.broadcast_to(row[None], (128, 1, 256)), ('gy', 'gz'),...  60 us
    ppermute x8, starting transfers between devices, shifted(): return lax.ppermute(x, axis, pairs)  32.9 us
    all_to_all x1, blocking collectives, gather_sum(): lax.all_to_all(jnp.broadcast_to(row[None], (128, 1, 128)), ('gy', 'gz'),...  22.8 us
    pallas_call x4, Pallas kernels, call(): pl.pallas_call(body, out_shape=shapes, in_specs=specs, out_specs=[VMEM] *...  19.8 us
    all_to_all x1, blocking collectives, gather_cells(): lax.all_to_all(jnp.broadcast_to(plane[None], (8, 8, 256)), 'gx', 0, 0, ti...  9.51 us
    all_to_all x1, starting transfers between devices, gather_cells(): lax.all_to_all(jnp.broadcast_to(plane[None], (8, 8, 256)), 'gx', 0, 0, ti...  7.14 us
    all_to_all x1, waiting for transfers between devices, gather_sum(): lax.all_to_all(jnp.broadcast_to(part[None, None], (8, 1, 128)), 'gx', 0,...  4.42 us
    all_to_all x1, waiting for transfers between devices, gather_cells(): lax.all_to_all(jnp.broadcast_to(plane[None], (8, 8, 256)), 'gx', 0, 0, ti...  4.15 us
  transfers between devices with their start and end apart: 10, of which 5 were waited for; matrix products, arithmetic and copies ran while one was open for 4% of the time, Pallas kernels for 0%

profile of v1, /device:TPU:1, one launch (start us, length us, event | category | flops | bytes accessed | tf_op | source)
XLA Modules:
  0.0 187.9 jit_solution(2222069557428477778)
XLA Ops:
  0.6 0.7 convert_element_type.8
  1.3 0.7 reshape.40.right_ref
  2.1 1.3 collective-permute-start.1
  3.4 4.7 %collective-permute-start = (f32[8,640]{1,0:T(8,128)S(1)}, f32[8,640]{1,0:T(8,128)S(1)}, u32[]{:S(2)}, u32[]{:S(2)}) collective-permute-start(f32[8,640]{1,0:T(8,128)S(1)} %pad_maximum_fusion.1), channel_id=1, source_target_pairs={{0,128},{128,256},{256,384},{384,512},{512,640},{640,768},{768,896... | collective-permute-start | bytes 61448 | tf_op jit(solution)/shard_map/ppermute | solution.py:482
  8.1 1.1 reduce_sum.45
  9.2 0.0 copy-start.2
  9.2 0.0 copy-start.3
  9.2 1.7 copy.13
  10.9 0.0 copy-start.4
  10.9 0.1 copy.14
  11.0 0.0 collective-permute-done
  11.0 6.1 %collective-permute-start.2 = (f32[24,640]{1,0:T(8,128)S(1)}, f32[24,640]{1,0:T(8,128)S(1)}, u32[]{:S(2)}, u32[]{:S(2)}) collective-permute-start(f32[24,640]{1,0:T(8,128)S(1)} %pad_maximum_fusion), channel_id=1, source_target_pairs={{0,16},{8,24},{16,32},{24,40},{32,48},{40,56},{48,64},{56,72},{64,... | collective-permute-start | bytes 184328 | tf_op jit(solution)/shard_map/ppermute | solution.py:482
  17.1 0.9 gather_fusion
  18.0 1.3 collective-permute-start.5
  19.3 1.3 collective-permute-start.4
  20.6 4.6 %collective-permute-start.3 = (f32[24,640]{1,0:T(8,128)S(1)}, f32[24,640]{1,0:T(8,128)S(1)}, u32[]{:S(2)}, u32[]{:S(2)}) collective-permute-start(f32[24,640]{1,0:T(8,128)S(1)} %pad_maximum_fusion), channel_id=1, source_target_pairs={{0,8},{8,16},{16,24},{24,32},{32,40},{40,48},{48,56},{56,64},{64,7... | collective-permute-start | bytes 184328 | tf_op jit(solution)/shard_map/ppermute | solution.py:482
  25.2 0.0 collective-permute-done.2
  25.3 1.2 collective-permute-done.3
  26.5 0.0 collective-permute-done.4
  26.6 0.1 collective-permute-done.5
  26.7 11.7 %collective-permute-start.7 = (f32[120,384]{1,0:T(8,128)S(1)}, f32[120,384]{1,0:T(8,128)S(1)}, u32[]{:S(2)}, u32[]{:S(2)}) collective-permute-start(f32[120,384]{1,0:T(8,128)S(1)} %get-tuple-element.30), channel_id=1, source_target_pairs={{1,0},{2,1},{3,2},{4,3},{5,4},{6,5},{7,6},{9,8},{10,9},{11,10},{12... | collective-permute-start | bytes 552968 | tf_op jit(solution)/shard_map/ppermute | solution.py:482
  38.4 1.9 %collective-permute-start.6 = (f32[120,384]{1,0:T(8,128)S(1)}, f32[120,384]{1,0:T(8,128)S(1)}, u32[]{:S(2)}, u32[]{:S(2)}) collective-permute-start(f32[120,384]{1,0:T(8,128)S(1)} %get-tuple-element.31), channel_id=1, source_target_pairs={{0,1},{1,2},{2,3},{3,4},{4,5},{5,6},{6,7},{8,9},{9,10},{10,11},{11... | collective-permute-start | bytes 552968 | tf_op jit(solution)/shard_map/ppermute | solution.py:482
  40.3 0.1 pad_add_fusion.place_ref
  40.4 0.0 collective-permute-done.7.high_ref
  40.4 2.4 %collective-permute-done.6.low_ref = f32[120,384]{1,0:T(8,128)S(1)} collective-permute-done((f32[120,384]{1,0:T(8,128)S(1)}, f32[120,384]{1,0:T(8,128)S(1)}, u32[]{:S(2)}, u32[]{:S(2)}) %collective-permute-start.6) | collective-permute-done | bytes 184352 | tf_op jit(solution)/shard_map/ppermute | solution.py:482
  42.8 4.8 %shard_map.68 = (f32[16,64,128]{2,1,0:T(8,128)S(1)}, s32[16,128]{1,0:T(8,128)S(1)}, f32[16,64,128]{2,1,0:T(8,128)S(1)}, f32[16,64,128]{2,1,0:T(8,128)S(1)}, f32[1,256]{1,0:T(1,128)S(1)}) custom-call(s32[3]{0:T(128)S(1)} %pad_add_fusion.place_ref, f32[3]{0:T(128)S(1)} %copy-done.2, f32[16]{0:T(128)S(1)} %copy-done.3, ...), custom_call_target="tpu_custom_call" | custom-call | tf_op jit(solution)/shard_map/pallas_call | solution.py:448
  47.6 0.8 copy-done
  48.4 0.1 broadcast_in_dim.23
  48.5 35.5 %all_to_all.30 = f32[128,1,256]{2,1,0:T(1,128)S(1)} all-to-all(f32[128,1,256]{2,1,0:T(1,128)S(1)} %broadcast_in_dim.23), channel_id=1, replica_groups=mesh['gx'=8,'gy'=16,'gz'=8] {'gy','gz'}, dimensions={0} | all-to-all | bytes 262144 | tf_op jit(solution)/shard_map/all_to_all | solution.py:499
  84.0 0.6 broadcast_in_dim.24
  84.6 7.1 %all-to-all-start.1 = ((f32[8,8,256]{2,1,0:T(8,128)}), f32[8,8,256]{2,1,0:T(8,128)S(1)}, u32[]{:S(2)}, u32[]{:S(2)}) async-start(f32[8,8,256]{2,1,0:T(8,128)} %broadcast_in_dim.24), calls=%async_computation.1 | async-start | bytes 131072 | tf_op jit(solution)/shard_map/all_to_all | solution.py:501
  91.8 2.9 %concatenate.25.blocks_ref = f32[1024,384]{1,0:T(8,128)S(1)} concatenate(f32[1024,64]{1,0:T(8,128)S(1)} %bitcast.27, f32[1024,64]{1,0:T(8,128)S(1)} %bitcast.28, f32[1024,64]{1,0:T(8,128)S(1)} %bitcast.29, f32[1024,64]{1,0:T(8,128)S(1)} %bitcast.30, f32[1024,64]{1,0:T(8,128)S(1)} %bitcast.31, f32[1024,64]{1,0:T(8,128)S(1)} %bitcast.32), dimensions={1} | concatenate | bytes 3145728 | tf_op jit(solution)/shard_map/concatenate | solution.py:520
  94.7 0.2 shard_map.69.packed_ref
  94.9 4.2 %all-to-all-done.1.gathered_ref.shifts_ref = f32[8,8,256]{2,1,0:T(8,128)S(1)} async-done(((f32[8,8,256]{2,1,0:T(8,128)}), f32[8,8,256]{2,1,0:T(8,128)S(1)}, u32[]{:S(2)}, u32[]{:S(2)}) %all-to-all-start.1) | async-done | bytes 65568 | tf_op jit(solution)/shard_map/all_to_all | solution.py:501
  99.0 1.0 copy-done.1
  100.1 8.7 %shard_map.70 = (f32[16,64,128]{2,1,0:T(8,128)S(1)}, f32[8,512]{1,0:T(8,128)S(1)}, f32[8,512]{1,0:T(8,128)S(1)}, f32[1,256]{1,0:T(1,128)S(1)}) custom-call(s32[3]{0:T(128)S(1)} %pad_add_fusion.place_ref, f32[3]{0:T(128)S(1)} %copy-done.2, f32[8,8,256]{2,1,0:T(8,128)S(1)} %all-to-all-done.1.gathered_ref.shifts_ref, ...), custom_call_target="tpu_custom_call" | custom-call | tf_op jit(solution)/shard_map/pallas_call | solution.py:448
  108.7 0.1 broadcast_in_dim.26
  108.8 24.5 %all_to_all.31 = f32[128,1,256]{2,1,0:T(1,128)S(1)} all-to-all(f32[128,1,256]{2,1,0:T(1,128)S(1)} %broadcast_in_dim.26), channel_id=1, replica_groups=mesh['gx'=8,'gy'=16,'gz'=8] {'gy','gz'}, dimensions={0} | all-to-all | bytes 262144 | tf_op jit(solution)/shard_map/all_to_all | solution.py:499
  133.4 9.5 %all_to_all.32.gathered_ref = f32[8,8,256]{2,1,0:T(8,128)S(1)} all-to-all(f32[8,8,256]{2,1,0:T(8,128)S(1)} %broadcast_in_dim.27), channel_id=1, replica_groups=mesh['gx'=8,'gy'=16,'gz'=8] {'gx'}, dimensions={0} | all-to-all | bytes 131072 | tf_op jit(solution)/shard_map/all_to_all | solution.py:501
  142.9 6.1 %shard_map.71 = (f32[8,512]{1,0:T(8,128)S(1)}, f32[8,512]{1,0:T(8,128)S(1)}, f32[8,512]{1,0:T(8,128)S(1)}, f32[1,128]{1,0:T(1,128)S(1)}, f32[1,128]{1,0:T(1,128)S(1)}) custom-call(s32[3]{0:T(128)S(1)} %pad_add_fusion.place_ref, f32[3]{0:T(128)S(1)} %copy-done.2, f32[8,8,256]{2,1,0:T(8,128)S(1)} %all_to_all.32.gathered_ref, ...), custom_call_target="tpu_custom_call" | custom-call | tf_op jit(solution)/shard_map/pallas_call | solution.py:448
  149.1 22.8 %all_to_all.33 = f32[128,1,128]{2,1,0:T(1,128)S(1)} all-to-all(f32[128,1,128]{2,1,0:T(1,128)S(1)} %broadcast_in_dim.53), channel_id=1, replica_groups=mesh['gx'=8,'gy'=16,'gz'=8] {'gy','gz'}, dimensions={0} | all-to-all | bytes 131072 | tf_op jit(solution)/shard_map/all_to_all | solution.py:505
  171.9 0.6 broadcast_in_dim.54
  172.5 3.3 %all-to-all-start.5 = ((f32[8,1,128]{2,1,0:T(1,128)}), f32[8,1,128]{2,1,0:T(1,128)S(1)}, u32[]{:S(2)}, u32[]{:S(2)}) async-start(f32[8,1,128]{2,1,0:T(1,128)} %broadcast_in_dim.54), calls=%async_computation.5 | async-start | bytes 8192 | tf_op jit(solution)/shard_map/all_to_all | solution.py:507
  175.8 0.6 fusion.2
  177.7 4.4 %all-to-all-done.5 = f32[8,1,128]{2,1,0:T(1,128)S(1)} async-done(((f32[8,1,128]{2,1,0:T(1,128)}), f32[8,1,128]{2,1,0:T(1,128)S(1)}, u32[]{:S(2)}, u32[]{:S(2)}) %all-to-all-start.5) | async-done | bytes 4128 | tf_op jit(solution)/shard_map/all_to_all | solution.py:507
  182.2 0.6 fusion.3
  186.7 0.6 reshape.45
  187.3 0.6 reshape.44
  (27 shorter events, 0.3 us)
Async XLA Ops:
  2.1 8.9 %collective-permute-start.1 = (f32[8,640]{1,0:T(8,128)S(1)}, f32[8,640]{1,0:T(8,128)S(1)}, u32[]{:S(2)}, u32[]{:S(2)}) collective-permute-start(f32[8,640]{1,0:T(8,128)S(1)} %pad_maximum_fusion.1), channel_id=1, source_target_pairs={{128,0},{256,128},{384,256},{512,384},{640,512},{768,640},{896,768... | collective-permute-start | bytes 61448 | tf_op jit(solution)/shard_map/ppermute | solution.py:482
  3.4 7.6 %collective-permute-start = (f32[8,640]{1,0:T(8,128)S(1)}, f32[8,640]{1,0:T(8,128)S(1)}, u32[]{:S(2)}, u32[]{:S(2)}) collective-permute-start(f32[8,640]{1,0:T(8,128)S(1)} %pad_maximum_fusion.1), channel_id=1, source_target_pairs={{0,128},{128,256},{256,384},{384,512},{512,640},{640,768},{768,896... | collective-permute-start | bytes 61448 | tf_op jit(solution)/shard_map/ppermute | solution.py:482
  9.2 33.6 %copy-start.2 = (f32[3]{0:T(128)S(1)}, f32[3]{0:T(128)}, u32[]{:S(2)}) copy-start(f32[3]{0:T(128)} %weights_ref.5) | copy-start | bytes 40
  9.2 33.6 %copy-start.3 = (f32[16]{0:T(128)S(1)}, f32[16]{0:T(128)}, u32[]{:S(2)}) copy-start(f32[16]{0:T(128)} %class_shift_ref.1) | copy-start | bytes 196
  10.9 80.9 %copy-start.4 = (f32[16,64,64]{2,1,0:T(8,128)S(1)}, f32[16,64,64]{2,1,0:T(8,128)}, u32[]{:S(2)}) copy-start(f32[16,64,64]{2,1,0:T(8,128)} %param.7) | copy-start | bytes 786436
  11.0 14.2 %collective-permute-start.2 = (f32[24,640]{1,0:T(8,128)S(1)}, f32[24,640]{1,0:T(8,128)S(1)}, u32[]{:S(2)}, u32[]{:S(2)}) collective-permute-start(f32[24,640]{1,0:T(8,128)S(1)} %pad_maximum_fusion), channel_id=1, source_target_pairs={{0,16},{8,24},{16,32},{24,40},{32,48},{40,56},{48,64},{56,72},{64,... | collective-permute-start | bytes 184328 | tf_op jit(solution)/shard_map/ppermute | solution.py:482
  18.0 8.6 %collective-permute-start.5 = (f32[24,640]{1,0:T(8,128)S(1)}, f32[24,640]{1,0:T(8,128)S(1)}, u32[]{:S(2)}, u32[]{:S(2)}) collective-permute-start(f32[24,640]{1,0:T(8,128)S(1)} %pad_maximum_fusion), channel_id=1, source_target_pairs={{16,0},{24,8},{32,16},{40,24},{48,32},{56,40},{64,48},{72,56},{80,... | collective-permute-start | bytes 184328 | tf_op jit(solution)/shard_map/ppermute | solution.py:482
  19.3 7.2 %collective-permute-start.4 = (f32[24,640]{1,0:T(8,128)S(1)}, f32[24,640]{1,0:T(8,128)S(1)}, u32[]{:S(2)}, u32[]{:S(2)}) collective-permute-start(f32[24,640]{1,0:T(8,128)S(1)} %pad_maximum_fusion), channel_id=1, source_target_pairs={{8,0},{16,8},{24,16},{32,24},{40,32},{48,40},{56,48},{64,56},{72,6... | collective-permute-start | bytes 184328 | tf_op jit(solution)/shard_map/ppermute | solution.py:482
  20.6 5.9 %collective-permute-start.3 = (f32[24,640]{1,0:T(8,128)S(1)}, f32[24,640]{1,0:T(8,128)S(1)}, u32[]{:S(2)}, u32[]{:S(2)}) collective-permute-start(f32[24,640]{1,0:T(8,128)S(1)} %pad_maximum_fusion), channel_id=1, source_target_pairs={{0,8},{8,16},{16,24},{24,32},{32,40},{40,48},{48,56},{56,64},{64,7... | collective-permute-start | bytes 184328 | tf_op jit(solution)/shard_map/ppermute | solution.py:482
  26.7 13.8 %collective-permute-start.7 = (f32[120,384]{1,0:T(8,128)S(1)}, f32[120,384]{1,0:T(8,128)S(1)}, u32[]{:S(2)}, u32[]{:S(2)}) collective-permute-start(f32[120,384]{1,0:T(8,128)S(1)} %get-tuple-element.30), channel_id=1, source_target_pairs={{1,0},{2,1},{3,2},{4,3},{5,4},{6,5},{7,6},{9,8},{10,9},{11,10},{12... | collective-permute-start | bytes 552968 | tf_op jit(solution)/shard_map/ppermute | solution.py:482
  38.4 4.4 %collective-permute-start.6 = (f32[120,384]{1,0:T(8,128)S(1)}, f32[120,384]{1,0:T(8,128)S(1)}, u32[]{:S(2)}, u32[]{:S(2)}) collective-permute-start(f32[120,384]{1,0:T(8,128)S(1)} %get-tuple-element.31), channel_id=1, source_target_pairs={{0,1},{1,2},{2,3},{3,4},{4,5},{5,6},{6,7},{8,9},{9,10},{10,11},{11... | collective-permute-start | bytes 552968 | tf_op jit(solution)/shard_map/ppermute | solution.py:482
  47.6 0.8 copy-start
  84.6 14.4 %all-to-all-start.1 = ((f32[8,8,256]{2,1,0:T(8,128)}), f32[8,8,256]{2,1,0:T(8,128)S(1)}, u32[]{:S(2)}, u32[]{:S(2)}) async-start(f32[8,8,256]{2,1,0:T(8,128)} %broadcast_in_dim.24), calls=%async_computation.1 | async-start | bytes 131072 | tf_op jit(solution)/shard_map/all_to_all | solution.py:501
  99.0 1.0 copy-start.1
  172.5 9.7 %all-to-all-start.5 = ((f32[8,1,128]{2,1,0:T(1,128)}), f32[8,1,128]{2,1,0:T(1,128)S(1)}, u32[]{:S(2)}, u32[]{:S(2)}) async-start(f32[8,1,128]{2,1,0:T(1,128)} %broadcast_in_dim.54), calls=%async_computation.5 | async-start | bytes 8192 | tf_op jit(solution)/shard_map/all_to_all | solution.py:507

commit v2 on v1

--- a/solution.py
+++ b/solution.py
@@ -274,14 +274,43 @@
         out_ref[:, 128 * pair : 128 * pair + 128] = both.T[56:64]
 
 
-def pack_kernel(blocks_ref, out_ref):
-    w = blocks_ref[...]
-    first = w.astype(jnp.bfloat16).astype(F32)
-    rest = w - first
+def own_right(own_ref):
+    return jnp.concatenate([own_ref[:, 0:256], own_ref[:, 384:640]], axis=1)
+
+
+def split(values):
+    first = values.astype(jnp.bfloat16).astype(F32)
+    rest = values - first
     second = rest.astype(jnp.bfloat16).astype(F32)
-    third = rest - second
-    column = iota(w.shape, 1)
-    out_ref[...] = jnp.where(column < 192, first, jnp.where(column < 320, second, third)).astype(jnp.bfloat16)
+    return first, second, rest - second
+
+
+def own_kernel(right_ref, marks_ref, out_ref):
+    out_ref[:, 256:384] = jnp.zeros((8, 128), F32)
+    for x in range(4):
+        rows = slice(2 * x, 2 * x + 2)
+        values = right_ref[x]
+        out_ref[rows, 0:256] = values[:, 0:256]
+        out_ref[rows, 384:640] = values[:, 256:512]
+        out_ref[rows, 256:264] = marks_ref[x].astype(F32)
+
+
+def pack_kernel(blocks_ref, packed_ref, table_ref):
+    diagonal = jnp.where(iota((64, 64), 0) == iota((64, 64), 1), 1.0, 0.0)
+    low = iota((64, 128), 1) < 64
+    rows = []
+    for k in range(CLASSES):
+        block = blocks_ref[k]
+        first, second, third = split(jnp.concatenate([block, block], axis=1))
+        at = slice(64 * k, 64 * k + 64)
+        packed_ref[at, 0:128] = first.astype(jnp.bfloat16)
+        packed_ref[at, 128:256] = jnp.where(low, first, second).astype(jnp.bfloat16)
+        packed_ref[at, 256:384] = jnp.where(low, second, third).astype(jnp.bfloat16)
+        diag = jnp.sum(block * diagonal, axis=0, keepdims=True)
+        rows.append(jnp.concatenate([diag, jnp.sum(block, axis=0, keepdims=True)], axis=1))
+    parts = split(jnp.concatenate(rows, axis=0))
+    table = jnp.concatenate(list(parts) + [jnp.zeros((80, 128), F32)], axis=0).T
+    table_ref[...] = table[:, 0:48].astype(jnp.bfloat16)
 
 
 def start_kernel(
@@ -310,17 +339,22 @@
     inside = (gx >= 0) & (gx < 8) & (gy >= 0) & (gy < 16) & (yd < 5)
     relax = jnp.where(inside, RELAX, 0.0)
 
-    def coefficients(s, carry):
-        row = class_ref[pl.ds(s, 1), :]
-        onehot = jnp.where(jnp.broadcast_to(row, (CLASSES, 128)) == iota((CLASSES, 128), 0), 1.0, 0.0)
-        both = dot(table_ref[...], onehot)
-        gz = gz0 - 1 + ((s + 4) >> 3)
-        valid = jnp.where((gz >= 0) & (gz < 8), 1.0, 0.0)
-        inverse_ref[s] = (relax * valid) / both[:64]
-        sums_ref[s] = both[64:]
-        return carry
-
-    lax.fori_loop(0, SLABS, coefficients, 0)
+    for pair in range(SLABS // 2):
+        slabs = (2 * pair, 2 * pair + 1)
+        halves = []
+        for s in slabs:
+            row = jnp.broadcast_to(class_ref[s : s + 1, :], (CLASSES, 128))
+            halves.append(jnp.where(row == iota((CLASSES, 128), 0), 1.0, 0.0))
+        onehot = jnp.concatenate(halves, axis=1)
+        onehot = jnp.concatenate([onehot] * 3, axis=0).astype(jnp.bfloat16)
+        both = jnp.dot(table_ref[...], onehot, preferred_element_type=F32)
+        for half, s in enumerate(slabs):
+            gz = gz0 - 1 + ((s + 4) >> 3)
+            valid = jnp.where((gz >= 0) & (gz < 8), 1.0, 0.0)
+            columns = slice(128 * half, 128 * half + 128)
+            inverse_ref[s] = (relax * valid) / both[:64, columns]
+            sums_ref[s] = both[64:, columns]
+
     restrict(field_ref, inverse_ref, sums_ref, weights_ref, total_ref, all_ref, cells_ref)
     own_marks = class_ref[4:12, :]
     shifts = jnp.zeros((8, 128), F32)
@@ -354,7 +388,8 @@
         apply_pair(iterate_ref, 2 * i + 1, packed_ref, class_ref, weights_ref, smooth)
         return carry
 
-    lax.fori_loop(0, 7, smooth_pair, 0)
+    for i in range(7):
+        smooth_pair(i, 0)
 
     def store(s, g, value):
         image_ref[s, pl.ds(8 * g, 8)] = value
@@ -363,7 +398,8 @@
         apply_pair(smooth_ref, 2 * i + 2, packed_ref, class_ref, weights_ref, store)
         return carry
 
-    lax.fori_loop(0, 6, image_pair, 0)
+    for i in range(6):
+        image_pair(i, 0)
     for s in (0, 1, 14, 15):
         image_ref[s] = jnp.zeros((64, 128), F32)
     restrict(image_ref, inverse_ref, sums_ref, weights_ref, total_ref, all_ref, cells_ref)
@@ -371,7 +407,7 @@
     compact(smooth_ref, own_direction_ref)
     compact(image_ref, own_image_ref)
     direction = own_direction_ref[...]
-    gamma = jnp.sum(jnp.sum(right_ref[...] * direction, axis=0, keepdims=True), axis=1, keepdims=True)
+    gamma = jnp.sum(jnp.sum(own_right(right_ref) * direction, axis=0, keepdims=True), axis=1, keepdims=True)
     delta = jnp.sum(jnp.sum(direction * own_image_ref[...], axis=0, keepdims=True), axis=1, keepdims=True)
     lane = iota((1, 128), 1)
     payload_ref[:, 128:256] = jnp.where(lane == 0, gamma, jnp.where(lane == 1, delta, 0.0))
@@ -402,7 +438,8 @@
         apply_pair(iterate_ref, 2 * i + 3, packed_ref, class_ref, weights_ref, smooth)
         return carry
 
-    lax.fori_loop(0, 5, smooth_pair, 0)
+    for i in range(5):
+        smooth_pair(i, 0)
 
     def store(s, g, value):
         second_ref[s, pl.ds(8 * g, 8)] = value
@@ -411,7 +448,8 @@
         apply_pair(smooth_ref, 2 * i + 4, packed_ref, class_ref, weights_ref, store)
         return carry
 
-    lax.fori_loop(0, 4, second_pair, 0)
+    for i in range(4):
+        second_pair(i, 0)
 
     sums = gathered_ref[0, :, 128:256]
     for g in range(1, 8):
@@ -425,7 +463,7 @@
     compact(second_ref, turned_ref)
     applied = own_image_ref[...] - step * turned_ref[...]
     applied_ref[...] = applied
-    residual = right_ref[...] - step * own_image_ref[...]
+    residual = own_right(right_ref) - step * own_image_ref[...]
     residual_ref[...] = residual
 
     def total(values):
@@ -436,6 +474,23 @@
     row = jnp.where(lane == 0, total(residual * smoothed), 0.0)
     row = jnp.where(lane == 1, total(smoothed * applied), row)
     payload_ref[...] = jnp.where(lane == 2, total(cross), row)
+
+
+def last_kernel(
+    parts_ref, known_ref, direction_ref, own_image_ref, smoothed_ref, applied_ref, residual_ref, field_ref, out_ref
+):
+    totals = parts_ref[0]
+    for gx in range(1, 8):
+        totals = totals + parts_ref[gx]
+    gamma, delta = known_ref[:, 0:1], known_ref[:, 1:2]
+    beta = totals[:, 0:1] / gamma
+    step = totals[:, 0:1] / (totals[:, 1:2] + beta * (totals[:, 2:3] + beta * delta))
+    direction = direction_ref[...]
+    field = (gamma / delta) * direction + step * (smoothed_ref[...] + beta * direction)
+    residual = residual_ref[...] - step * (applied_ref[...] + beta * own_image_ref[...])
+    for x in range(4):
+        field_ref[x] = field[2 * x : 2 * x + 2]
+        out_ref[x] = residual[2 * x : 2 * x + 2]
 
 
 VMEM = pl.BlockSpec(memory_space=pltpu.VMEM)
@@ -451,7 +506,7 @@
         in_specs=specs,
         out_specs=[VMEM] * len(shapes),
         scratch_shapes=[pltpu.VMEM(shape, F32) for shape in scratch],
-        compiler_params=pltpu.CompilerParams(vmem_limit_bytes=40 * 1024 * 1024),
+        compiler_params=pltpu.CompilerParams(vmem_limit_bytes=16 * 1024 * 1024),
     )(*args)
 
 
@@ -504,41 +559,28 @@
 def gather_sum(row):
     parts = lax.all_to_all(jnp.broadcast_to(row[None], (128, 1, 128)), ("gy", "gz"), 0, 0, tiled=True)
     part = parts.reshape(128, 128).sum(axis=0)
-    parts = lax.all_to_all(jnp.broadcast_to(part[None, None], (8, 1, 128)), "gx", 0, 0, tiled=True)
-    return parts.reshape(8, 128).sum(axis=0)
+    return lax.all_to_all(jnp.broadcast_to(part[None, None], (8, 1, 128)), "gx", 0, 0, tiled=True)
 
 
 def per_device(right_side, element_class, class_blocks, class_shift, face_weights):
     place = jnp.stack([lax.axis_index(axis) for axis in AXES]).astype(jnp.int32)
-    right = right_side.reshape(OWN)
-    marks = jnp.pad(element_class.reshape(8, 8).astype(F32), ((0, 0), (0, 120)))
-    own = jnp.concatenate([right[:, 0:256], marks, right[:, 256:512]], axis=1)
+    own = call(own_kernel, 0, [((8, 640), F32)], [], right_side, element_class)[0]
     middle, low, high = extend(own)
-
-    blocks = class_blocks.reshape(CLASSES * NODES, NODES)
-    packed = call(
-        pack_kernel, 0, [((CLASSES * NODES, 384), jnp.bfloat16)], [], jnp.concatenate([blocks] * 6, axis=1)
-    )[0]
-    table = jnp.concatenate(
-        [jnp.diagonal(class_blocks, axis1=1, axis2=2), class_blocks.sum(axis=1)], axis=1
-    ).T
-
+    packed, table = call(
+        pack_kernel, 0, [((CLASSES * NODES, 384), jnp.bfloat16), ((128, 48), jnp.bfloat16)], [], class_blocks
+    )
     field, classes, inverse, sums, row = start_call(place, face_weights, class_shift, middle, low, high, table)
     gathered = gather_cells(row)
     image, direction, own_image, row = first_call(
-        place, face_weights, gathered, field, classes, inverse, sums, packed, right
+        place, face_weights, gathered, field, classes, inverse, sums, packed, own
     )
     again = gather_cells(row)
     residual, smoothed, applied, known, row = second_call(
-        place, face_weights, again, gathered, image, classes, inverse, packed, right, direction, own_image
-    )
-    totals = gather_sum(row)
-    gamma, delta = known[0, 0], known[0, 1]
-    beta = totals[0] / gamma
-    step = totals[0] / (totals[1] + beta * (totals[2] + beta * delta))
-    solution_field = (gamma / delta) * direction + step * (smoothed + beta * direction)
-    residual = residual - step * (applied + beta * own_image)
-    return (solution_field.reshape(right_side.shape), residual.reshape(right_side.shape))
+        place, face_weights, again, gathered, image, classes, inverse, packed, own, direction, own_image
+    )
+    parts = gather_sum(row)
+    shapes = [(right_side.shape, F32)] * 2
+    return tuple(call(last_kernel, 0, shapes, [], parts, known, direction, own_image, smoothed, applied, residual))
 
 
 def solution(mesh):

time: 189 us -> 173 us (0.915)
  blocking collectives: 92.3 us -> 117 us
  local copies, waits for them, and re-layouts: 12.1 us -> 1.72 us
  starting transfers between devices: 43.4 us -> 33.5 us
  waiting for transfers between devices: 12.2 us -> 4.19 us
  between operations: 6.1 us -> 0.85 us
  Pallas kernels: 19.8 us -> 15 us
    all_to_all x1 -> x2, blocking collectives: 9.51 us -> 25.3 us  [gather_cells(): lax.all_to_all(jnp.broadcast_to(plane[None], (8, 8, 256)), 'gx', 0, 0, ti...]
    all_to_all x2 -> x0, starting transfers between devices: 10.4 us -> none  [the longest x1 7.14 us: gather_cells(): lax.all_to_all(jnp.broadcast_to(plane[None], (8, 8, 256)), 'gx', 0, 0, ti...]
    all_to_all x0 -> x1, blocking collectives: none -> 8.89 us  [gather_sum(): lax.all_to_all(jnp.broadcast_to(part[None, None], (8, 1, 128)), 'gx', 0,...]
    all_to_all x2 -> x0, waiting for transfers between devices: 8.57 us -> none  [the longest x1 4.42 us: gather_sum(): lax.all_to_all(jnp.broadcast_to(part[None, None], (8, 1, 128)), 'gx', 0,...]
    pallas_call x4 -> x6, Pallas kernels: 19.8 us -> 15 us  [call(): pl.pallas_call(body, out_shape=shapes, in_specs=specs, out_specs=[VMEM] *...]
    concatenate x1 -> x0, local copies, waits for them, and re-layouts: 2.86 us -> none  [per_device(): jnp.concatenate([blocks] * 6, axis=1)]
    unnamed x16, local copies, waits for them, and re-layouts: 3.56 us -> 1.44 us
    reshape x3 -> x0, local copies, waits for them, and re-layouts: 1.97 us -> none  [the longest x1 0.73 us: per_device(): right = right_side.reshape(OWN)]
  transfers between devices with their start and end apart: 10 -> 8, of which waited for: 5 -> 3; matrix products, arithmetic and copies ran while one was open for 4% -> 0% of each run, Pallas kernels for 0% -> 0%
where the time goes in v2:
time: 173 us; the launch traced here: 172 us
  blocking collectives  117 us (68%)
  starting transfers between devices  33.5 us (19%)
  Pallas kernels  15 us (9%)
  waiting for transfers between devices  4.19 us (2%)
    all_to_all x2, blocking collectives, gather_cells(): lax.all_to_all(jnp.broadcast_to(row[None], (128, 1, 256)), ('gy', 'gz'),...  60 us
    ppermute x8, starting transfers between devices, shifted(): return lax.ppermute(x, axis, pairs)  33.5 us
    all_to_all x2, blocking collectives, gather_cells(): lax.all_to_all(jnp.broadcast_to(plane[None], (8, 8, 256)), 'gx', 0, 0, ti...  25.3 us
    all_to_all x1, blocking collectives, gather_sum(): lax.all_to_all(jnp.broadcast_to(row[None], (128, 1, 128)), ('gy', 'gz'),...  22.8 us
    pallas_call x6, Pallas kernels, call(): pl.pallas_call(body, out_shape=shapes, in_specs=specs, out_specs=[VMEM] *...  15 us
    all_to_all x1, blocking collectives, gather_sum(): lax.all_to_all(jnp.broadcast_to(part[None, None], (8, 1, 128)), 'gx', 0,...  8.89 us
    ppermute x8, waiting for transfers between devices, shifted(): return lax.ppermute(x, axis, pairs)  4.19 us
  transfers between devices with their start and end apart: 8, of which 3 were waited for; matrix products, arithmetic and copies ran while one was open for 0% of the time, Pallas kernels for 0%

profile of v2, /device:TPU:1, one launch (start us, length us, event | category | flops | bytes accessed | tf_op | source)
XLA Modules:
  0.0 172.4 jit_solution(16333951481759561126)
XLA Ops:
  0.6 0.0 copy-start.1
  0.6 0.7 copy-done.1
  1.3 0.0 copy-start.3
  1.4 0.7 copy-done.3
  2.0 1.3 collective-permute-start.1
  3.3 4.7 %collective-permute-start = (f32[8,640]{1,0:T(8,128)S(1)}, f32[8,640]{1,0:T(8,128)S(1)}, u32[]{:S(2)}, u32[]{:S(2)}) collective-permute-start(f32[8,640]{1,0:T(8,128)S(1)} %shard_map.68.right_ref), channel_id=1, source_target_pairs={{0,128},{128,256},{256,384},{384,512},{512,640},{640,768},{768,896... | collective-permute-start | bytes 61448 | tf_op jit(solution)/shard_map/ppermute | solution.py:537
  8.0 0.0 collective-permute-done.1
  8.0 0.9 collective-permute-done
  8.9 6.0 %collective-permute-start.2 = (f32[24,640]{1,0:T(8,128)S(1)}, f32[24,640]{1,0:T(8,128)S(1)}, u32[]{:S(2)}, u32[]{:S(2)}) collective-permute-start(f32[24,640]{1,0:T(8,128)S(1)} %pad_maximum_fusion), channel_id=1, source_target_pairs={{0,16},{8,24},{16,32},{24,40},{32,48},{40,56},{48,64},{56,72},{64,... | collective-permute-start | bytes 184328 | tf_op jit(solution)/shard_map/ppermute | solution.py:537
  14.9 1.3 collective-permute-start.5
  16.2 1.3 collective-permute-start.4
  17.5 4.6 %collective-permute-start.3 = (f32[24,640]{1,0:T(8,128)S(1)}, f32[24,640]{1,0:T(8,128)S(1)}, u32[]{:S(2)}, u32[]{:S(2)}) collective-permute-start(f32[24,640]{1,0:T(8,128)S(1)} %pad_maximum_fusion), channel_id=1, source_target_pairs={{0,8},{8,16},{16,24},{24,32},{32,40},{40,48},{48,56},{56,64},{64,7... | collective-permute-start | bytes 184328 | tf_op jit(solution)/shard_map/ppermute | solution.py:537
  22.1 0.0 collective-permute-done.2
  22.1 1.2 collective-permute-done.3
  23.4 0.0 copy-start
  23.4 0.0 collective-permute-done.4
  23.5 0.0 collective-permute-done.5
  23.5 12.5 %collective-permute-start.7 = (f32[120,384]{1,0:T(8,128)S(1)}, f32[120,384]{1,0:T(8,128)S(1)}, u32[]{:S(2)}, u32[]{:S(2)}) collective-permute-start(f32[120,384]{1,0:T(8,128)S(1)} %get-tuple-element.34), channel_id=1, source_target_pairs={{1,0},{2,1},{3,2},{4,3},{5,4},{6,5},{7,6},{9,8},{10,9},{11,10},{12... | collective-permute-start | bytes 552968 | tf_op jit(solution)/shard_map/ppermute | solution.py:537
  36.0 1.9 %collective-permute-start.6 = (f32[120,384]{1,0:T(8,128)S(1)}, f32[120,384]{1,0:T(8,128)S(1)}, u32[]{:S(2)}, u32[]{:S(2)}) collective-permute-start(f32[120,384]{1,0:T(8,128)S(1)} %get-tuple-element.35), channel_id=1, source_target_pairs={{0,1},{1,2},{2,3},{3,4},{4,5},{5,6},{6,7},{8,9},{9,10},{10,11},{11... | collective-permute-start | bytes 552968 | tf_op jit(solution)/shard_map/ppermute | solution.py:537
  37.9 0.0 copy-done
  37.9 0.3 shard_map.69
  38.3 0.1 pad_add_fusion.place_ref
  38.4 0.0 copy-start.2
  38.4 0.0 copy-start.4
  38.4 0.0 collective-permute-done.7.high_ref
  38.4 2.0 %collective-permute-done.6.low_ref = f32[120,384]{1,0:T(8,128)S(1)} collective-permute-done((f32[120,384]{1,0:T(8,128)S(1)}, f32[120,384]{1,0:T(8,128)S(1)}, u32[]{:S(2)}, u32[]{:S(2)}) %collective-permute-start.6) | collective-permute-done | bytes 184352 | tf_op jit(solution)/shard_map/ppermute | solution.py:537
  40.4 0.0 copy-done.2
  40.4 0.0 copy-done.4
  40.4 1.9 %shard_map.70 = (f32[16,64,128]{2,1,0:T(8,128)S(1)}, s32[16,128]{1,0:T(8,128)S(1)}, f32[16,64,128]{2,1,0:T(8,128)S(1)}, f32[16,64,128]{2,1,0:T(8,128)S(1)}, f32[1,256]{1,0:T(1,128)S(1)}) custom-call(s32[3]{0:T(128)S(1)} %pad_add_fusion.place_ref, f32[3]{0:T(128)S(1)} %copy-done.2, f32[16]{0:T(128)S(1)} %copy-done.4, ...), custom_call_target="tpu_custom_call" | custom-call | tf_op jit(solution)/shard_map/pallas_call | solution.py:503
  42.3 0.1 broadcast_in_dim.19
  42.4 35.5 %all_to_all.30 = f32[128,1,256]{2,1,0:T(1,128)S(1)} all-to-all(f32[128,1,256]{2,1,0:T(1,128)S(1)} %broadcast_in_dim.19), channel_id=1, replica_groups=mesh['gx'=8,'gy'=16,'gz'=8] {'gy','gz'}, dimensions={0} | all-to-all | bytes 262144 | tf_op jit(solution)/shard_map/all_to_all | solution.py:554
  77.9 15.8 %all_to_all.31.gathered_ref.shifts_ref = f32[8,8,256]{2,1,0:T(8,128)S(1)} all-to-all(f32[8,8,256]{2,1,0:T(8,128)S(1)} %broadcast_in_dim.20), channel_id=1, replica_groups=mesh['gx'=8,'gy'=16,'gz'=8] {'gx'}, dimensions={0} | all-to-all | bytes 131072 | tf_op jit(solution)/shard_map/all_to_all | solution.py:556
  93.7 6.9 %shard_map.71 = (f32[16,64,128]{2,1,0:T(8,128)S(1)}, f32[8,512]{1,0:T(8,128)S(1)}, f32[8,512]{1,0:T(8,128)S(1)}, f32[1,256]{1,0:T(1,128)S(1)}) custom-call(s32[3]{0:T(128)S(1)} %pad_add_fusion.place_ref, f32[3]{0:T(128)S(1)} %copy-done.2, f32[8,8,256]{2,1,0:T(8,128)S(1)} %all_to_all.31.gathered_ref.shifts_ref, ...), custom_call_target="tpu_custom_call" | custom-call | tf_op jit(solution)/shard_map/pallas_call | solution.py:503
  100.7 0.1 broadcast_in_dim.22
  100.8 24.5 %all_to_all.32 = f32[128,1,256]{2,1,0:T(1,128)S(1)} all-to-all(f32[128,1,256]{2,1,0:T(1,128)S(1)} %broadcast_in_dim.22), channel_id=1, replica_groups=mesh['gx'=8,'gy'=16,'gz'=8] {'gy','gz'}, dimensions={0} | all-to-all | bytes 262144 | tf_op jit(solution)/shard_map/all_to_all | solution.py:554
  125.3 9.5 %all_to_all.33.gathered_ref = f32[8,8,256]{2,1,0:T(8,128)S(1)} all-to-all(f32[8,8,256]{2,1,0:T(8,128)S(1)} %broadcast_in_dim.23), channel_id=1, replica_groups=mesh['gx'=8,'gy'=16,'gz'=8] {'gx'}, dimensions={0} | all-to-all | bytes 131072 | tf_op jit(solution)/shard_map/all_to_all | solution.py:556
  134.8 4.8 %shard_map.72 = (f32[8,512]{1,0:T(8,128)S(1)}, f32[8,512]{1,0:T(8,128)S(1)}, f32[8,512]{1,0:T(8,128)S(1)}, f32[1,128]{1,0:T(1,128)S(1)}, f32[1,128]{1,0:T(1,128)S(1)}) custom-call(s32[3]{0:T(128)S(1)} %pad_add_fusion.place_ref, f32[3]{0:T(128)S(1)} %copy-done.2, f32[8,8,256]{2,1,0:T(8,128)S(1)} %all_to_all.33.gathered_ref, ...), custom_call_target="tpu_custom_call" | custom-call | tf_op jit(solution)/shard_map/pallas_call | solution.py:503
  139.6 22.8 %all_to_all.34 = f32[128,1,128]{2,1,0:T(1,128)S(1)} all-to-all(f32[128,1,128]{2,1,0:T(1,128)S(1)} %broadcast_in_dim.49), channel_id=1, replica_groups=mesh['gx'=8,'gy'=16,'gz'=8] {'gy','gz'}, dimensions={0} | all-to-all | bytes 131072 | tf_op jit(solution)/shard_map/all_to_all | solution.py:560
  162.5 8.9 %all_to_all.35.parts_ref = f32[8,1,128]{2,1,0:T(1,128)S(1)} all-to-all(f32[8,1,128]{2,1,0:T(1,128)S(1)} %broadcast_in_dim.50), channel_id=1, replica_groups=mesh['gx'=8,'gy'=16,'gz'=8] {'gx'}, dimensions={0} | all-to-all | bytes 8192 | tf_op jit(solution)/shard_map/all_to_all | solution.py:562
  171.4 1.0 shard_map.73
  (17 shorter events, 0.2 us)
Async XLA Ops:
  0.6 0.7 copy-start.1
  1.3 0.7 copy-start.3
  2.0 6.0 %collective-permute-start.1 = (f32[8,640]{1,0:T(8,128)S(1)}, f32[8,640]{1,0:T(8,128)S(1)}, u32[]{:S(2)}, u32[]{:S(2)}) collective-permute-start(f32[8,640]{1,0:T(8,128)S(1)} %shard_map.68.right_ref), channel_id=1, source_target_pairs={{128,0},{256,128},{384,256},{512,384},{640,512},{768,640},{896,768... | collective-permute-start | bytes 61448 | tf_op jit(solution)/shard_map/ppermute | solution.py:537
  3.3 5.6 %collective-permute-start = (f32[8,640]{1,0:T(8,128)S(1)}, f32[8,640]{1,0:T(8,128)S(1)}, u32[]{:S(2)}, u32[]{:S(2)}) collective-permute-start(f32[8,640]{1,0:T(8,128)S(1)} %shard_map.68.right_ref), channel_id=1, source_target_pairs={{0,128},{128,256},{256,384},{384,512},{512,640},{640,768},{768,896... | collective-permute-start | bytes 61448 | tf_op jit(solution)/shard_map/ppermute | solution.py:537
  8.9 13.2 %collective-permute-start.2 = (f32[24,640]{1,0:T(8,128)S(1)}, f32[24,640]{1,0:T(8,128)S(1)}, u32[]{:S(2)}, u32[]{:S(2)}) collective-permute-start(f32[24,640]{1,0:T(8,128)S(1)} %pad_maximum_fusion), channel_id=1, source_target_pairs={{0,16},{8,24},{16,32},{24,40},{32,48},{40,56},{48,64},{56,72},{64,... | collective-permute-start | bytes 184328 | tf_op jit(solution)/shard_map/ppermute | solution.py:537
  14.9 8.6 %collective-permute-start.5 = (f32[24,640]{1,0:T(8,128)S(1)}, f32[24,640]{1,0:T(8,128)S(1)}, u32[]{:S(2)}, u32[]{:S(2)}) collective-permute-start(f32[24,640]{1,0:T(8,128)S(1)} %pad_maximum_fusion), channel_id=1, source_target_pairs={{16,0},{24,8},{32,16},{40,24},{48,32},{56,40},{64,48},{72,56},{80,... | collective-permute-start | bytes 184328 | tf_op jit(solution)/shard_map/ppermute | solution.py:537
  16.2 7.3 %collective-permute-start.4 = (f32[24,640]{1,0:T(8,128)S(1)}, f32[24,640]{1,0:T(8,128)S(1)}, u32[]{:S(2)}, u32[]{:S(2)}) collective-permute-start(f32[24,640]{1,0:T(8,128)S(1)} %pad_maximum_fusion), channel_id=1, source_target_pairs={{8,0},{16,8},{24,16},{32,24},{40,32},{48,40},{56,48},{64,56},{72,6... | collective-permute-start | bytes 184328 | tf_op jit(solution)/shard_map/ppermute | solution.py:537
  17.5 5.9 %collective-permute-start.3 = (f32[24,640]{1,0:T(8,128)S(1)}, f32[24,640]{1,0:T(8,128)S(1)}, u32[]{:S(2)}, u32[]{:S(2)}) collective-permute-start(f32[24,640]{1,0:T(8,128)S(1)} %pad_maximum_fusion), channel_id=1, source_target_pairs={{0,8},{8,16},{16,24},{24,32},{32,40},{40,48},{48,56},{56,64},{64,7... | collective-permute-start | bytes 184328 | tf_op jit(solution)/shard_map/ppermute | solution.py:537
  23.4 14.5 %copy-start = (f32[16,64,64]{2,1,0:T(8,128)S(1)}, f32[16,64,64]{2,1,0:T(8,128)}, u32[]{:S(2)}) copy-start(f32[16,64,64]{2,1,0:T(8,128)} %blocks_ref.1) | copy-start | bytes 786436
  23.5 14.8 %collective-permute-start.7 = (f32[120,384]{1,0:T(8,128)S(1)}, f32[120,384]{1,0:T(8,128)S(1)}, u32[]{:S(2)}, u32[]{:S(2)}) collective-permute-start(f32[120,384]{1,0:T(8,128)S(1)} %get-tuple-element.34), channel_id=1, source_target_pairs={{1,0},{2,1},{3,2},{4,3},{5,4},{6,5},{7,6},{9,8},{10,9},{11,10},{12... | collective-permute-start | bytes 552968 | tf_op jit(solution)/shard_map/ppermute | solution.py:537
  36.0 4.4 %collective-permute-start.6 = (f32[120,384]{1,0:T(8,128)S(1)}, f32[120,384]{1,0:T(8,128)S(1)}, u32[]{:S(2)}, u32[]{:S(2)}) collective-permute-start(f32[120,384]{1,0:T(8,128)S(1)} %get-tuple-element.35), channel_id=1, source_target_pairs={{0,1},{1,2},{2,3},{3,4},{4,5},{5,6},{6,7},{8,9},{9,10},{10,11},{11... | collective-permute-start | bytes 552968 | tf_op jit(solution)/shard_map/ppermute | solution.py:537
  38.4 2.0 %copy-start.2 = (f32[3]{0:T(128)S(1)}, f32[3]{0:T(128)}, u32[]{:S(2)}) copy-start(f32[3]{0:T(128)} %weights_ref.5) | copy-start | bytes 40
  38.4 2.0 %copy-start.4 = (f32[16]{0:T(128)S(1)}, f32[16]{0:T(128)}, u32[]{:S(2)}) copy-start(f32[16]{0:T(128)} %class_shift_ref.1) | copy-start | bytes 196

commit v3 on v2

v3 whole, which is shorter than its diff:
```python
import jax
import jax.numpy as jnp
from jax import lax
from jax.experimental import pallas as pl
from jax.experimental.pallas import tpu as pltpu
from jax.sharding import PartitionSpec as P

NODES = 64
CLASSES = 16
SLABS = 16
RELAX = 0.6
F32 = jnp.float32
HIGHEST = lax.Precision.HIGHEST
AXES = ("gx", "gy", "gz")


def dot(left, right):
    return jnp.dot(left, right, precision=HIGHEST, preferred_element_type=F32)


def iota(shape, dim):
    return lax.broadcasted_iota(jnp.int32, shape, dim)


def roll(values, shift, axis):
    return pltpu.roll(values, shift % values.shape[axis], axis)


def lane_places(shape):
    lane = iota(shape, len(shape) - 1)
    yd = (lane * 171) >> 12
    rest = lane - 24 * yd
    return rest >> 1, yd, rest & 1


def beside_1(v, lane, sub):
    a, b, gy = lane >> 6, (lane >> 4) & 3, lane & 15
    swapped = [roll(x, 64, 1) for x in v]
    result = []
    for gx in range(8):
        x = v[gx]
        total = swapped[gx] + jnp.where((gy & 1) == 0, roll(x, -1, 1), roll(x, 1, 1))
        if gx % 2 == 0:
            total = total + jnp.where(a == 1, swapped[gx + 1], 0.0)
        else:
            total = total + jnp.where(a == 0, swapped[gx - 1], 0.0)
        after = jnp.where((sub & 1) == 0, roll(roll(x, -1, 0), 48, 1), 0.0)
        before = jnp.where((sub & 1) == 1, roll(roll(x, 1, 0), -48, 1), 0.0)
        total = total + jnp.where(b < 3, roll(x, -16, 1), after)
        total = total + jnp.where(b > 0, roll(x, 16, 1), before)
        result.append(total)
    return result


def beside_2(v, lane, sub):
    b, gy = (lane >> 4) & 3, lane & 15
    result = []
    for gx in range(8):
        x = v[gx]
        total = jnp.where((gy & 2) == 0, roll(x, -2, 1), roll(x, 2, 1))
        if gx % 4 < 3:
            total = total + v[gx + 1]
        if gx % 4 > 0:
            total = total + v[gx - 1]
        after = jnp.where((sub & 3) < 3, roll(roll(x, -1, 0), 32, 1), 0.0)
        before = jnp.where((sub & 3) > 0, roll(roll(x, 1, 0), -32, 1), 0.0)
        total = total + jnp.where(b < 2, roll(x, -32, 1), after)
        total = total + jnp.where(b >= 2, roll(x, 32, 1), before)
        result.append(total)
    return result


def beside_3(v, lane, sub):
    gy = lane & 15
    result = []
    for gx in range(8):
        x = v[gx]
        total = jnp.where((gy & 4) == 0, roll(x, -4, 1), roll(x, 4, 1))
        if gx + 2 < 8:
            total = total + v[gx + 2]
        if gx - 2 >= 0:
            total = total + v[gx - 2]
        total = total + jnp.where(sub < 7, roll(x, -1, 0), 0.0)
        total = total + jnp.where(sub > 0, roll(x, 1, 0), 0.0)
        result.append(total)
    return result


def coarsen_1(v, lane):
    b, gy = (lane >> 4) & 3, lane & 15
    result = []
    for x in v:
        x = x + roll(x, 64, 1)
        x = x + jnp.where((b & 1) == 0, roll(x, -16, 1), roll(x, 16, 1))
        x = x + jnp.where((gy & 1) == 0, roll(x, -1, 1), roll(x, 1, 1))
        result.append(x)
    return result


def coarsen_2(v, lane):
    b, gy = (lane >> 4) & 3, lane & 15
    result = []
    for gx in range(8):
        x = v[gx] + v[gx ^ 1]
        x = x + jnp.where(b < 2, roll(x, -32, 1), roll(x, 32, 1))
        x = x + jnp.where((gy & 2) == 0, roll(x, -2, 1), roll(x, 2, 1))
        result.append(x)
    return result


def coarse_cycle(source, shift):
    lane, sub = iota((8, 128), 1), iota((8, 128), 0)
    eight = range(8)

    def remainder(beside, q, d, x):
        around = beside(x, lane, sub)
        return [q[i] - (d[i] * x[i] - around[i]) for i in eight]

    d1 = [6.0 + s for s in shift]
    shift2 = [0.125 * s for s in coarsen_1(shift, lane)]
    d2 = [6.0 + s for s in shift2]
    d3 = [6.0 + 0.125 * s for s in coarsen_2(shift2, lane)]
    w1 = [RELAX / d for d in d1]
    w2 = [RELAX / d for d in d2]
    w3 = [RELAX / d for d in d3]
    x1 = [w1[i] * source[i] for i in eight]
    q2 = [0.25 * t for t in coarsen_1(remainder(beside_1, source, d1, x1), lane)]
    x2 = [w2[i] * q2[i] for i in eight]
    q3 = [0.25 * t for t in coarsen_2(remainder(beside_2, q2, d2, x2), lane)]
    x3 = [w3[i] * q3[i] for i in eight]
    for _ in range(3):
        t3 = remainder(beside_3, q3, d3, x3)
        x3 = [x3[i] + w3[i] * t3[i] for i in eight]
    x2 = [x2[i] + x3[i] for i in eight]
    t2 = remainder(beside_2, q2, d2, x2)
    x2 = [x2[i] + w2[i] * t2[i] for i in eight]
    x1 = [x1[i] + x2[i] for i in eight]
    t1 = remainder(beside_1, source, d1, x1)
    return [x1[i] + w1[i] * t1[i] for i in eight]


def place_correction(coarse, place_ref, pad_ref, rows_ref, out_ref):
    gx0, gy0, gz0 = place_ref[0], place_ref[1], place_ref[2]
    pad_ref[...] = jnp.zeros_like(pad_ref)
    for gx in range(8):
        pad_ref[gx + 1, 8:16, :] = coarse[gx]
    rows_ref[...] = jnp.zeros_like(rows_ref)
    for e in range(3):
        for d in range(3):
            rows_ref[3 * e + d : 3 * e + d + 1, :] = pad_ref[gx0 + d, pl.ds(gz0 + 7 + e, 1), :]
    shape = (128, 512)
    source = iota(shape, 0)
    column = iota(shape, 1)
    target = column & 127
    yd = (target * 171) >> 12
    x = (target - 24 * yd) >> 1
    hit = ((source >> 4) & 3) == (column >> 7)
    hit = hit & ((source >> 6) == ((x >> 1) & 1))
    hit = hit & ((source & 15) == gy0 - 2 + yd) & (target < 120)
    spread = dot(rows_ref[...], jnp.where(hit, 1.0, 0.0))
    lane_x, _, _ = lane_places((1, 128))
    part = lane_x >> 2
    for t in range(8):
        e, b = (t + 2) // 4, (t + 2) % 4
        pieces = [spread[3 * e + d : 3 * e + d + 1, 128 * b : 128 * b + 128] for d in range(3)]
        row = jnp.where(part == 0, pieces[0], jnp.where(part == 1, pieces[1], pieces[2]))
        out_ref[2 * t : 2 * t + 1, :] = row
        out_ref[2 * t + 1 : 2 * t + 2, :] = row


def groups(values):
    return [values[8 * g : 8 * g + 8] for g in range(8)]


def packed_places(shape):
    lane = iota(shape, len(shape) - 1)
    rest = (lane & 63) + 4
    yd = 1 + ((rest * 171) >> 12)
    rest = rest - 24 * (yd - 1)
    return rest >> 1, yd, rest & 1, lane >> 6


def dense(values, marks, packed_ref):
    first = values.astype(jnp.bfloat16)
    rest = values - first.astype(F32)
    second = rest.astype(jnp.bfloat16)
    third = (rest - second.astype(F32)).astype(jnp.bfloat16)
    stack = jnp.concatenate([first, second, third, first, second, first], axis=0)
    products = jnp.dot(packed_ref[...], stack, preferred_element_type=F32)
    result = []
    for part, row in enumerate(marks):
        row = jnp.broadcast_to(row, (8, 128))
        columns = slice(128 * part, 128 * part + 128)
        chosen = [products[8 * g : 8 * g + 8, columns] for g in range(8)]
        for k in range(1, CLASSES):
            hit = row == k
            for g in range(8):
                at = 64 * k + 8 * g
                chosen[g] = jnp.where(hit, products[at : at + 8, columns], chosen[g])
        result.append(chosen)
    return result


class Full:
    def __init__(self, slab):
        self.parts = groups(slab)
        self.yi = lane_places((8, 128))[2]

    def here(self, g):
        return self.parts[g]

    def shift(self, g, step):
        return roll(self.parts[g], -step, 1)


class Pack:
    def __init__(self, low, high):
        self.low, self.high = groups(low), groups(high)
        self.yi = packed_places((8, 128))[2]

    def here(self, g):
        return self.shift(g, 0)

    def shift(self, g, step):
        lane = iota((8, 128), 1)
        return jnp.where(lane < 64, roll(self.low[g], -28 - step, 1), roll(self.high[g], 36 - step, 1))


class Block(Full):
    def __init__(self, block):
        self.parts = groups(block)
        self.yi = packed_places((8, 128))[2]


def upward_y(view, g):
    return jnp.where(view.yi == 0, view.shift(g, 1), view.shift(g, 23))


def downward_y(view, g):
    return jnp.where(view.yi == 1, view.shift(g, -1), view.shift(g, -23))


def face_weights_of(weights_ref):
    sub = iota((8, 128), 0)
    wx, wy, wz = weights_ref[0], weights_ref[1], weights_ref[2]
    top = jnp.where((sub & 3) == 3, wz, 0.0), jnp.where(sub >= 4, wy, 0.0)
    bottom = jnp.where((sub & 3) == 0, wz, 0.0), jnp.where(sub < 4, wy, 0.0)
    return wx, top, bottom


def coupling(before, view, after, weights_ref):
    wx, (wz_top, wy_top), (wz_bottom, wy_bottom) = face_weights_of(weights_ref)
    result = []
    for g in range(8):
        term = wz_top * roll(after[g], 3, 0) + wz_bottom * roll(before[g], -3, 0)
        if g % 2 == 1:
            term = term + wy_top * roll(upward_y(view, g - 1), 4, 0)
        else:
            term = term + wy_bottom * roll(downward_y(view, g + 1), 4, 0)
        if g >= 6:
            term = term + wx * view.shift(g - 6, 2)
        if g < 2:
            term = term + wx * view.shift(g + 6, -2)
        result.append(term)
    return result


def constant_coupling(before, here, after, yi, weights_ref):
    wx, (wz_top, wy_top), (wz_bottom, wy_bottom) = face_weights_of(weights_ref)

    def wide(row):
        return jnp.broadcast_to(row, (8, 128))

    here = wide(here)
    up = jnp.where(yi == 0, roll(here, -1, 1), roll(here, -23, 1))
    down = jnp.where(yi == 1, roll(here, 1, 1), roll(here, 23, 1))
    along = wz_top * wide(after) + wz_bottom * wide(before)
    even, odd = along + wy_bottom * down, along + wy_top * up
    result = [even if g % 2 == 0 else odd for g in range(8)]
    for g in (0, 1):
        result[g] = result[g] + wx * roll(here, 2, 1)
    for g in (6, 7):
        result[g] = result[g] + wx * roll(here, -2, 1)
    return result


def block_before(ref, j):
    return ref[j - 1] if j > 0 else roll(ref[5], 64, 1)


def block_after(ref, j):
    return ref[j + 1] if j < 5 else roll(ref[0], 64, 1)


def restrict(source_ref, inverse_ref, sums_ref, weights_ref, all_ref, out_ref):
    wx, (wz_top, wy_top), (wz_bottom, wy_bottom) = face_weights_of(weights_ref)
    _, _, yi, _ = packed_places((8, 128))
    totals = []
    for j in range(6):
        r = source_ref[j]
        x = inverse_ref[j] * r
        d = groups(r - sums_ref[j] * x)
        xs = groups(x)
        even = (xs[0] + xs[2]) + (xs[4] + xs[6])
        odd = (xs[1] + xs[3]) + (xs[5] + xs[7])
        local = ((d[0] + d[1]) + (d[2] + d[3])) + ((d[4] + d[5]) + (d[6] + d[7]))
        local = local + wx * (roll(xs[0] + xs[1], -2, 1) + roll(xs[6] + xs[7], 2, 1))
        local = local + wy_bottom * jnp.where(yi == 0, roll(even, -1, 1), roll(even, -23, 1))
        local = local + wy_top * jnp.where(yi == 1, roll(odd, 1, 1), roll(odd, 23, 1))
        totals.append(local)
        all_ref[j] = even + odd
    out_ref[...] = jnp.zeros_like(out_ref)
    for j in range(6):
        value = totals[j] + wz_bottom * block_after(all_ref, j) + wz_top * block_before(all_ref, j)
        out_ref[j : j + 1, :] = jnp.sum(value, axis=0, keepdims=True)


def payload(cells, place_ref, scale):
    shape = (128, 256)
    source, column = iota(shape, 0), iota(shape, 1)
    target, own = column & 127, (source & 63) - 28
    hit = (own >= 0) & (own < 8) & ((source >> 6) == (column >> 7))
    hit = hit & ((own >> 2) == (target >> 6)) & ((target & 15) == place_ref[1])
    spread = dot(cells, jnp.where(hit, scale, 0.0))
    block, column = iota((8, 256), 0), iota((8, 256), 1)
    z = block - 2 + 6 * (column >> 7)
    keep = (block < 6) & (z >= 0) & (z < 8) & ((z >> 1) == ((column >> 4) & 3))
    row = jnp.sum(jnp.where(keep, spread, 0.0), axis=0, keepdims=True)
    return row[:, 0:128] + row[:, 128:256]


def gather_own(planes):
    lane = iota((64, 128), 1)
    result = jnp.zeros((64, 128), F32)
    for z, (plane, first) in enumerate(planes):
        result = jnp.where((lane >> 3) == z, roll(plane, 8 * z - first, 1), result)
    return result


def own_of_packed(blocks):
    return gather_own([(blocks[z + 2], 28) if z < 4 else (blocks[z - 4], 92) for z in range(8)])


def own_rows(first, second, first_ref, second_ref):
    turned = jnp.concatenate([first, second], axis=0).T
    low = iota((8, 128), 1) < 64
    for pair in range(4):
        even = turned[16 * pair : 16 * pair + 8]
        odd = turned[16 * pair + 8 : 16 * pair + 16]
        columns = slice(128 * pair, 128 * pair + 128)
        first_ref[:, columns] = jnp.where(low, even, roll(odd, 64, 1))
        second_ref[:, columns] = jnp.where(low, roll(even, 64, 1), odd)


def coefficients(rows, table_ref):
    halves = []
    for row in rows:
        wide = jnp.broadcast_to(row, (CLASSES, 128))
        halves.append(jnp.where(wide == iota((CLASSES, 128), 0), 1.0, 0.0))
    onehot = jnp.concatenate(halves, axis=1)
    onehot = jnp.concatenate([onehot] * 3, axis=0).astype(jnp.bfloat16)
    return jnp.dot(table_ref[...], onehot, preferred_element_type=F32)


def relaxation(x, yd, slab, place_ref):
    gx, gy = place_ref[0] - 1 + (x >> 2), place_ref[1] - 2 + yd
    gz = place_ref[2] - 1 + ((slab + 4) >> 3)
    inside = (gx >= 0) & (gx < 8) & (gy >= 0) & (gy < 16) & (gz >= 0) & (gz < 8) & (yd < 5)
    return jnp.where(inside, RELAX, 0.0)


def total(values):
    return jnp.sum(jnp.sum(values, axis=0, keepdims=True), axis=1, keepdims=True)


def own_right(own_ref):
    return jnp.concatenate([own_ref[:, 0:256], own_ref[:, 384:640]], axis=1)


def split(values):
    first = values.astype(jnp.bfloat16).astype(F32)
    rest = values - first
    second = rest.astype(jnp.bfloat16).astype(F32)
    return first, second, rest - second


def own_kernel(right_ref, marks_ref, out_ref):
    out_ref[:, 256:384] = jnp.zeros((8, 128), F32)
    for x in range(4):
        rows = slice(2 * x, 2 * x + 2)
        values = right_ref[x]
        out_ref[rows, 0:256] = values[:, 0:256]
        out_ref[rows, 384:640] = values[:, 256:512]
        out_ref[rows, 256:264] = marks_ref[x].astype(F32)


def pack_kernel(blocks_ref, packed_ref, table_ref):
    diagonal = jnp.where(iota((64, 64), 0) == iota((64, 64), 1), 1.0, 0.0)
    low = iota((64, 128), 1) < 64
    rows = []
    for k in range(CLASSES):
        block = blocks_ref[k]
        first, second, third = split(jnp.concatenate([block, block], axis=1))
        at = slice(64 * k, 64 * k + 64)
        packed_ref[at, 0:128] = first.astype(jnp.bfloat16)
        packed_ref[at, 128:256] = jnp.where(low, first, second).astype(jnp.bfloat16)
        packed_ref[at, 256:384] = jnp.where(low, second, third).astype(jnp.bfloat16)
        diag = jnp.sum(block * diagonal, axis=0, keepdims=True)
        rows.append(jnp.concatenate([diag, jnp.sum(block, axis=0, keepdims=True)], axis=1))
    parts = split(jnp.concatenate(rows, axis=0))
    table = jnp.concatenate(list(parts) + [jnp.zeros((80, 128), F32)], axis=0).T
    table_ref[...] = table[:, 0:48].astype(jnp.bfloat16)


def start_kernel(
    place_ref, weights_ref, class_shift_ref, below_ref, here_ref, above_ref, table_ref,
    class_ref, inverse_ref, sums_ref, payload_ref,
    field_ref, all_ref, cells_ref,
):
    def window(block):
        columns = slice(128 * block, 128 * block + 128)
        return jnp.concatenate([below_ref[4:24, columns], here_ref[:, columns], above_ref[0:20, columns]], axis=0)

    for j in (0, 2, 4):
        both = jnp.concatenate([window(2 + j // 2), window(5 + j // 2)], axis=0).T
        field_ref[j] = both[:64]
        field_ref[j + 1] = both[64:]
    marks = window(0)
    marks = jnp.concatenate([marks, marks], axis=0).T[0:16].astype(jnp.int32)
    low = iota((1, 128), 1) < 64
    class_ref[...] = jnp.zeros((8, 128), jnp.int32)
    x, yd, _, half = packed_places((1, 128))
    for j in range(6):
        class_ref[j : j + 1, :] = jnp.where(low, marks[2 + j : 3 + j], marks[8 + j : 9 + j])
    for j in (0, 2, 4):
        both = coefficients([class_ref[j : j + 1, :], class_ref[j + 1 : j + 2, :]], table_ref)
        for part in range(2):
            columns = slice(128 * part, 128 * part + 128)
            relax = relaxation(x, yd, 2 + j + part + 6 * half, place_ref)
            inverse_ref[j + part] = relax / both[:64, columns]
            sums_ref[j + part] = both[64:, columns]
    restrict(field_ref, inverse_ref, sums_ref, weights_ref, all_ref, cells_ref)
    shifts = jnp.zeros((8, 128), F32)
    for k in range(CLASSES):
        shifts = jnp.where(class_ref[...] == k, class_shift_ref[k], shifts)
    payload_ref[:, 0:128] = payload(cells_ref[...], place_ref, 1.0 / NODES)
    payload_ref[:, 128:256] = payload(shifts, place_ref, 0.125)


def local_kernel(
    place_ref, weights_ref, far_below_ref, below_ref, here_ref, above_ref, far_above_ref, table_ref, packed_ref,
    smooth_ref, inverse_ref, keep_ref,
    field_ref, iterate_ref, class_ref,
):
    def turned(block):
        columns = slice(128 * block, 128 * block + 128)
        middle = [ref[:, columns] for ref in (below_ref, here_ref, above_ref)]
        nothing = jnp.zeros((24, 128), F32)
        first = far_below_ref[:, columns] if block < 8 else nothing
        last = far_above_ref[:, columns] if block < 8 else nothing
        return jnp.concatenate([first] + middle + [last, jnp.zeros((8, 128), F32)], axis=0).T

    class_ref[...] = turned(0)[0:16].astype(jnp.int32)
    x, yd, _ = lane_places((1, 128))
    for pair in range(SLABS // 2):
        block = turned(pair + 1)
        both = coefficients([class_ref[2 * pair + i : 2 * pair + i + 1, :] for i in (0, 1)], table_ref)
        for part in range(2):
            s = 2 * pair + part
            columns = slice(128 * part, 128 * part + 128)
            values = block[64 * part : 64 * part + 64]
            inverse = relaxation(x, yd, s, place_ref) / both[:64, columns]
            field_ref[s] = values
            inverse_ref[s] = inverse
            keep_ref[s] = 1.0 - inverse * both[64:, columns]
            iterate_ref[s] = inverse * values
    for s in (0, 15):
        smooth_ref[s] = jnp.zeros((64, 128), F32)
    for s in range(1, 14, 2):
        planes = [iterate_ref[s + i] for i in (-1, 0, 1, 2)]
        marks = [class_ref[s + i : s + i + 1, :] for i in (0, 1)]
        chosen = dense(jnp.concatenate(planes[1:3], axis=1), marks, packed_ref)
        for part in range(2):
            faces = coupling(groups(planes[part]), Full(planes[part + 1]), groups(planes[part + 2]), weights_ref)
            for g in range(8):
                at = (s + part, slice(8 * g, 8 * g + 8))
                value = chosen[part][g] - faces[g]
                smooth_ref[at] = iterate_ref[at] + inverse_ref[at] * (field_ref[at] - value)


def first_kernel(
    place_ref, weights_ref, gathered_ref, local_ref, inverse_ref, keep_ref, class_ref, near_inverse_ref, sums_ref,
    packed_ref, right_ref,
    image_ref, own_direction_ref, own_image_ref, payload_ref,
    smooth_ref, pad_ref, rows_ref, shift_ref, all_ref, cells_ref,
):
    coarse = coarse_cycle(
        [gathered_ref[g, :, 0:128] for g in range(8)], [gathered_ref[g, :, 128:256] for g in range(8)]
    )
    place_correction(coarse, place_ref, pad_ref, rows_ref, shift_ref)
    _, _, yi = lane_places((8, 128))
    for s in range(1, 15):
        here = shift_ref[s : s + 1, :]
        faces = constant_coupling(shift_ref[s - 1 : s, :], here, shift_ref[s + 1 : s + 2, :], yi, weights_ref)
        here = jnp.broadcast_to(here, (8, 128))
        for g in range(8):
            at = (s, slice(8 * g, 8 * g + 8))
            smooth_ref[at] = local_ref[at] + (keep_ref[at] * here + inverse_ref[at] * faces[g])

    lane = iota((64, 128), 1)

    def block(j):
        return jnp.where(lane < 64, roll(smooth_ref[2 + j], -28, 1), roll(smooth_ref[8 + j], 36, 1))

    blocks = [block(j) for j in range(-1, 7)]
    for j in (0, 2, 4):
        marks = [class_ref[j + i : j + i + 1, :] for i in (0, 1)]
        chosen = dense(jnp.concatenate([blocks[j + 1], blocks[j + 2]], axis=1), marks, packed_ref)
        for part in range(2):
            at = j + part
            view = Pack(smooth_ref[2 + at], smooth_ref[8 + at])
            faces = coupling(groups(blocks[at]), view, groups(blocks[at + 2]), weights_ref)
            for g in range(8):
                image_ref[at, 8 * g : 8 * g + 8] = chosen[part][g] - faces[g]
    restrict(image_ref, near_inverse_ref, sums_ref, weights_ref, all_ref, cells_ref)
    payload_ref[:, 0:128] = payload(cells_ref[...], place_ref, 1.0 / NODES)
    own_z = gather_own([(smooth_ref[z + 4], 56) for z in range(8)])
    own_rows(own_z, own_of_packed(image_ref), own_direction_ref, own_image_ref)
    direction = own_direction_ref[...]
    lane = iota((1, 128), 1)
    gamma, delta = total(own_right(right_ref) * direction), total(direction * own_image_ref[...])
    payload_ref[:, 128:256] = jnp.where(lane == 0, gamma, jnp.where(lane == 1, delta, 0.0))


def near_kernel(
    weights_ref, image_ref, class_ref, inverse_ref, packed_ref,
    smooth_ref,
    iterate_ref,
):
    for j in range(6):
        iterate_ref[j] = inverse_ref[j] * image_ref[j]
    for j in (0, 2, 4):
        marks = [class_ref[j + i : j + i + 1, :] for i in (0, 1)]
        chosen = dense(jnp.concatenate([iterate_ref[j], iterate_ref[j + 1]], axis=1), marks, packed_ref)
        for part in range(2):
            at = j + part
            before, after = groups(block_before(iterate_ref, at)), groups(block_after(iterate_ref, at))
            faces = coupling(before, Block(iterate_ref[at]), after, weights_ref)
            for g in range(8):
                place = (at, slice(8 * g, 8 * g + 8))
                value = chosen[part][g] - faces[g]
                smooth_ref[place] = iterate_ref[place] + inverse_ref[place] * (image_ref[place] - value)


def second_kernel(
    place_ref, weights_ref, gathered_ref, shifts_ref, local_ref, class_ref, inverse_ref, sums_ref, packed_ref,
    right_ref, own_direction_ref, own_image_ref,
    residual_ref, smoothed_ref, applied_ref, known_ref, payload_ref,
    smooth_ref, pad_ref, rows_ref, shift_ref, turned_ref, image_ref, near_ref,
):
    coarse = coarse_cycle(
        [gathered_ref[g, :, 0:128] for g in range(8)], [shifts_ref[g, :, 128:256] for g in range(8)]
    )
    place_correction(coarse, place_ref, pad_ref, rows_ref, shift_ref)
    lane = iota((8, 128), 1)
    near_ref[...] = jnp.where(lane < 64, roll(shift_ref[2:10, :], -28, 1), roll(shift_ref[8:16, :], 36, 1))
    _, _, yi, _ = packed_places((8, 128))

    def row(j):
        return near_ref[j : j + 1, :]

    for j in range(6):
        before = row(j - 1) if j > 0 else roll(row(5), 64, 1)
        after = row(j + 1) if j < 5 else roll(row(0), 64, 1)
        faces = constant_coupling(before, row(j), after, yi, weights_ref)
        here = jnp.broadcast_to(row(j), (8, 128))
        for g in range(8):
            at = (j, slice(8 * g, 8 * g + 8))
            inverse = inverse_ref[at]
            smooth_ref[at] = local_ref[at] + (here + inverse * (faces[g] - sums_ref[at] * here))

    own_y = own_of_packed(smooth_ref)
    own_marks = gather_own(
        [(jnp.broadcast_to(class_ref[j : j + 1, :].astype(F32), (64, 128)), first)
         for j, first in [(2, 28), (3, 28), (4, 28), (5, 28), (0, 92), (1, 92), (2, 92), (3, 92)]]
    )
    chosen = dense(own_y, [own_marks[0:1].astype(jnp.int32)], packed_ref)[0]
    for j in range(6):
        before, after = groups(block_before(smooth_ref, j)), groups(block_after(smooth_ref, j))
        faces = coupling(before, Block(smooth_ref[j]), after, weights_ref)
        for g in range(8):
            image_ref[j, 8 * g : 8 * g + 8] = faces[g]
    own_v = jnp.concatenate(chosen, axis=0) - own_of_packed(image_ref)

    sums = gathered_ref[0, :, 128:256]
    for g in range(1, 8):
        sums = sums + gathered_ref[g, :, 128:256]
    sums = jnp.sum(sums, axis=0, keepdims=True)
    known_ref[...] = sums
    step = sums[:, 0:1] / sums[:, 1:2]
    own_rows(own_y, own_v, smoothed_ref, turned_ref)
    smoothed = own_direction_ref[...] - step * smoothed_ref[...]
    smoothed_ref[...] = smoothed
    applied = own_image_ref[...] - step * turned_ref[...]
    applied_ref[...] = applied
    residual = own_right(right_ref) - step * own_image_ref[...]
    residual_ref[...] = residual
    lane = iota((1, 128), 1)
    cross = own_direction_ref[...] * applied + own_image_ref[...] * smoothed
    values = jnp.where(lane == 0, total(residual * smoothed), 0.0)
    values = jnp.where(lane == 1, total(smoothed * applied), values)
    payload_ref[...] = jnp.where(lane == 2, total(cross), values)


def last_kernel(
    parts_ref, known_ref, direction_ref, own_image_ref, smoothed_ref, applied_ref, residual_ref, field_ref, out_ref
):
    totals = parts_ref[0]
    for gx in range(1, 8):
        totals = totals + parts_ref[gx]
    gamma, delta = known_ref[:, 0:1], known_ref[:, 1:2]
    beta = totals[:, 0:1] / gamma
    step = totals[:, 0:1] / (totals[:, 1:2] + beta * (totals[:, 2:3] + beta * delta))
    direction = direction_ref[...]
    field = (gamma / delta) * direction + step * (smoothed_ref[...] + beta * direction)
    residual = residual_ref[...] - step * (applied_ref[...] + beta * own_image_ref[...])
    for x in range(4):
        field_ref[x] = field[2 * x : 2 * x + 2]
        out_ref[x] = residual[2 * x : 2 * x + 2]


VMEM = pl.BlockSpec(memory_space=pltpu.VMEM)
SMEM = pl.BlockSpec(memory_space=pltpu.SMEM)


def call(body, scalars, out_shape, scratch, *args, flops=10**7):
    specs = [SMEM] * scalars + [VMEM] * (len(args) - scalars)
    shapes = [jax.ShapeDtypeStruct(shape, dtype) for shape, dtype in out_shape]
    return pl.pallas_call(
        body,
        out_shape=shapes,
        in_specs=specs,
        out_specs=[VMEM] * len(shapes),
        scratch_shapes=[pltpu.VMEM(shape, dtype) for shape, dtype in scratch],
        cost_estimate=pl.CostEstimate(flops=flops, bytes_accessed=10**6, transcendentals=0),
        compiler_params=pltpu.CompilerParams(vmem_limit_bytes=16 * 1024 * 1024),
    )(*args)


FIELD = ((SLABS, NODES, 128), F32)
BLOCKS = ((6, NODES, 128), F32)
MARKS = ((8, 128), jnp.int32)
OWN = ((8, 512), F32)
CELLS = ((8, 128), F32)
ROW, WIDE = ((1, 128), F32), ((1, 256), F32)
COARSE_SCRATCH = [((10, 24, 128), F32), ((16, 128), F32), ((16, 128), F32)]
SUM_SCRATCH = [((6, 8, 128), F32), CELLS]
PAIR_FLOPS = 2 * 1024 * 384 * 256


def start_call(*args):
    return call(start_kernel, 3, [MARKS, BLOCKS, BLOCKS, WIDE], [BLOCKS] + SUM_SCRATCH, *args)


def local_call(*args):
    scratch = [FIELD, FIELD, ((SLABS, 128), jnp.int32)]
    return call(local_kernel, 2, [FIELD, FIELD, FIELD], scratch, *args, flops=7 * PAIR_FLOPS)


def first_call(*args):
    scratch = [FIELD] + COARSE_SCRATCH + SUM_SCRATCH
    return call(first_kernel, 2, [BLOCKS, OWN, OWN, WIDE], scratch, *args, flops=3 * PAIR_FLOPS)


def near_call(*args):
    return call(near_kernel, 1, [BLOCKS], [BLOCKS], *args, flops=3 * PAIR_FLOPS)[0]


def second_call(*args):
    scratch = [BLOCKS] + COARSE_SCRATCH + [OWN, BLOCKS, CELLS]
    return call(second_kernel, 2, [OWN, OWN, OWN, ROW, ROW], scratch, *args, flops=PAIR_FLOPS)


def shifted(x, axis, step):
    size = lax.axis_size(axis)
    pairs = [(i, i + step) for i in range(size) if 0 <= i + step < size]
    return lax.ppermute(x, axis, pairs)


def extend_xz(own):
    wide = jnp.concatenate([shifted(own, "gx", 1), own, shifted(own, "gx", -1)], axis=0)
    low = shifted(wide[:, 256:640], "gz", 1)
    high = shifted(wide[:, 0:384], "gz", -1)
    nothing = jnp.zeros((24, 112), F32)
    pieces = [low[:, 4:8], wide[:, 256:264], high[:, 256:260], nothing]
    return jnp.concatenate(pieces + [low[:, 128:384], wide[:, 0:256], wide[:, 384:640], high[:, 0:256]], axis=1)


def gather_cells(row):
    parts = lax.all_to_all(jnp.broadcast_to(row[None], (128, 1, 256)), ("gy", "gz"), 0, 0, tiled=True)
    plane = parts.reshape(16, 8, 256).sum(axis=0)
    return lax.all_to_all(jnp.broadcast_to(plane[None], (8, 8, 256)), "gx", 0, 0, tiled=True)


def gather_sum(row):
    parts = lax.all_to_all(jnp.broadcast_to(row[None], (128, 1, 128)), ("gy", "gz"), 0, 0, tiled=True)
    part = parts.reshape(128, 128).sum(axis=0)
    return lax.all_to_all(jnp.broadcast_to(part[None, None], (8, 1, 128)), "gx", 0, 0, tiled=True)


def per_device(right_side, element_class, class_blocks, class_shift, face_weights):
    place = jnp.stack([lax.axis_index(axis) for axis in AXES]).astype(jnp.int32)
    own = call(own_kernel, 0, [((8, 640), F32)], [], right_side, element_class)[0]
    here = extend_xz(own)
    below, above = shifted(here, "gy", 1), shifted(here, "gy", -1)
    packed, table = call(
        pack_kernel, 0, [((CLASSES * NODES, 384), jnp.bfloat16), ((128, 48), jnp.bfloat16)], [], class_blocks
    )
    marks, near_inverse, sums, row = start_call(place, face_weights, class_shift, below, here, above, table)
    gathered = gather_cells(row)
    far_below, far_above = shifted(here[:, 0:1024], "gy", 2), shifted(here[:, 0:1024], "gy", -2)
    local, inverse, keep = local_call(
        place, face_weights, far_below, below, here, above, far_above, table, packed
    )
    image, direction, own_image, row = first_call(
        place, face_weights, gathered, local, inverse, keep, marks, near_inverse, sums, packed, own
    )
    again = gather_cells(row)
    near = near_call(face_weights, image, marks, near_inverse, packed)
    residual, smoothed, applied, known, row = second_call(
        place, face_weights, again, gathered, near, marks, near_inverse, sums, packed, own, direction, own_image
    )
    parts = gather_sum(row)
    shapes = [(right_side.shape, F32)] * 2
    return tuple(call(last_kernel, 0, shapes, [], parts, known, direction, own_image, smoothed, applied, residual))


def solution(mesh):
    in_specs = (P("gx", "gy", "gz"), P("gx", "gy", "gz"), P(), P(), P())
    out_specs = (P("gx", "gy", "gz"), P("gx", "gy", "gz"))
    return jax.shard_map(
        per_device, mesh=mesh, in_specs=in_specs, out_specs=out_specs, check_vma=False
    )
```

time: 173 us -> 165 us (0.954)
  blocking collectives: 117 us -> 56.9 us
  starting transfers between devices: 33.5 us -> 59.8 us
  waiting for transfers between devices: 4.19 us -> 27.3 us
  local copies, waits for them, and re-layouts: 1.72 us -> 6.04 us
    all_to_all x2 -> x1, blocking collectives: 60 us -> 25.2 us  [gather_cells(): lax.all_to_all(jnp.broadcast_to(row[None], (128, 1, 256)), ('gy', 'gz'),...]
    all_to_all x0 -> x3, starting transfers between devices: none -> 30.7 us  [the longest x1 20.1 us: gather_cells(): lax.all_to_all(jnp.broadcast_to(row[None], (128, 1, 256)), ('gy', 'gz'),...]
    all_to_all x2 -> x0, blocking collectives: 25.3 us -> none  [gather_cells(): lax.all_to_all(jnp.broadcast_to(plane[None], (8, 8, 256)), 'gx', 0, 0, ti...]
    all_to_all x0 -> x3, waiting for transfers between devices: none -> 20.5 us  [the longest x1 11.1 us: gather_cells(): lax.all_to_all(jnp.broadcast_to(row[None], (128, 1, 256)), ('gy', 'gz'),...]
    ppermute x8, starting transfers between devices: 33.5 us -> 29.2 us  [shifted(): return lax.ppermute(x, axis, pairs)]
    ppermute x8, waiting for transfers between devices: 4.19 us -> 6.77 us  [shifted(): return lax.ppermute(x, axis, pairs)]
    pallas_call x6 -> x8, Pallas kernels: 15 us -> 13.3 us  [call(): pl.pallas_call(body, out_shape=shapes, in_specs=specs, out_specs=[VMEM] *...]
  transfers between devices with their start and end apart: 8 -> 11, of which waited for: 3 -> 7; matrix products, arithmetic and copies ran while one was open for 0% -> 0% of each run, Pallas kernels for 0% -> 3%
where the time goes in v3:
time: 165 us; the launch traced here: 164 us
  starting transfers between devices  59.8 us (36%)
  blocking collectives  56.9 us (34%)
  waiting for transfers between devices  27.3 us (17%)
  Pallas kernels  13.3 us (8%)
  local copies, waits for them, and re-layouts  6.04 us (4%)
    ppermute x8, starting transfers between devices, shifted(): return lax.ppermute(x, axis, pairs)  29.2 us
    all_to_all x1, blocking collectives, gather_cells(): lax.all_to_all(jnp.broadcast_to(row[None], (128, 1, 256)), ('gy', 'gz'),...  25.2 us
    all_to_all x1, blocking collectives, gather_sum(): lax.all_to_all(jnp.broadcast_to(row[None], (128, 1, 128)), ('gy', 'gz'),...  22.8 us
    all_to_all x1, starting transfers between devices, gather_cells(): lax.all_to_all(jnp.broadcast_to(row[None], (128, 1, 256)), ('gy', 'gz'),...  20.1 us
    pallas_call x8, Pallas kernels, call(): pl.pallas_call(body, out_shape=shapes, in_specs=specs, out_specs=[VMEM] *...  13.3 us
    all_to_all x1, waiting for transfers between devices, gather_cells(): lax.all_to_all(jnp.broadcast_to(row[None], (128, 1, 256)), ('gy', 'gz'),...  11.1 us
    all_to_all x2, starting transfers between devices, gather_cells(): lax.all_to_all(jnp.broadcast_to(plane[None], (8, 8, 256)), 'gx', 0, 0, ti...  10.6 us
    all_to_all x2, waiting for transfers between devices, gather_cells(): lax.all_to_all(jnp.broadcast_to(plane[None], (8, 8, 256)), 'gx', 0, 0, ti...  9.47 us
  transfers between devices with their start and end apart: 11, of which 7 were waited for; matrix products, arithmetic and copies ran while one was open for 0% of the time, Pallas kernels for 3%

profile of v3, /device:TPU:1, one launch (start us, length us, event | category | flops | bytes accessed | tf_op | source)
XLA Modules:
  0.0 164.4 jit_solution(3857351140498481830)
XLA Ops:
  0.6 0.0 copy-start.1
  0.6 0.7 copy-done.1
  1.4 0.7 copy-done.3
  2.0 4.0 %collective-permute-start = (f32[8,640]{1,0:T(8,128)S(1)}, f32[8,640]{1,0:T(8,128)S(1)}, u32[]{:S(2)}, u32[]{:S(2)}) collective-permute-start(f32[8,640]{1,0:T(8,128)S(1)} %shard_map.68.right_ref), channel_id=1, source_target_pairs={{0,128},{128,256},{256,384},{384,512},{512,640},{640,768},{768,896... | collective-permute-start | bytes 61448 | tf_op jit(solution)/shard_map/ppermute | solution.py:687
  6.1 1.3 collective-permute-start.1
  7.4 0.0 copy-start
  7.4 1.0 copy-done
  8.4 0.3 shard_map.69
  8.8 0.0 collective-permute-done
  8.8 1.8 %collective-permute-done.1 = f32[8,640]{1,0:T(8,128)S(1)} collective-permute-done((f32[8,640]{1,0:T(8,128)S(1)}, f32[8,640]{1,0:T(8,128)S(1)}, u32[]{:S(2)}, u32[]{:S(2)}) %collective-permute-start.1) | collective-permute-done | bytes 20512 | tf_op jit(solution)/shard_map/ppermute | solution.py:687
  10.6 5.1 %collective-permute-start.2 = (f32[24,384]{1,0:T(8,128)S(1)}, f32[24,384]{1,0:T(8,128)S(1)}, u32[]{:S(2)}, u32[]{:S(2)}) collective-permute-start(f32[24,384]{1,0:T(8,128)S(1)} %get-tuple-element.41), channel_id=1, source_target_pairs={{0,1},{1,2},{2,3},{3,4},{4,5},{5,6},{6,7},{8,9},{9,10},{10,11},{11... | collective-permute-start | bytes 110600 | tf_op jit(solution)/shard_map/ppermute | solution.py:687
  15.8 10.7 %collective-permute-start.3 = (f32[24,384]{1,0:T(8,128)S(1)}, f32[24,384]{1,0:T(8,128)S(1)}, u32[]{:S(2)}, u32[]{:S(2)}) collective-permute-start(f32[24,384]{1,0:T(8,128)S(1)} %get-tuple-element.40), channel_id=1, source_target_pairs={{1,0},{2,1},{3,2},{4,3},{5,4},{6,5},{7,6},{9,8},{10,9},{11,10},{12... | collective-permute-start | bytes 110600 | tf_op jit(solution)/shard_map/ppermute | solution.py:687
  26.4 0.0 collective-permute-done.2
  26.5 0.6 copy-done.6
  27.1 0.1 slice.42
  27.1 0.1 collective-permute-done.3
  27.3 0.7 slice-done.1
  28.0 0.0 slice-done
  28.0 0.1 concatenate.7.here_ref
  28.1 1.3 collective-permute-start.4
  29.4 1.3 collective-permute-start.5
  30.7 0.1 pad_add_fusion.place_ref
  30.8 1.0 collective-permute-done.4.below_ref
  31.8 3.8 %collective-permute-done.5.above_ref = f32[24,1152]{1,0:T(8,128)S(1)} collective-permute-done((f32[24,1152]{1,0:T(8,128)S(1)}, f32[24,1152]{1,0:T(8,128)S(1)}, u32[]{:S(2)}, u32[]{:S(2)}) %collective-permute-start.5) | collective-permute-done | bytes 110624 | tf_op jit(solution)/shard_map/ppermute | solution.py:687
  35.6 0.0 copy-done.4
  35.6 1.1 shard_map.70
  36.7 0.7 broadcast_in_dim.22
  37.4 20.1 %all-to-all-start = ((f32[128,1,256]{2,1,0:T(1,128)}), f32[128,1,256]{2,1,0:T(1,128)S(1)}, u32[]{:S(2)}, u32[]{:S(2)}) async-start(f32[128,1,256]{2,1,0:T(1,128)} %broadcast_in_dim.22), calls=%async_computation | async-start | bytes 262144 | tf_op jit(solution)/shard_map/all_to_all | solution.py:700
  57.5 4.2 %collective-permute-start.6 = (f32[24,1024]{1,0:T(8,128)S(1)}, f32[24,1024]{1,0:T(8,128)S(1)}, u32[]{:S(2)}, u32[]{:S(2)}) collective-permute-start(f32[24,1024]{1,0:T(8,128)S(1)} %slice.50), channel_id=1, source_target_pairs={{0,16},{8,24},{16,32},{24,40},{32,48},{40,56},{48,64},{56,72},{64,... | collective-permute-start | bytes 294920 | tf_op jit(solution)/shard_map/ppermute | solution.py:687
  61.8 1.3 collective-permute-start.7
  63.1 11.1 %all-to-all-done = f32[128,1,256]{2,1,0:T(1,128)S(1)} async-done(((f32[128,1,256]{2,1,0:T(1,128)}), f32[128,1,256]{2,1,0:T(1,128)S(1)}, u32[]{:S(2)}, u32[]{:S(2)}) %all-to-all-start) | async-done | bytes 131104 | tf_op jit(solution)/shard_map/all_to_all | solution.py:700
  74.2 0.6 broadcast_in_dim.23
  74.8 7.0 %all-to-all-start.1 = ((f32[8,8,256]{2,1,0:T(8,128)}), f32[8,8,256]{2,1,0:T(8,128)S(1)}, u32[]{:S(2)}, u32[]{:S(2)}) async-start(f32[8,8,256]{2,1,0:T(8,128)} %broadcast_in_dim.23), calls=%async_computation.1 | async-start | bytes 131072 | tf_op jit(solution)/shard_map/all_to_all | solution.py:702
  81.8 0.0 collective-permute-done.6.far_below_ref
  81.8 0.0 collective-permute-done.7.far_above_ref
  81.8 3.0 %shard_map.71 = (f32[16,64,128]{2,1,0:T(8,128)S(1)}, f32[16,64,128]{2,1,0:T(8,128)S(1)}, f32[16,64,128]{2,1,0:T(8,128)S(1)}) custom-call(s32[3]{0:T(128)S(1)} %pad_add_fusion.place_ref, f32[3]{0:T(128)S(1)} %copy-done.2, f32[24,1024]{1,0:T(8,128)S(1)} %collective-permute-done.6.far_below_ref, f32[24,1152]{1,0:T(8,128)S(1)} %collective-permute-done.4.below_ref, ...), custom_call_target="tpu_custom_call" | custom-call | flops 1409286144 | bytes 1000000 | tf_op jit(solution)/shard_map/pallas_call | solution.py:639
  84.8 4.1 %all-to-all-done.1.gathered_ref.shifts_ref = f32[8,8,256]{2,1,0:T(8,128)S(1)} async-done(((f32[8,8,256]{2,1,0:T(8,128)}), f32[8,8,256]{2,1,0:T(8,128)S(1)}, u32[]{:S(2)}, u32[]{:S(2)}) %all-to-all-start.1) | async-done | bytes 65568 | tf_op jit(solution)/shard_map/all_to_all | solution.py:702
  88.9 3.5 %shard_map.72 = (f32[6,64,128]{2,1,0:T(8,128)S(1)}, f32[8,512]{1,0:T(8,128)S(1)}, f32[8,512]{1,0:T(8,128)S(1)}, f32[1,256]{1,0:T(1,128)S(1)}) custom-call(s32[3]{0:T(128)S(1)} %pad_add_fusion.place_ref, f32[3]{0:T(128)S(1)} %copy-done.2, f32[8,8,256]{2,1,0:T(8,128)S(1)} %all-to-all-done.1.gathered_ref.shifts_ref, ...), custom_call_target="tpu_custom_call" | custom-call | flops 603979776 | bytes 1000000 | tf_op jit(solution)/shard_map/pallas_call | solution.py:639
  92.5 0.1 broadcast_in_dim.50
  92.5 25.2 %all_to_all.30 = f32[128,1,256]{2,1,0:T(1,128)S(1)} all-to-all(f32[128,1,256]{2,1,0:T(1,128)S(1)} %broadcast_in_dim.50), channel_id=1, replica_groups=mesh['gx'=8,'gy'=16,'gz'=8] {'gy','gz'}, dimensions={0} | all-to-all | bytes 262144 | tf_op jit(solution)/shard_map/all_to_all | solution.py:700
  117.8 0.6 broadcast_in_dim.51
  118.4 3.5 %all-to-all-start.3 = ((f32[8,8,256]{2,1,0:T(8,128)}), f32[8,8,256]{2,1,0:T(8,128)S(1)}, u32[]{:S(2)}, u32[]{:S(2)}) async-start(f32[8,8,256]{2,1,0:T(8,128)} %broadcast_in_dim.51), calls=%async_computation.3 | async-start | bytes 131072 | tf_op jit(solution)/shard_map/all_to_all | solution.py:702
  121.9 1.5 shard_map.73.local_ref
  123.5 5.3 %all-to-all-done.3.gathered_ref = f32[8,8,256]{2,1,0:T(8,128)S(1)} async-done(((f32[8,8,256]{2,1,0:T(8,128)}), f32[8,8,256]{2,1,0:T(8,128)S(1)}, u32[]{:S(2)}, u32[]{:S(2)}) %all-to-all-start.3) | async-done | bytes 65568 | tf_op jit(solution)/shard_map/all_to_all | solution.py:702
  128.8 2.8 %shard_map.74 = (f32[8,512]{1,0:T(8,128)S(1)}, f32[8,512]{1,0:T(8,128)S(1)}, f32[8,512]{1,0:T(8,128)S(1)}, f32[1,128]{1,0:T(1,128)S(1)}, f32[1,128]{1,0:T(1,128)S(1)}) custom-call(s32[3]{0:T(128)S(1)} %pad_add_fusion.place_ref, f32[3]{0:T(128)S(1)} %copy-done.2, f32[8,8,256]{2,1,0:T(8,128)S(1)} %all-to-all-done.3.gathered_ref, ...), custom_call_target="tpu_custom_call" | custom-call | flops 201326592 | bytes 1000000 | tf_op jit(solution)/shard_map/pallas_call | solution.py:639
  131.7 22.8 %all_to_all.31 = f32[128,1,128]{2,1,0:T(1,128)S(1)} all-to-all(f32[128,1,128]{2,1,0:T(1,128)S(1)} %broadcast_in_dim.53), channel_id=1, replica_groups=mesh['gx'=8,'gy'=16,'gz'=8] {'gy','gz'}, dimensions={0} | all-to-all | bytes 131072 | tf_op jit(solution)/shard_map/all_to_all | solution.py:706
  154.5 8.9 %all_to_all.32.parts_ref = f32[8,1,128]{2,1,0:T(1,128)S(1)} all-to-all(f32[8,1,128]{2,1,0:T(1,128)S(1)} %broadcast_in_dim.54), channel_id=1, replica_groups=mesh['gx'=8,'gy'=16,'gz'=8] {'gx'}, dimensions={0} | all-to-all | bytes 8192 | tf_op jit(solution)/shard_map/all_to_all | solution.py:708
  163.4 1.0 shard_map.75
  (22 shorter events, 0.2 us)
Async XLA Ops:
  0.6 0.7 copy-start.1
  1.3 0.7 copy-start.3
  2.0 6.7 %collective-permute-start = (f32[8,640]{1,0:T(8,128)S(1)}, f32[8,640]{1,0:T(8,128)S(1)}, u32[]{:S(2)}, u32[]{:S(2)}) collective-permute-start(f32[8,640]{1,0:T(8,128)S(1)} %shard_map.68.right_ref), channel_id=1, source_target_pairs={{0,128},{128,256},{256,384},{384,512},{512,640},{640,768},{768,896... | collective-permute-start | bytes 61448 | tf_op jit(solution)/shard_map/ppermute | solution.py:687
  6.1 4.5 %collective-permute-start.1 = (f32[8,640]{1,0:T(8,128)S(1)}, f32[8,640]{1,0:T(8,128)S(1)}, u32[]{:S(2)}, u32[]{:S(2)}) collective-permute-start(f32[8,640]{1,0:T(8,128)S(1)} %shard_map.68.right_ref), channel_id=1, source_target_pairs={{128,0},{256,128},{384,256},{512,384},{640,512},{768,640},{896,768... | collective-permute-start | bytes 61448 | tf_op jit(solution)/shard_map/ppermute | solution.py:687
  7.4 1.0 copy-start
  10.6 15.8 %copy-start.5 = (f32[24,640]{1,0:T(8,128)}, f32[24,640]{1,0:T(8,128)S(1)}, u32[]{:S(2)}) copy-start(f32[24,640]{1,0:T(8,128)S(1)} %pad_maximum_fusion) | copy-start | bytes 184324
  10.6 15.8 %collective-permute-start.2 = (f32[24,384]{1,0:T(8,128)S(1)}, f32[24,384]{1,0:T(8,128)S(1)}, u32[]{:S(2)}, u32[]{:S(2)}) collective-permute-start(f32[24,384]{1,0:T(8,128)S(1)} %get-tuple-element.41), channel_id=1, source_target_pairs={{0,1},{1,2},{2,3},{3,4},{4,5},{5,6},{6,7},{8,9},{9,10},{10,11},{11... | collective-permute-start | bytes 110600 | tf_op jit(solution)/shard_map/ppermute | solution.py:687
  15.8 11.5 %collective-permute-start.3 = (f32[24,384]{1,0:T(8,128)S(1)}, f32[24,384]{1,0:T(8,128)S(1)}, u32[]{:S(2)}, u32[]{:S(2)}) collective-permute-start(f32[24,384]{1,0:T(8,128)S(1)} %get-tuple-element.40), channel_id=1, source_target_pairs={{1,0},{2,1},{3,2},{4,3},{5,4},{6,5},{7,6},{9,8},{10,9},{11,10},{12... | collective-permute-start | bytes 110600 | tf_op jit(solution)/shard_map/ppermute | solution.py:687
  26.5 0.6 copy-start.6
  27.3 0.7 slice-start.1
  27.3 0.7 slice-start
  28.1 3.7 %collective-permute-start.4 = (f32[24,1152]{1,0:T(8,128)S(1)}, f32[24,1152]{1,0:T(8,128)S(1)}, u32[]{:S(2)}, u32[]{:S(2)}) collective-permute-start(f32[24,1152]{1,0:T(8,128)S(1)} %concatenate.7.here_ref), channel_id=1, source_target_pairs={{0,8},{8,16},{16,24},{24,32},{32,40},{40,48},{48,56},{56,64},{64,7... | collective-permute-start | bytes 331784 | tf_op jit(solution)/shard_map/ppermute | solution.py:687
  29.4 6.2 %collective-permute-start.5 = (f32[24,1152]{1,0:T(8,128)S(1)}, f32[24,1152]{1,0:T(8,128)S(1)}, u32[]{:S(2)}, u32[]{:S(2)}) collective-permute-start(f32[24,1152]{1,0:T(8,128)S(1)} %concatenate.7.here_ref), channel_id=1, source_target_pairs={{8,0},{16,8},{24,16},{32,24},{40,32},{48,40},{56,48},{64,56},{72,6... | collective-permute-start | bytes 331784 | tf_op jit(solution)/shard_map/ppermute | solution.py:687
  30.8 4.8 %copy-start.2 = (f32[3]{0:T(128)S(1)}, f32[3]{0:T(128)}, u32[]{:S(2)}) copy-start(f32[3]{0:T(128)} %weights_ref.9) | copy-start | bytes 40
  30.8 4.8 %copy-start.4 = (f32[16]{0:T(128)S(1)}, f32[16]{0:T(128)}, u32[]{:S(2)}) copy-start(f32[16]{0:T(128)} %class_shift_ref.1) | copy-start | bytes 196
  37.4 36.7 %all-to-all-start = ((f32[128,1,256]{2,1,0:T(1,128)}), f32[128,1,256]{2,1,0:T(1,128)S(1)}, u32[]{:S(2)}, u32[]{:S(2)}) async-start(f32[128,1,256]{2,1,0:T(1,128)} %broadcast_in_dim.22), calls=%async_computation | async-start | bytes 262144 | tf_op jit(solution)/shard_map/all_to_all | solution.py:700
  57.5 24.3 %collective-permute-start.6 = (f32[24,1024]{1,0:T(8,128)S(1)}, f32[24,1024]{1,0:T(8,128)S(1)}, u32[]{:S(2)}, u32[]{:S(2)}) collective-permute-start(f32[24,1024]{1,0:T(8,128)S(1)} %slice.50), channel_id=1, source_target_pairs={{0,16},{8,24},{16,32},{24,40},{32,48},{40,56},{48,64},{56,72},{64,... | collective-permute-start | bytes 294920 | tf_op jit(solution)/shard_map/ppermute | solution.py:687
  61.8 20.1 %collective-permute-start.7 = (f32[24,1024]{1,0:T(8,128)S(1)}, f32[24,1024]{1,0:T(8,128)S(1)}, u32[]{:S(2)}, u32[]{:S(2)}) collective-permute-start(f32[24,1024]{1,0:T(8,128)S(1)} %slice.50), channel_id=1, source_target_pairs={{16,0},{24,8},{32,16},{40,24},{48,32},{56,40},{64,48},{72,56},{80,... | collective-permute-start | bytes 294920 | tf_op jit(solution)/shard_map/ppermute | solution.py:687
  74.8 14.2 %all-to-all-start.1 = ((f32[8,8,256]{2,1,0:T(8,128)}), f32[8,8,256]{2,1,0:T(8,128)S(1)}, u32[]{:S(2)}, u32[]{:S(2)}) async-start(f32[8,8,256]{2,1,0:T(8,128)} %broadcast_in_dim.23), calls=%async_computation.1 | async-start | bytes 131072 | tf_op jit(solution)/shard_map/all_to_all | solution.py:702
  118.4 10.4 %all-to-all-start.3 = ((f32[8,8,256]{2,1,0:T(8,128)}), f32[8,8,256]{2,1,0:T(8,128)S(1)}, u32[]{:S(2)}, u32[]{:S(2)}) async-start(f32[8,8,256]{2,1,0:T(8,128)} %broadcast_in_dim.51), calls=%async_computation.3 | async-start | bytes 131072 | tf_op jit(solution)/shard_map/all_to_all | solution.py:702

commit v4 on v3

--- a/solution.py
+++ b/solution.py
@@ -384,20 +384,122 @@
     return first, second, rest - second
 
 
-def own_kernel(right_ref, marks_ref, out_ref):
-    out_ref[:, 256:384] = jnp.zeros((8, 128), F32)
+def cell_parts(own_ref, table, weights_ref, shift_ref):
+    pieces = []
+    for pair in range(4):
+        start = 128 * pair if pair < 2 else 128 * pair + 128
+        values = own_ref[:, start : start + 128]
+        pieces += [values, roll(values, 64, 1)]
+    b = jnp.concatenate(pieces + [jnp.zeros((64, 128), F32)], axis=0).T[0:64]
+    turned = jnp.concatenate([own_ref[:, 256:384], jnp.zeros((120, 128), F32)], axis=0).T
+    lane = iota((1, 128), 1)
+    marks = jnp.zeros((1, 128), F32)
+    for z in range(8):
+        marks = jnp.where((lane >> 3) == z, roll(turned[z : z + 1], 8 * z, 1), marks)
+    marks = marks.astype(jnp.int32)
+    both = coefficients([marks], table)
+    x0 = (RELAX / both[:64]) * b
+    d, xs = groups(b - both[64:] * x0), groups(x0)
+    wx, wy, wz = weights_ref[0], weights_ref[1], weights_ref[2]
+    sub = iota((8, 128), 0)
+    even = (xs[0] + xs[2]) + (xs[4] + xs[6])
+    odd = (xs[1] + xs[3]) + (xs[5] + xs[7])
+    every = even + odd
+
+    def along(values):
+        return jnp.sum(values, axis=0, keepdims=True)
+
+    local = along(((d[0] + d[1]) + (d[2] + d[3])) + ((d[4] + d[5]) + (d[6] + d[7])))
+    x_low, x_high = wx * along(xs[0] + xs[1]), wx * along(xs[6] + xs[7])
+    y_low, y_high = wy * along(jnp.where(sub < 4, even, 0.0)), wy * along(jnp.where(sub >= 4, odd, 0.0))
+    z_low = wz * along(jnp.where((sub & 3) == 0, every, 0.0))
+    z_high = wz * along(jnp.where((sub & 3) == 3, every, 0.0))
+    x, yi, z = (lane >> 1) & 3, lane & 1, lane >> 3
+    local = local + jnp.where(x > 0, roll(x_high, 2, 1), 0.0) + jnp.where(x < 3, roll(x_low, -2, 1), 0.0)
+    local = local + jnp.where(yi == 1, roll(y_high, 1, 1), roll(y_low, -1, 1))
+    local = local + jnp.where(z > 0, roll(z_high, 8, 1), 0.0) + jnp.where(z < 7, roll(z_low, -8, 1), 0.0)
+    shifts = jnp.zeros((1, 128), F32)
+    for k in range(CLASSES):
+        shifts = jnp.where(marks == k, shift_ref[k], shifts)
+    scale = 1.0 / NODES
+    return jnp.concatenate(
+        [
+            scale * local,
+            scale * jnp.where(yi == 1, y_high, 0.0),
+            scale * jnp.where(yi == 0, y_low, 0.0),
+            0.125 * shifts,
+            scale * jnp.where(x == 3, x_high, jnp.where(x == 0, x_low, 0.0)),
+            scale * jnp.where(z == 7, z_high, jnp.where(z == 0, z_low, 0.0)),
+            jnp.zeros((2, 128), F32),
+        ],
+        axis=0,
+    )
+
+
+def front_kernel(
+    place_ref, weights_in, shift_in, right_in, marks_in, blocks_in,
+    own_ref, table_ref, payload_ref,
+    weights_ref, shift_ref, right_ref, marks_ref, blocks_ref, sems,
+):
+    moves = [(blocks_in, blocks_ref), (right_in, right_ref), (marks_in, marks_ref)]
+    moves += [(weights_in, weights_ref), (shift_in, shift_ref)]
+    copies = [pltpu.make_async_copy(source, target, sems.at[i]) for i, (source, target) in enumerate(moves)]
+    for copy in copies:
+        copy.start()
+    for copy in copies:
+        copy.wait()
+    own_ref[:, 256:384] = jnp.zeros((8, 128), F32)
     for x in range(4):
         rows = slice(2 * x, 2 * x + 2)
         values = right_ref[x]
-        out_ref[rows, 0:256] = values[:, 0:256]
-        out_ref[rows, 384:640] = values[:, 256:512]
-        out_ref[rows, 256:264] = marks_ref[x].astype(F32)
-
-
-def pack_kernel(blocks_ref, packed_ref, table_ref):
+        own_ref[rows, 0:256] = values[:, 0:256]
+        own_ref[rows, 384:640] = values[:, 256:512]
+        own_ref[rows, 256:264] = marks_ref[x].astype(F32)
     diagonal = jnp.where(iota((64, 64), 0) == iota((64, 64), 1), 1.0, 0.0)
+    rows = []
+    for k in range(CLASSES):
+        block = blocks_ref[k]
+        diag = jnp.sum(block * diagonal, axis=0, keepdims=True)
+        rows.append(jnp.concatenate([diag, jnp.sum(block, axis=0, keepdims=True)], axis=1))
+    parts = split(jnp.concatenate(rows, axis=0))
+    table = jnp.concatenate(list(parts) + [jnp.zeros((80, 128), F32)], axis=0).T
+    table_ref[...] = table[:, 0:48].astype(jnp.bfloat16)
+
+    parts = cell_parts(own_ref, table_ref, weights_ref, shift_ref)
+    shape = (128, 128)
+    source, target = iota(shape, 0), iota(shape, 1)
+    hit = (source < 64) & (((source >> 2) & 1) == (target >> 6)) & ((source >> 4) == ((target >> 4) & 3))
+    cells = dot(parts, jnp.where(hit, 1.0, 0.0))
+    lane = iota((1, 128), 1)
+    b, gy, gy0 = (lane >> 4) & 3, lane & 15, place_ref[1]
+    own = gy == gy0
+    row = jnp.where(own, cells[0:1], jnp.where(gy == gy0 + 1, cells[1:2], 0.0))
+    payload_ref[:, 0:128] = row + jnp.where(gy == gy0 - 1, cells[2:3], 0.0)
+    payload_ref[:, 128:256] = jnp.where(own, cells[3:4], 0.0)
+    payload_ref[:, 256:384] = jnp.where(own, roll(cells[4:5], 64, 1), 0.0)
+    high = jnp.where(own & (b == 3), roll(cells[5:6], 48, 1), 0.0)
+    payload_ref[:, 384:512] = jnp.where(own & (b == 0), roll(cells[5:6], -48, 1), high)
+
+
+def join_parts(gathered_ref):
+    lane, sub = iota((8, 128), 1), iota((8, 128), 0)
+    a, b = lane >> 6, (lane >> 4) & 3
+    result = []
+    for gx in range(8):
+        value = gathered_ref[gx, :, 0:128]
+        if gx > 0:
+            value = value + jnp.where(a == 0, gathered_ref[gx - 1, :, 256:384], 0.0)
+        if gx < 7:
+            value = value + jnp.where(a == 1, gathered_ref[gx + 1, :, 256:384], 0.0)
+        z = gathered_ref[gx, :, 384:512]
+        value = value + jnp.where((b == 0) & (sub > 0), roll(z, 1, 0), 0.0)
+        value = value + jnp.where((b == 3) & (sub < 7), roll(z, -1, 0), 0.0)
+        result.append(value)
+    return result
+
+
+def pack_kernel(blocks_ref, packed_ref):
     low = iota((64, 128), 1) < 64
-    rows = []
     for k in range(CLASSES):
         block = blocks_ref[k]
         first, second, third = split(jnp.concatenate([block, block], axis=1))
@@ -405,27 +507,10 @@
         packed_ref[at, 0:128] = first.astype(jnp.bfloat16)
         packed_ref[at, 128:256] = jnp.where(low, first, second).astype(jnp.bfloat16)
         packed_ref[at, 256:384] = jnp.where(low, second, third).astype(jnp.bfloat16)
-        diag = jnp.sum(block * diagonal, axis=0, keepdims=True)
-        rows.append(jnp.concatenate([diag, jnp.sum(block, axis=0, keepdims=True)], axis=1))
-    parts = split(jnp.concatenate(rows, axis=0))
-    table = jnp.concatenate(list(parts) + [jnp.zeros((80, 128), F32)], axis=0).T
-    table_ref[...] = table[:, 0:48].astype(jnp.bfloat16)
-
-
-def start_kernel(
-    place_ref, weights_ref, class_shift_ref, below_ref, here_ref, above_ref, table_ref,
-    class_ref, inverse_ref, sums_ref, payload_ref,
-    field_ref, all_ref, cells_ref,
-):
-    def window(block):
-        columns = slice(128 * block, 128 * block + 128)
-        return jnp.concatenate([below_ref[4:24, columns], here_ref[:, columns], above_ref[0:20, columns]], axis=0)
-
-    for j in (0, 2, 4):
-        both = jnp.concatenate([window(2 + j // 2), window(5 + j // 2)], axis=0).T
-        field_ref[j] = both[:64]
-        field_ref[j + 1] = both[64:]
-    marks = window(0)
+
+
+def coefficient_kernel(place_ref, below_ref, here_ref, above_ref, table_ref, class_ref, inverse_ref, sums_ref):
+    marks = jnp.concatenate([below_ref[4:24, 0:128], here_ref[:, 0:128], above_ref[0:20, 0:128]], axis=0)
     marks = jnp.concatenate([marks, marks], axis=0).T[0:16].astype(jnp.int32)
     low = iota((1, 128), 1) < 64
     class_ref[...] = jnp.zeros((8, 128), jnp.int32)
@@ -439,12 +524,6 @@
             relax = relaxation(x, yd, 2 + j + part + 6 * half, place_ref)
             inverse_ref[j + part] = relax / both[:64, columns]
             sums_ref[j + part] = both[64:, columns]
-    restrict(field_ref, inverse_ref, sums_ref, weights_ref, all_ref, cells_ref)
-    shifts = jnp.zeros((8, 128), F32)
-    for k in range(CLASSES):
-        shifts = jnp.where(class_ref[...] == k, class_shift_ref[k], shifts)
-    payload_ref[:, 0:128] = payload(cells_ref[...], place_ref, 1.0 / NODES)
-    payload_ref[:, 128:256] = payload(shifts, place_ref, 0.125)
 
 
 def local_kernel(
@@ -455,9 +534,7 @@
     def turned(block):
         columns = slice(128 * block, 128 * block + 128)
         middle = [ref[:, columns] for ref in (below_ref, here_ref, above_ref)]
-        nothing = jnp.zeros((24, 128), F32)
-        first = far_below_ref[:, columns] if block < 8 else nothing
-        last = far_above_ref[:, columns] if block < 8 else nothing
+        first, last = far_below_ref[:, columns], far_above_ref[:, columns]
         return jnp.concatenate([first] + middle + [last, jnp.zeros((8, 128), F32)], axis=0).T
 
     class_ref[...] = turned(0)[0:16].astype(jnp.int32)
@@ -494,9 +571,7 @@
     image_ref, own_direction_ref, own_image_ref, payload_ref,
     smooth_ref, pad_ref, rows_ref, shift_ref, all_ref, cells_ref,
 ):
-    coarse = coarse_cycle(
-        [gathered_ref[g, :, 0:128] for g in range(8)], [gathered_ref[g, :, 128:256] for g in range(8)]
-    )
+    coarse = coarse_cycle(join_parts(gathered_ref), [gathered_ref[g, :, 128:256] for g in range(8)])
     place_correction(coarse, place_ref, pad_ref, rows_ref, shift_ref)
     _, _, yi = lane_places((8, 128))
     for s in range(1, 15):
@@ -633,15 +708,15 @@
 SMEM = pl.BlockSpec(memory_space=pltpu.SMEM)
 
 
-def call(body, scalars, out_shape, scratch, *args, flops=10**7):
-    specs = [SMEM] * scalars + [VMEM] * (len(args) - scalars)
+def call(body, scalars, out_shape, scratch, *args, flops=10**7, space=VMEM):
+    specs = [SMEM] * scalars + [space] * (len(args) - scalars)
     shapes = [jax.ShapeDtypeStruct(shape, dtype) for shape, dtype in out_shape]
     return pl.pallas_call(
         body,
         out_shape=shapes,
         in_specs=specs,
         out_specs=[VMEM] * len(shapes),
-        scratch_shapes=[pltpu.VMEM(shape, dtype) for shape, dtype in scratch],
+        scratch_shapes=[entry if not isinstance(entry, tuple) else pltpu.VMEM(*entry) for entry in scratch],
         cost_estimate=pl.CostEstimate(flops=flops, bytes_accessed=10**6, transcendentals=0),
         compiler_params=pltpu.CompilerParams(vmem_limit_bytes=16 * 1024 * 1024),
     )(*args)
@@ -658,8 +733,19 @@
 PAIR_FLOPS = 2 * 1024 * 384 * 256
 
 
-def start_call(*args):
-    return call(start_kernel, 3, [MARKS, BLOCKS, BLOCKS, WIDE], [BLOCKS] + SUM_SCRATCH, *args)
+def front_call(*args):
+    scratch = [pltpu.SMEM((3,), F32), pltpu.SMEM((CLASSES,), F32), ((4, 2, 512), F32), ((4, 2, 8), jnp.int32)]
+    scratch += [((CLASSES, NODES, NODES), F32), pltpu.SemaphoreType.DMA((5,))]
+    shapes = [((8, 640), F32), ((128, 48), jnp.bfloat16), ((1, 512), F32)]
+    return call(front_kernel, 1, shapes, scratch, *args, space=pl.BlockSpec(memory_space=pltpu.HBM))
+
+
+def pack_call(blocks):
+    return call(pack_kernel, 0, [((CLASSES * NODES, 384), jnp.bfloat16)], [], blocks)[0]
+
+
+def coefficient_call(*args):
+    return call(coefficient_kernel, 1, [MARKS, BLOCKS, BLOCKS], [], *args)
 
 
 def local_call(*args):
@@ -697,9 +783,10 @@
 
 
 def gather_cells(row):
-    parts = lax.all_to_all(jnp.broadcast_to(row[None], (128, 1, 256)), ("gy", "gz"), 0, 0, tiled=True)
-    plane = parts.reshape(16, 8, 256).sum(axis=0)
-    return lax.all_to_all(jnp.broadcast_to(plane[None], (8, 8, 256)), "gx", 0, 0, tiled=True)
+    width = row.shape[1]
+    parts = lax.all_to_all(jnp.broadcast_to(row[None], (128, 1, width)), ("gy", "gz"), 0, 0, tiled=True)
+    plane = parts.reshape(16, 8, width).sum(axis=0)
+    return lax.all_to_all(jnp.broadcast_to(plane[None], (8, 8, width)), "gx", 0, 0, tiled=True)
 
 
 def gather_sum(row):
@@ -710,15 +797,13 @@
 
 def per_device(right_side, element_class, class_blocks, class_shift, face_weights):
     place = jnp.stack([lax.axis_index(axis) for axis in AXES]).astype(jnp.int32)
-    own = call(own_kernel, 0, [((8, 640), F32)], [], right_side, element_class)[0]
+    own, table, row = front_call(place, face_weights, class_shift, right_side, element_class, class_blocks)
+    gathered = gather_cells(row)
+    packed = pack_call(class_blocks)
     here = extend_xz(own)
     below, above = shifted(here, "gy", 1), shifted(here, "gy", -1)
-    packed, table = call(
-        pack_kernel, 0, [((CLASSES * NODES, 384), jnp.bfloat16), ((128, 48), jnp.bfloat16)], [], class_blocks
-    )
-    marks, near_inverse, sums, row = start_call(place, face_weights, class_shift, below, here, above, table)
-    gathered = gather_cells(row)
-    far_below, far_above = shifted(here[:, 0:1024], "gy", 2), shifted(here[:, 0:1024], "gy", -2)
+    far_below, far_above = shifted(here, "gy", 2), shifted(here, "gy", -2)
+    marks, near_inverse, sums = coefficient_call(place, below, here, above, table)
     local, inverse, keep = local_call(
         place, face_weights, far_below, below, here, above, far_above, table, packed
     )

time: 165 us -> 160 us (0.970)
  waiting for transfers between devices: 27.3 us -> 15.1 us
  blocking collectives: 56.9 us -> 67.8 us
  starting transfers between devices: 59.8 us -> 55.3 us
    all_to_all x3, waiting for transfers between devices: 20.5 us -> 6.96 us  [the longest x2 6.96 us: gather_cells(): lax.all_to_all(jnp.broadcast_to(plane[None], (8, 8, width)), 'gx', 0, 0,...]
    all_to_all x1, blocking collectives: 25.2 us -> 36 us  [gather_cells(): lax.all_to_all(jnp.broadcast_to(row[None], (128, 1, width)), ('gy', 'gz')...]
    ppermute x8, starting transfers between devices: 29.2 us -> 20.8 us  [shifted(): return lax.ppermute(x, axis, pairs)]
    all_to_all x3, starting transfers between devices: 30.7 us -> 34.5 us  [the longest x1 24.1 us: gather_cells(): lax.all_to_all(jnp.broadcast_to(row[None], (128, 1, width)), ('gy', 'gz')...]
  transfers between devices with their start and end apart: 11 -> 11, of which waited for: 7 -> 5; matrix products, arithmetic and copies ran while one was open for 0% -> 1% of each run, Pallas kernels for 3% -> 3%
where the time goes in v4:
time: 160 us
  blocking collectives  67.8 us (42%)
  starting transfers between devices  55.3 us (35%)
  waiting for transfers between devices  15.1 us (9%)
  Pallas kernels  14.7 us (9%)
  local copies, waits for them, and re-layouts  5.62 us (4%)
    all_to_all x1, blocking collectives, gather_cells(): lax.all_to_all(jnp.broadcast_to(row[None], (128, 1, width)), ('gy', 'gz')...  36 us
    all_to_all x1, starting transfers between devices, gather_cells(): lax.all_to_all(jnp.broadcast_to(row[None], (128, 1, width)), ('gy', 'gz')...  24.1 us
    all_to_all x1, blocking collectives, gather_sum(): lax.all_to_all(jnp.broadcast_to(row[None], (128, 1, 128)), ('gy', 'gz'),...  22.9 us
    ppermute x8, starting transfers between devices, shifted(): return lax.ppermute(x, axis, pairs)  20.8 us
    pallas_call x8, Pallas kernels, call(): pl.pallas_call(body, out_shape=shapes, in_specs=specs, out_specs=[VMEM] *...  14.7 us
    all_to_all x2, starting transfers between devices, gather_cells(): lax.all_to_all(jnp.broadcast_to(plane[None], (8, 8, width)), 'gx', 0, 0,...  10.4 us
    all_to_all x1, blocking collectives, gather_sum(): lax.all_to_all(jnp.broadcast_to(part[None, None], (8, 1, 128)), 'gx', 0,...  8.89 us
    ppermute x8, waiting for transfers between devices, shifted(): return lax.ppermute(x, axis, pairs)  8.13 us
  transfers between devices with their start and end apart: 11, of which 5 were waited for; matrix products, arithmetic and copies ran while one was open for 1% of the time, Pallas kernels for 3%

profile of v4, /device:TPU:1, one launch (start us, length us, event | category | flops | bytes accessed | tf_op | source)
XLA Modules:
  0.0 159.6 jit_solution(16849624593480305938)
XLA Ops:
  0.6 0.0 copy-start.4
  0.7 0.0 copy-start.3
  0.7 0.0 copy-start.5
  0.7 0.1 pad_add_fusion.place_ref
  0.8 0.6 copy-done.2
  1.4 0.0 copy-done.5
  1.4 1.0 copy-done
  2.4 1.9 %shard_map.68 = (f32[8,640]{1,0:T(8,128)S(1)}, bf16[128,48]{1,0:T(8,128)(2,1)S(1)}, f32[1,512]{1,0:T(1,128)S(1)}) custom-call(s32[3]{0:T(128)S(1)} %pad_add_fusion.place_ref, f32[3]{0:T(128)S(1)} %copy-done.3, f32[16]{0:T(128)S(1)} %copy-done.5, f32[4,2,512]{2,1,0:T(2,128)S(1)} %copy-done.2, s32[4,2,8]{2,1,0:T(2,128)S(1)} %copy-done.4, f32[16,64,64]{2,1,0:T(8,128)S(1)} %copy-done), custom_call_target="tpu_custom_call" | custom-call | flops 10000000 | bytes 1000000 | tf_op jit(solution)/shard_map/pallas_call | solution.py:714
  4.3 0.8 broadcast_in_dim.21
  5.2 24.1 %all-to-all-start = ((f32[128,1,512]{2,1,0:T(1,128)}), f32[128,1,512]{2,1,0:T(1,128)S(1)}, u32[]{:S(2)}, u32[]{:S(2)}) async-start(f32[128,1,512]{2,1,0:T(1,128)} %broadcast_in_dim.21), calls=%async_computation | async-start | bytes 524288 | tf_op jit(solution)/shard_map/all_to_all | solution.py:787
  29.2 3.2 %collective-permute-start = (f32[8,640]{1,0:T(8,128)S(1)}, f32[8,640]{1,0:T(8,128)S(1)}, u32[]{:S(2)}, u32[]{:S(2)}) collective-permute-start(f32[8,640]{1,0:T(8,128)S(1)} %get-tuple-element.21.right_ref), channel_id=1, source_target_pairs={{0,128},{128,256},{256,384},{384,512},{512,640},{640,768},{768,896... | collective-permute-start | bytes 61448 | tf_op jit(solution)/shard_map/ppermute | solution.py:773
  32.4 1.3 collective-permute-start.1
  33.7 0.0 collective-permute-done
  33.8 3.5 %collective-permute-done.1 = f32[8,640]{1,0:T(8,128)S(1)} collective-permute-done((f32[8,640]{1,0:T(8,128)S(1)}, f32[8,640]{1,0:T(8,128)S(1)}, u32[]{:S(2)}, u32[]{:S(2)}) %collective-permute-start.1) | collective-permute-done | bytes 20512 | tf_op jit(solution)/shard_map/ppermute | solution.py:773
  37.3 4.7 %collective-permute-start.2 = (f32[24,384]{1,0:T(8,128)S(1)}, f32[24,384]{1,0:T(8,128)S(1)}, u32[]{:S(2)}, u32[]{:S(2)}) collective-permute-start(f32[24,384]{1,0:T(8,128)S(1)} %get-tuple-element.41), channel_id=1, source_target_pairs={{0,1},{1,2},{2,3},{3,4},{4,5},{5,6},{6,7},{8,9},{9,10},{10,11},{11... | collective-permute-start | bytes 110600 | tf_op jit(solution)/shard_map/ppermute | solution.py:773
  42.0 1.9 %collective-permute-start.3 = (f32[24,384]{1,0:T(8,128)S(1)}, f32[24,384]{1,0:T(8,128)S(1)}, u32[]{:S(2)}, u32[]{:S(2)}) collective-permute-start(f32[24,384]{1,0:T(8,128)S(1)} %get-tuple-element.40), channel_id=1, source_target_pairs={{1,0},{2,1},{3,2},{4,3},{5,4},{6,5},{7,6},{9,8},{10,9},{11,10},{12... | collective-permute-start | bytes 110600 | tf_op jit(solution)/shard_map/ppermute | solution.py:773
  43.9 0.0 collective-permute-done.2
  43.9 0.1 slice.37
  44.0 3.6 %collective-permute-done.3 = f32[24,384]{1,0:T(8,128)S(1)} collective-permute-done((f32[24,384]{1,0:T(8,128)S(1)}, f32[24,384]{1,0:T(8,128)S(1)}, u32[]{:S(2)}, u32[]{:S(2)}) %collective-permute-start.3) | collective-permute-done | bytes 36896 | tf_op jit(solution)/shard_map/ppermute | solution.py:773
  47.6 0.1 concatenate.7.here_ref
  47.7 4.0 %collective-permute-start.4 = (f32[24,1152]{1,0:T(8,128)S(1)}, f32[24,1152]{1,0:T(8,128)S(1)}, u32[]{:S(2)}, u32[]{:S(2)}) collective-permute-start(f32[24,1152]{1,0:T(8,128)S(1)} %concatenate.7.here_ref), channel_id=1, source_target_pairs={{0,16},{8,24},{16,32},{24,40},{32,48},{40,56},{48,64},{56,72},{64,... | collective-permute-start | bytes 331784 | tf_op jit(solution)/shard_map/ppermute | solution.py:773
  51.7 3.1 %collective-permute-start.5 = (f32[24,1152]{1,0:T(8,128)S(1)}, f32[24,1152]{1,0:T(8,128)S(1)}, u32[]{:S(2)}, u32[]{:S(2)}) collective-permute-start(f32[24,1152]{1,0:T(8,128)S(1)} %concatenate.7.here_ref), channel_id=1, source_target_pairs={{0,8},{8,16},{16,24},{24,32},{32,40},{40,48},{48,56},{56,64},{64,7... | collective-permute-start | bytes 331784 | tf_op jit(solution)/shard_map/ppermute | solution.py:773
  54.8 1.3 collective-permute-start.6
  56.1 1.3 collective-permute-start.7
  57.4 0.0 all-to-all-done
  57.4 0.7 broadcast_in_dim.22
  58.1 6.9 %all-to-all-start.1 = ((f32[8,8,512]{2,1,0:T(8,128)}), f32[8,8,512]{2,1,0:T(8,128)S(1)}, u32[]{:S(2)}, u32[]{:S(2)}) async-start(f32[8,8,512]{2,1,0:T(8,128)} %broadcast_in_dim.22), calls=%async_computation.1 | async-start | bytes 262144 | tf_op jit(solution)/shard_map/all_to_all | solution.py:789
  65.0 0.3 shard_map.69.packed_ref
  65.3 0.0 collective-permute-done.5.below_ref
  65.3 0.0 collective-permute-done.6.above_ref
  65.3 0.8 shard_map.71
  66.1 0.0 collective-permute-done.4.far_below_ref
  66.1 1.1 collective-permute-done.7.far_above_ref
  67.2 0.6 copy-done.6
  67.8 0.9 copy-done.7
  68.7 2.9 %shard_map.70 = (f32[16,64,128]{2,1,0:T(8,128)S(1)}, f32[16,64,128]{2,1,0:T(8,128)S(1)}, f32[16,64,128]{2,1,0:T(8,128)S(1)}) custom-call(s32[3]{0:T(128)S(1)} %pad_add_fusion.place_ref, f32[3]{0:T(128)S(1)} %copy-done.3, f32[24,1152]{1,0:T(8,128)S(1)} %collective-permute-done.4.far_below_ref, f32[24,1152]{1,0:T(8,128)S(1)} %collective-permute-done.5.below_ref, ...), custom_call_target="tpu_custom_call" | custom-call | flops 1409286144 | bytes 1000000 | tf_op jit(solution)/shard_map/pallas_call | solution.py:714
  71.7 1.6 %all-to-all-done.1.gathered_ref.shifts_ref = f32[8,8,512]{2,1,0:T(8,128)S(1)} async-done(((f32[8,8,512]{2,1,0:T(8,128)}), f32[8,8,512]{2,1,0:T(8,128)S(1)}, u32[]{:S(2)}, u32[]{:S(2)}) %all-to-all-start.1) | async-done | bytes 131104 | tf_op jit(solution)/shard_map/all_to_all | solution.py:789
  73.3 3.5 %shard_map.72 = (f32[6,64,128]{2,1,0:T(8,128)S(1)}, f32[8,512]{1,0:T(8,128)S(1)}, f32[8,512]{1,0:T(8,128)S(1)}, f32[1,256]{1,0:T(1,128)S(1)}) custom-call(s32[3]{0:T(128)S(1)} %pad_add_fusion.place_ref, f32[3]{0:T(128)S(1)} %copy-done.3, f32[8,8,512]{2,1,0:T(8,128)S(1)} %all-to-all-done.1.gathered_ref.shifts_ref, ...), custom_call_target="tpu_custom_call" | custom-call | flops 603979776 | bytes 1000000 | tf_op jit(solution)/shard_map/pallas_call | solution.py:714
  76.8 0.1 broadcast_in_dim.50
  76.8 36.0 %all_to_all.30 = f32[128,1,256]{2,1,0:T(1,128)S(1)} all-to-all(f32[128,1,256]{2,1,0:T(1,128)S(1)} %broadcast_in_dim.50), channel_id=1, replica_groups=mesh['gx'=8,'gy'=16,'gz'=8] {'gy','gz'}, dimensions={0} | all-to-all | bytes 262144 | tf_op jit(solution)/shard_map/all_to_all | solution.py:787
  112.8 0.6 broadcast_in_dim.51
  113.4 3.5 %all-to-all-start.3 = ((f32[8,8,256]{2,1,0:T(8,128)}), f32[8,8,256]{2,1,0:T(8,128)S(1)}, u32[]{:S(2)}, u32[]{:S(2)}) async-start(f32[8,8,256]{2,1,0:T(8,128)} %broadcast_in_dim.51), calls=%async_computation.3 | async-start | bytes 131072 | tf_op jit(solution)/shard_map/all_to_all | solution.py:789
  117.0 1.5 shard_map.73.local_ref
  118.5 5.3 %all-to-all-done.3.gathered_ref = f32[8,8,256]{2,1,0:T(8,128)S(1)} async-done(((f32[8,8,256]{2,1,0:T(8,128)}), f32[8,8,256]{2,1,0:T(8,128)S(1)}, u32[]{:S(2)}, u32[]{:S(2)}) %all-to-all-start.3) | async-done | bytes 65568 | tf_op jit(solution)/shard_map/all_to_all | solution.py:789
  123.9 2.8 %shard_map.74 = (f32[8,512]{1,0:T(8,128)S(1)}, f32[8,512]{1,0:T(8,128)S(1)}, f32[8,512]{1,0:T(8,128)S(1)}, f32[1,128]{1,0:T(1,128)S(1)}, f32[1,128]{1,0:T(1,128)S(1)}) custom-call(s32[3]{0:T(128)S(1)} %pad_add_fusion.place_ref, f32[3]{0:T(128)S(1)} %copy-done.3, f32[8,8,256]{2,1,0:T(8,128)S(1)} %all-to-all-done.3.gathered_ref, ...), custom_call_target="tpu_custom_call" | custom-call | flops 201326592 | bytes 1000000 | tf_op jit(solution)/shard_map/pallas_call | solution.py:714
  126.7 22.9 %all_to_all.31 = f32[128,1,128]{2,1,0:T(1,128)S(1)} all-to-all(f32[128,1,128]{2,1,0:T(1,128)S(1)} %broadcast_in_dim.53), channel_id=1, replica_groups=mesh['gx'=8,'gy'=16,'gz'=8] {'gy','gz'}, dimensions={0} | all-to-all | bytes 131072 | tf_op jit(solution)/shard_map/all_to_all | solution.py:793
  149.6 8.9 %all_to_all.32.parts_ref = f32[8,1,128]{2,1,0:T(1,128)S(1)} all-to-all(f32[8,1,128]{2,1,0:T(1,128)S(1)} %broadcast_in_dim.54), channel_id=1, replica_groups=mesh['gx'=8,'gy'=16,'gz'=8] {'gx'}, dimensions={0} | all-to-all | bytes 8192 | tf_op jit(solution)/shard_map/all_to_all | solution.py:795
  158.5 1.0 shard_map.75
  (23 shorter events, 0.2 us)
Async XLA Ops:
  0.6 0.7 copy-start.2
  0.6 0.7 copy-start.4
  0.7 0.7 copy-start.3
  0.7 0.7 copy-start.5
  1.4 1.0 copy-start
  5.2 52.2 %all-to-all-start = ((f32[128,1,512]{2,1,0:T(1,128)}), f32[128,1,512]{2,1,0:T(1,128)S(1)}, u32[]{:S(2)}, u32[]{:S(2)}) async-start(f32[128,1,512]{2,1,0:T(1,128)} %broadcast_in_dim.21), calls=%async_computation | async-start | bytes 524288 | tf_op jit(solution)/shard_map/all_to_all | solution.py:787
  29.2 4.5 %collective-permute-start = (f32[8,640]{1,0:T(8,128)S(1)}, f32[8,640]{1,0:T(8,128)S(1)}, u32[]{:S(2)}, u32[]{:S(2)}) collective-permute-start(f32[8,640]{1,0:T(8,128)S(1)} %get-tuple-element.21.right_ref), channel_id=1, source_target_pairs={{0,128},{128,256},{256,384},{384,512},{512,640},{640,768},{768,896... | collective-permute-start | bytes 61448 | tf_op jit(solution)/shard_map/ppermute | solution.py:773
  32.4 4.8 %collective-permute-start.1 = (f32[8,640]{1,0:T(8,128)S(1)}, f32[8,640]{1,0:T(8,128)S(1)}, u32[]{:S(2)}, u32[]{:S(2)}) collective-permute-start(f32[8,640]{1,0:T(8,128)S(1)} %get-tuple-element.21.right_ref), channel_id=1, source_target_pairs={{128,0},{256,128},{384,256},{512,384},{640,512},{768,640},{896,768... | collective-permute-start | bytes 61448 | tf_op jit(solution)/shard_map/ppermute | solution.py:773
  37.3 6.6 %collective-permute-start.2 = (f32[24,384]{1,0:T(8,128)S(1)}, f32[24,384]{1,0:T(8,128)S(1)}, u32[]{:S(2)}, u32[]{:S(2)}) collective-permute-start(f32[24,384]{1,0:T(8,128)S(1)} %get-tuple-element.41), channel_id=1, source_target_pairs={{0,1},{1,2},{2,3},{3,4},{4,5},{5,6},{6,7},{8,9},{9,10},{10,11},{11... | collective-permute-start | bytes 110600 | tf_op jit(solution)/shard_map/ppermute | solution.py:773
  42.0 5.6 %collective-permute-start.3 = (f32[24,384]{1,0:T(8,128)S(1)}, f32[24,384]{1,0:T(8,128)S(1)}, u32[]{:S(2)}, u32[]{:S(2)}) collective-permute-start(f32[24,384]{1,0:T(8,128)S(1)} %get-tuple-element.40), channel_id=1, source_target_pairs={{1,0},{2,1},{3,2},{4,3},{5,4},{6,5},{7,6},{9,8},{10,9},{11,10},{12... | collective-permute-start | bytes 110600 | tf_op jit(solution)/shard_map/ppermute | solution.py:773
  44.0 21.0 %copy-start.1 = (f32[16,64,64]{2,1,0:T(8,128)S(1)}, f32[16,64,64]{2,1,0:T(8,128)}, u32[]{:S(2)}) copy-start(f32[16,64,64]{2,1,0:T(8,128)} %blocks_ref.1) | copy-start | bytes 786436
  47.7 18.5 %collective-permute-start.4 = (f32[24,1152]{1,0:T(8,128)S(1)}, f32[24,1152]{1,0:T(8,128)S(1)}, u32[]{:S(2)}, u32[]{:S(2)}) collective-permute-start(f32[24,1152]{1,0:T(8,128)S(1)} %concatenate.7.here_ref), channel_id=1, source_target_pairs={{0,16},{8,24},{16,32},{24,40},{32,48},{40,56},{48,64},{56,72},{64,... | collective-permute-start | bytes 331784 | tf_op jit(solution)/shard_map/ppermute | solution.py:773
  51.7 13.6 %collective-permute-start.5 = (f32[24,1152]{1,0:T(8,128)S(1)}, f32[24,1152]{1,0:T(8,128)S(1)}, u32[]{:S(2)}, u32[]{:S(2)}) collective-permute-start(f32[24,1152]{1,0:T(8,128)S(1)} %concatenate.7.here_ref), channel_id=1, source_target_pairs={{0,8},{8,16},{16,24},{24,32},{32,40},{40,48},{48,56},{56,64},{64,7... | collective-permute-start | bytes 331784 | tf_op jit(solution)/shard_map/ppermute | solution.py:773
  54.8 10.5 %collective-permute-start.6 = (f32[24,1152]{1,0:T(8,128)S(1)}, f32[24,1152]{1,0:T(8,128)S(1)}, u32[]{:S(2)}, u32[]{:S(2)}) collective-permute-start(f32[24,1152]{1,0:T(8,128)S(1)} %concatenate.7.here_ref), channel_id=1, source_target_pairs={{8,0},{16,8},{24,16},{32,24},{40,32},{48,40},{56,48},{64,56},{72,6... | collective-permute-start | bytes 331784 | tf_op jit(solution)/shard_map/ppermute | solution.py:773
  56.1 11.1 %collective-permute-start.7 = (f32[24,1152]{1,0:T(8,128)S(1)}, f32[24,1152]{1,0:T(8,128)S(1)}, u32[]{:S(2)}, u32[]{:S(2)}) collective-permute-start(f32[24,1152]{1,0:T(8,128)S(1)} %concatenate.7.here_ref), channel_id=1, source_target_pairs={{16,0},{24,8},{32,16},{40,24},{48,32},{56,40},{64,48},{72,56},{80,... | collective-permute-start | bytes 331784 | tf_op jit(solution)/shard_map/ppermute | solution.py:773
  58.1 15.2 %all-to-all-start.1 = ((f32[8,8,512]{2,1,0:T(8,128)}), f32[8,8,512]{2,1,0:T(8,128)S(1)}, u32[]{:S(2)}, u32[]{:S(2)}) async-start(f32[8,8,512]{2,1,0:T(8,128)} %broadcast_in_dim.22), calls=%async_computation.1 | async-start | bytes 262144 | tf_op jit(solution)/shard_map/all_to_all | solution.py:789
  67.2 0.6 copy-start.6
  67.8 0.9 copy-start.7
  113.4 10.4 %all-to-all-start.3 = ((f32[8,8,256]{2,1,0:T(8,128)}), f32[8,8,256]{2,1,0:T(8,128)S(1)}, u32[]{:S(2)}, u32[]{:S(2)}) async-start(f32[8,8,256]{2,1,0:T(8,128)} %broadcast_in_dim.51), calls=%async_computation.3 | async-start | bytes 131072 | tf_op jit(solution)/shard_map/all_to_all | solution.py:789

commit v5 on v4

--- a/solution.py
+++ b/solution.py
@@ -296,6 +296,7 @@
     wx, (wz_top, wy_top), (wz_bottom, wy_bottom) = face_weights_of(weights_ref)
     _, _, yi, _ = packed_places((8, 128))
     totals = []
+    out_ref[...] = jnp.zeros_like(out_ref)
     for j in range(6):
         r = source_ref[j]
         x = inverse_ref[j] * r
@@ -305,11 +306,11 @@
         odd = (xs[1] + xs[3]) + (xs[5] + xs[7])
         local = ((d[0] + d[1]) + (d[2] + d[3])) + ((d[4] + d[5]) + (d[6] + d[7]))
         local = local + wx * (roll(xs[0] + xs[1], -2, 1) + roll(xs[6] + xs[7], 2, 1))
-        local = local + wy_bottom * jnp.where(yi == 0, roll(even, -1, 1), roll(even, -23, 1))
-        local = local + wy_top * jnp.where(yi == 1, roll(odd, 1, 1), roll(odd, 23, 1))
-        totals.append(local)
+        upper, lower = wy_top * odd, wy_bottom * even
+        totals.append(local + jnp.where(yi == 0, roll(lower, -1, 1), roll(upper, 1, 1)))
         all_ref[j] = even + odd
-    out_ref[...] = jnp.zeros_like(out_ref)
+        out_ref[8 + j : 9 + j, :] = jnp.sum(jnp.where(yi == 1, upper, 0.0), axis=0, keepdims=True)
+        out_ref[16 + j : 17 + j, :] = jnp.sum(jnp.where(yi == 0, lower, 0.0), axis=0, keepdims=True)
     for j in range(6):
         value = totals[j] + wz_bottom * block_after(all_ref, j) + wz_top * block_before(all_ref, j)
         out_ref[j : j + 1, :] = jnp.sum(value, axis=0, keepdims=True)
@@ -318,14 +319,16 @@
 def payload(cells, place_ref, scale):
     shape = (128, 256)
     source, column = iota(shape, 0), iota(shape, 1)
-    target, own = column & 127, (source & 63) - 28
-    hit = (own >= 0) & (own < 8) & ((source >> 6) == (column >> 7))
-    hit = hit & ((own >> 2) == (target >> 6)) & ((target & 15) == place_ref[1])
+    own = (source & 63) - 28
+    hit = (own >= 0) & (own < 8) & ((source >> 6) == (column >> 7)) & ((own >> 2) == ((column & 127) >> 6))
     spread = dot(cells, jnp.where(hit, scale, 0.0))
     block, column = iota((8, 256), 0), iota((8, 256), 1)
     z = block - 2 + 6 * (column >> 7)
     keep = (block < 6) & (z >= 0) & (z < 8) & ((z >> 1) == ((column >> 4) & 3))
-    row = jnp.sum(jnp.where(keep, spread, 0.0), axis=0, keepdims=True)
+    gy, gy0 = column & 15, place_ref[1]
+    value = jnp.where(gy == gy0, spread[0:8], jnp.where(gy == gy0 + 1, spread[8:16], 0.0))
+    value = value + jnp.where(gy == gy0 - 1, spread[16:24], 0.0)
+    row = jnp.sum(jnp.where(keep, value, 0.0), axis=0, keepdims=True)
     return row[:, 0:128] + row[:, 128:256]
 
 
@@ -437,17 +440,9 @@
 
 
 def front_kernel(
-    place_ref, weights_in, shift_in, right_in, marks_in, blocks_in,
+    place_ref, weights_ref, shift_ref, right_ref, marks_ref, blocks_ref,
     own_ref, table_ref, payload_ref,
-    weights_ref, shift_ref, right_ref, marks_ref, blocks_ref, sems,
 ):
-    moves = [(blocks_in, blocks_ref), (right_in, right_ref), (marks_in, marks_ref)]
-    moves += [(weights_in, weights_ref), (shift_in, shift_ref)]
-    copies = [pltpu.make_async_copy(source, target, sems.at[i]) for i, (source, target) in enumerate(moves)]
-    for copy in copies:
-        copy.start()
-    for copy in copies:
-        copy.wait()
     own_ref[:, 256:384] = jnp.zeros((8, 128), F32)
     for x in range(4):
         rows = slice(2 * x, 2 * x + 2)
@@ -527,15 +522,14 @@
 
 
 def local_kernel(
-    place_ref, weights_ref, far_below_ref, below_ref, here_ref, above_ref, far_above_ref, table_ref, packed_ref,
+    place_ref, weights_ref, below_ref, here_ref, above_ref, table_ref, packed_ref,
     smooth_ref, inverse_ref, keep_ref,
     field_ref, iterate_ref, class_ref,
 ):
     def turned(block):
         columns = slice(128 * block, 128 * block + 128)
         middle = [ref[:, columns] for ref in (below_ref, here_ref, above_ref)]
-        first, last = far_below_ref[:, columns], far_above_ref[:, columns]
-        return jnp.concatenate([first] + middle + [last, jnp.zeros((8, 128), F32)], axis=0).T
+        return jnp.concatenate([jnp.zeros((24, 128), F32)] + middle + [jnp.zeros((32, 128), F32)], axis=0).T
 
     class_ref[...] = turned(0)[0:16].astype(jnp.int32)
     x, yd, _ = lane_places((1, 128))
@@ -568,7 +562,7 @@
 def first_kernel(
     place_ref, weights_ref, gathered_ref, local_ref, inverse_ref, keep_ref, class_ref, near_inverse_ref, sums_ref,
     packed_ref, right_ref,
-    image_ref, own_direction_ref, own_image_ref, payload_ref,
+    image_ref, edge_ref, own_direction_ref, own_image_ref, payload_ref,
     smooth_ref, pad_ref, rows_ref, shift_ref, all_ref, cells_ref,
 ):
     coarse = coarse_cycle(join_parts(gathered_ref), [gathered_ref[g, :, 128:256] for g in range(8)])
@@ -597,6 +591,10 @@
             faces = coupling(groups(blocks[at]), view, groups(blocks[at + 2]), weights_ref)
             for g in range(8):
                 image_ref[at, 8 * g : 8 * g + 8] = chosen[part][g] - faces[g]
+    own = (lane & 63) >= 20
+    own = own & ((lane & 63) < 44)
+    for j in range(3):
+        edge_ref[j] = jnp.where(own, image_ref[j], roll(image_ref[j + 3], 32, 1))
     restrict(image_ref, near_inverse_ref, sums_ref, weights_ref, all_ref, cells_ref)
     payload_ref[:, 0:128] = payload(cells_ref[...], place_ref, 1.0 / NODES)
     own_z = gather_own([(smooth_ref[z + 4], 56) for z in range(8)])
@@ -608,11 +606,15 @@
 
 
 def near_kernel(
-    weights_ref, image_ref, class_ref, inverse_ref, packed_ref,
+    weights_ref, own_ref, below_ref, above_ref, class_ref, inverse_ref, packed_ref,
     smooth_ref,
-    iterate_ref,
+    iterate_ref, image_ref,
 ):
+    lane = iota((64, 128), 1) & 63
     for j in range(6):
+        below = roll(below_ref[j % 3], -24 if j < 3 else -56, 1)
+        above = roll(above_ref[j % 3], 24 if j < 3 else -8, 1)
+        image_ref[j] = jnp.where(lane < 20, below, jnp.where(lane < 44, own_ref[j], above))
         iterate_ref[j] = inverse_ref[j] * image_ref[j]
     for j in (0, 2, 4):
         marks = [class_ref[j + i : j + i + 1, :] for i in (0, 1)]
@@ -708,15 +710,15 @@
 SMEM = pl.BlockSpec(memory_space=pltpu.SMEM)
 
 
-def call(body, scalars, out_shape, scratch, *args, flops=10**7, space=VMEM):
-    specs = [SMEM] * scalars + [space] * (len(args) - scalars)
+def call(body, scalars, out_shape, scratch, *args, flops=10**7):
+    specs = [SMEM] * scalars + [VMEM] * (len(args) - scalars)
     shapes = [jax.ShapeDtypeStruct(shape, dtype) for shape, dtype in out_shape]
     return pl.pallas_call(
         body,
         out_shape=shapes,
         in_specs=specs,
         out_specs=[VMEM] * len(shapes),
-        scratch_shapes=[entry if not isinstance(entry, tuple) else pltpu.VMEM(*entry) for entry in scratch],
+        scratch_shapes=[pltpu.VMEM(shape, dtype) for shape, dtype in scratch],
         cost_estimate=pl.CostEstimate(flops=flops, bytes_accessed=10**6, transcendentals=0),
         compiler_params=pltpu.CompilerParams(vmem_limit_bytes=16 * 1024 * 1024),
     )(*args)
@@ -729,15 +731,13 @@
 CELLS = ((8, 128), F32)
 ROW, WIDE = ((1, 128), F32), ((1, 256), F32)
 COARSE_SCRATCH = [((10, 24, 128), F32), ((16, 128), F32), ((16, 128), F32)]
-SUM_SCRATCH = [((6, 8, 128), F32), CELLS]
+SUM_SCRATCH = [((6, 8, 128), F32), ((24, 128), F32)]
+EDGE = ((3, NODES, 128), F32)
 PAIR_FLOPS = 2 * 1024 * 384 * 256
 
 
 def front_call(*args):
-    scratch = [pltpu.SMEM((3,), F32), pltpu.SMEM((CLASSES,), F32), ((4, 2, 512), F32), ((4, 2, 8), jnp.int32)]
-    scratch += [((CLASSES, NODES, NODES), F32), pltpu.SemaphoreType.DMA((5,))]
-    shapes = [((8, 640), F32), ((128, 48), jnp.bfloat16), ((1, 512), F32)]
-    return call(front_kernel, 1, shapes, scratch, *args, space=pl.BlockSpec(memory_space=pltpu.HBM))
+    return call(front_kernel, 3, [((8, 640), F32), ((128, 48), jnp.bfloat16), ((1, 512), F32)], [], *args)
 
 
 def pack_call(blocks):
@@ -755,11 +755,11 @@
 
 def first_call(*args):
     scratch = [FIELD] + COARSE_SCRATCH + SUM_SCRATCH
-    return call(first_kernel, 2, [BLOCKS, OWN, OWN, WIDE], scratch, *args, flops=3 * PAIR_FLOPS)
+    return call(first_kernel, 2, [BLOCKS, EDGE, OWN, OWN, WIDE], scratch, *args, flops=3 * PAIR_FLOPS)
 
 
 def near_call(*args):
-    return call(near_kernel, 1, [BLOCKS], [BLOCKS], *args, flops=3 * PAIR_FLOPS)[0]
+    return call(near_kernel, 1, [BLOCKS], [BLOCKS, BLOCKS], *args, flops=3 * PAIR_FLOPS)[0]
 
 
 def second_call(*args):
@@ -802,16 +802,14 @@
     packed = pack_call(class_blocks)
     here = extend_xz(own)
     below, above = shifted(here, "gy", 1), shifted(here, "gy", -1)
-    far_below, far_above = shifted(here, "gy", 2), shifted(here, "gy", -2)
     marks, near_inverse, sums = coefficient_call(place, below, here, above, table)
-    local, inverse, keep = local_call(
-        place, face_weights, far_below, below, here, above, far_above, table, packed
-    )
-    image, direction, own_image, row = first_call(
+    local, inverse, keep = local_call(place, face_weights, below, here, above, table, packed)
+    image, edge, direction, own_image, row = first_call(
         place, face_weights, gathered, local, inverse, keep, marks, near_inverse, sums, packed, own
     )
     again = gather_cells(row)
-    near = near_call(face_weights, image, marks, near_inverse, packed)
+    from_below, from_above = shifted(edge, "gy", 1), shifted(edge, "gy", -1)
+    near = near_call(face_weights, image, from_below, from_above, marks, near_inverse, packed)
     residual, smoothed, applied, known, row = second_call(
         place, face_weights, again, gathered, near, marks, near_inverse, sums, packed, own, direction, own_image
     )

time: 160 us -> 152 us (0.950)
  blocking collectives: 67.8 us -> 32.2 us
  starting transfers between devices: 55.3 us -> 74.6 us
  waiting for transfers between devices: 15.1 us -> 24.8 us
    all_to_all x1 -> x0, blocking collectives: 36 us -> none  [gather_cells(): lax.all_to_all(jnp.broadcast_to(row[None], (128, 1, width)), ('gy', 'gz')...]
    all_to_all x1 -> x2, starting transfers between devices: 24.1 us -> 42.4 us  [gather_cells(): lax.all_to_all(jnp.broadcast_to(row[None], (128, 1, width)), ('gy', 'gz')...]
    all_to_all x1 -> x2, waiting for transfers between devices: 0.01 us -> 10.8 us  [gather_cells(): lax.all_to_all(jnp.broadcast_to(row[None], (128, 1, width)), ('gy', 'gz')...]
    ppermute x8, waiting for transfers between devices: 8.13 us -> 4.51 us  [shifted(): return lax.ppermute(x, axis, pairs)]
    all_to_all x2, waiting for transfers between devices: 6.96 us -> 9.56 us  [gather_cells(): lax.all_to_all(jnp.broadcast_to(plane[None], (8, 8, width)), 'gx', 0, 0,...]
    unnamed x18 -> x14, local copies, waits for them, and re-layouts: 3.2 us -> 1.66 us
  transfers between devices with their start and end apart: 11 -> 12, of which waited for: 5 -> 5; matrix products, arithmetic and copies ran while one was open for 1% -> 1% of each run, Pallas kernels for 3% -> 4%
where the time goes in v5:
time: 152 us
  starting transfers between devices  74.6 us (49%)
  blocking collectives  32.2 us (21%)
  waiting for transfers between devices  24.8 us (16%)
  Pallas kernels  14.2 us (9%)
  local copies, waits for them, and re-layouts  4.75 us (3%)
    all_to_all x2, starting transfers between devices, gather_cells(): lax.all_to_all(jnp.broadcast_to(row[None], (128, 1, width)), ('gy', 'gz')...  42.4 us
    all_to_all x1, blocking collectives, gather_sum(): lax.all_to_all(jnp.broadcast_to(row[None], (128, 1, 128)), ('gy', 'gz'),...  23.3 us
    ppermute x8, starting transfers between devices, shifted(): return lax.ppermute(x, axis, pairs)  21.6 us
    pallas_call x8, Pallas kernels, call(): pl.pallas_call(body, out_shape=shapes, in_specs=specs, out_specs=[VMEM] *...  14.2 us
    all_to_all x2, waiting for transfers between devices, gather_cells(): lax.all_to_all(jnp.broadcast_to(row[None], (128, 1, width)), ('gy', 'gz')...  10.8 us
    all_to_all x2, starting transfers between devices, gather_cells(): lax.all_to_all(jnp.broadcast_to(plane[None], (8, 8, width)), 'gx', 0, 0,...  10.6 us
    all_to_all x2, waiting for transfers between devices, gather_cells(): lax.all_to_all(jnp.broadcast_to(plane[None], (8, 8, width)), 'gx', 0, 0,...  9.56 us
    all_to_all x1, blocking collectives, gather_sum(): lax.all_to_all(jnp.broadcast_to(part[None, None], (8, 1, 128)), 'gx', 0,...  8.89 us
  transfers between devices with their start and end apart: 12, of which 5 were waited for; matrix products, arithmetic and copies ran while one was open for 1% of the time, Pallas kernels for 4%

profile of v5, /device:TPU:1, one launch (start us, length us, event | category | flops | bytes accessed | tf_op | source)
XLA Modules:
  0.0 151.6 jit_solution(18218818683727887757)
XLA Ops:
  0.6 0.0 copy-start.2
  0.6 0.0 copy-start.4
  0.7 0.0 copy-start.3
  0.7 0.0 copy-start.5
  0.7 0.1 pad_add_fusion.place_ref
  0.8 0.6 copy-done.2
  1.4 0.0 copy-done.5
  1.4 1.0 copy-done
  2.4 1.2 shard_map.68
  3.6 0.9 broadcast_in_dim.21
  4.5 24.1 %all-to-all-start = ((f32[128,1,512]{2,1,0:T(1,128)}), f32[128,1,512]{2,1,0:T(1,128)S(1)}, u32[]{:S(2)}, u32[]{:S(2)}) async-start(f32[128,1,512]{2,1,0:T(1,128)} %broadcast_in_dim.21), calls=%async_computation | async-start | bytes 524288 | tf_op jit(solution)/shard_map/all_to_all | solution.py:787
  28.6 3.2 %collective-permute-start = (f32[8,640]{1,0:T(8,128)S(1)}, f32[8,640]{1,0:T(8,128)S(1)}, u32[]{:S(2)}, u32[]{:S(2)}) collective-permute-start(f32[8,640]{1,0:T(8,128)S(1)} %get-tuple-element.22.right_ref), channel_id=1, source_target_pairs={{0,128},{128,256},{256,384},{384,512},{512,640},{640,768},{768,896... | collective-permute-start | bytes 61448 | tf_op jit(solution)/shard_map/ppermute | solution.py:773
  31.8 1.3 collective-permute-start.1
  33.1 0.0 collective-permute-done
  33.1 3.5 %collective-permute-done.1 = f32[8,640]{1,0:T(8,128)S(1)} collective-permute-done((f32[8,640]{1,0:T(8,128)S(1)}, f32[8,640]{1,0:T(8,128)S(1)}, u32[]{:S(2)}, u32[]{:S(2)}) %collective-permute-start.1) | collective-permute-done | bytes 20512 | tf_op jit(solution)/shard_map/ppermute | solution.py:773
  36.6 3.9 %collective-permute-start.3 = (f32[24,384]{1,0:T(8,128)S(1)}, f32[24,384]{1,0:T(8,128)S(1)}, u32[]{:S(2)}, u32[]{:S(2)}) collective-permute-start(f32[24,384]{1,0:T(8,128)S(1)} %get-tuple-element.42), channel_id=1, source_target_pairs={{1,0},{2,1},{3,2},{4,3},{5,4},{6,5},{7,6},{9,8},{10,9},{11,10},{12... | collective-permute-start | bytes 110600 | tf_op jit(solution)/shard_map/ppermute | solution.py:773
  40.6 2.7 %collective-permute-start.2 = (f32[24,384]{1,0:T(8,128)S(1)}, f32[24,384]{1,0:T(8,128)S(1)}, u32[]{:S(2)}, u32[]{:S(2)}) collective-permute-start(f32[24,384]{1,0:T(8,128)S(1)} %get-tuple-element.43), channel_id=1, source_target_pairs={{0,1},{1,2},{2,3},{3,4},{4,5},{5,6},{6,7},{8,9},{9,10},{10,11},{11... | collective-permute-start | bytes 110600 | tf_op jit(solution)/shard_map/ppermute | solution.py:773
  43.3 0.0 collective-permute-done.3
  43.3 1.0 collective-permute-done.2
  44.3 0.1 slice.37
  44.4 0.1 concatenate.7.here_ref
  44.4 1.3 collective-permute-start.5
  45.7 4.0 %collective-permute-start.4 = (f32[24,1152]{1,0:T(8,128)S(1)}, f32[24,1152]{1,0:T(8,128)S(1)}, u32[]{:S(2)}, u32[]{:S(2)}) collective-permute-start(f32[24,1152]{1,0:T(8,128)S(1)} %concatenate.7.here_ref), channel_id=1, source_target_pairs={{0,8},{8,16},{16,24},{24,32},{32,40},{40,48},{48,56},{56,64},{64,7... | collective-permute-start | bytes 331784 | tf_op jit(solution)/shard_map/ppermute | solution.py:773
  49.7 0.0 all-to-all-done
  49.8 0.7 broadcast_in_dim.22
  50.4 7.0 %all-to-all-start.1 = ((f32[8,8,512]{2,1,0:T(8,128)}), f32[8,8,512]{2,1,0:T(8,128)S(1)}, u32[]{:S(2)}, u32[]{:S(2)}) async-start(f32[8,8,512]{2,1,0:T(8,128)} %broadcast_in_dim.22), calls=%async_computation.1 | async-start | bytes 262144 | tf_op jit(solution)/shard_map/all_to_all | solution.py:789
  57.5 0.3 shard_map.69.packed_ref
  57.7 0.0 collective-permute-done.5.above_ref
  57.7 0.0 collective-permute-done.4.below_ref
  57.8 0.8 shard_map.71
  58.6 2.9 %shard_map.70 = (f32[16,64,128]{2,1,0:T(8,128)S(1)}, f32[16,64,128]{2,1,0:T(8,128)S(1)}, f32[16,64,128]{2,1,0:T(8,128)S(1)}) custom-call(s32[3]{0:T(128)S(1)} %pad_add_fusion.place_ref, f32[3]{0:T(128)S(1)} %copy-done.3, f32[24,1152]{1,0:T(8,128)S(1)} %collective-permute-done.4.below_ref, f32[24,1152]{1,0:T(8,128)S(1)} %concatenate.7.here_ref, ...), custom_call_target="tpu_custom_call" | custom-call | flops 1409286144 | bytes 1000000 | tf_op jit(solution)/shard_map/pallas_call | solution.py:716
  61.5 4.3 %all-to-all-done.1.gathered_ref.shifts_ref = f32[8,8,512]{2,1,0:T(8,128)S(1)} async-done(((f32[8,8,512]{2,1,0:T(8,128)}), f32[8,8,512]{2,1,0:T(8,128)S(1)}, u32[]{:S(2)}, u32[]{:S(2)}) %all-to-all-start.1) | async-done | bytes 131104 | tf_op jit(solution)/shard_map/all_to_all | solution.py:789
  65.8 3.5 %shard_map.72 = (f32[6,64,128]{2,1,0:T(8,128)S(1)}, f32[3,64,128]{2,1,0:T(8,128)S(1)}, f32[8,512]{1,0:T(8,128)S(1)}, f32[8,512]{1,0:T(8,128)S(1)}, f32[1,256]{1,0:T(1,128)S(1)}) custom-call(s32[3]{0:T(128)S(1)} %pad_add_fusion.place_ref, f32[3]{0:T(128)S(1)} %copy-done.3, f32[8,8,512]{2,1,0:T(8,128)S(1)} %all-to-all-done.1.gathered_ref.shifts_ref, ...), custom_call_target="tpu_custom_call" | custom-call | flops 603979776 | bytes 1000000 | tf_op jit(solution)/shard_map/pallas_call | solution.py:716
  69.3 0.7 broadcast_in_dim.50
  70.0 18.3 %all-to-all-start.2 = ((f32[128,1,256]{2,1,0:T(1,128)}), f32[128,1,256]{2,1,0:T(1,128)S(1)}, u32[]{:S(2)}, u32[]{:S(2)}) async-start(f32[128,1,256]{2,1,0:T(1,128)} %broadcast_in_dim.50), calls=%async_computation.2 | async-start | bytes 262144 | tf_op jit(solution)/shard_map/all_to_all | solution.py:787
  88.4 1.3 collective-permute-start.7
  89.7 4.0 %collective-permute-start.6 = (f32[3,64,128]{2,1,0:T(8,128)S(1)}, f32[3,64,128]{2,1,0:T(8,128)S(1)}, u32[]{:S(2)}, u32[]{:S(2)}) collective-permute-start(f32[3,64,128]{2,1,0:T(8,128)S(1)} %get-tuple-element.32), channel_id=1, source_target_pairs={{0,8},{8,16},{16,24},{24,32},{32,40},{40,48},{48,56},{56,64},{64,7... | collective-permute-start | bytes 294920 | tf_op jit(solution)/shard_map/ppermute | solution.py:773
  93.7 10.8 %all-to-all-done.2 = f32[128,1,256]{2,1,0:T(1,128)S(1)} async-done(((f32[128,1,256]{2,1,0:T(1,128)}), f32[128,1,256]{2,1,0:T(1,128)S(1)}, u32[]{:S(2)}, u32[]{:S(2)}) %all-to-all-start.2) | async-done | bytes 131104 | tf_op jit(solution)/shard_map/all_to_all | solution.py:787
  104.5 0.6 broadcast_in_dim.51
  105.1 3.5 %all-to-all-start.3 = ((f32[8,8,256]{2,1,0:T(8,128)}), f32[8,8,256]{2,1,0:T(8,128)S(1)}, u32[]{:S(2)}, u32[]{:S(2)}) async-start(f32[8,8,256]{2,1,0:T(8,128)} %broadcast_in_dim.51), calls=%async_computation.3 | async-start | bytes 131072 | tf_op jit(solution)/shard_map/all_to_all | solution.py:789
  108.6 0.0 collective-permute-done.7.above_ref
  108.6 0.0 collective-permute-done.6.below_ref
  108.6 1.6 %shard_map.73.local_ref = f32[6,64,128]{2,1,0:T(8,128)S(1)} custom-call(f32[3]{0:T(128)S(1)} %copy-done.3, f32[6,64,128]{2,1,0:T(8,128)S(1)} %get-tuple-element.31.own_ref, f32[3,64,128]{2,1,0:T(8,128)S(1)} %collective-permute-done.6.below_ref, f32[3,64,128]{2,1,0:T(8,128)S(1)} %collective-permute-done.7.above_ref, ...), custom_call_target="tpu_custom_call" | custom-call | flops 603979776 | bytes 1000000 | tf_op jit(solution)/shard_map/pallas_call | solution.py:716
  110.3 5.2 %all-to-all-done.3.gathered_ref = f32[8,8,256]{2,1,0:T(8,128)S(1)} async-done(((f32[8,8,256]{2,1,0:T(8,128)}), f32[8,8,256]{2,1,0:T(8,128)S(1)}, u32[]{:S(2)}, u32[]{:S(2)}) %all-to-all-start.3) | async-done | bytes 65568 | tf_op jit(solution)/shard_map/all_to_all | solution.py:789
  115.5 2.8 %shard_map.74 = (f32[8,512]{1,0:T(8,128)S(1)}, f32[8,512]{1,0:T(8,128)S(1)}, f32[8,512]{1,0:T(8,128)S(1)}, f32[1,128]{1,0:T(1,128)S(1)}, f32[1,128]{1,0:T(1,128)S(1)}) custom-call(s32[3]{0:T(128)S(1)} %pad_add_fusion.place_ref, f32[3]{0:T(128)S(1)} %copy-done.3, f32[8,8,256]{2,1,0:T(8,128)S(1)} %all-to-all-done.3.gathered_ref, ...), custom_call_target="tpu_custom_call" | custom-call | flops 201326592 | bytes 1000000 | tf_op jit(solution)/shard_map/pallas_call | solution.py:716
  118.3 23.3 %all_to_all.30 = f32[128,1,128]{2,1,0:T(1,128)S(1)} all-to-all(f32[128,1,128]{2,1,0:T(1,128)S(1)} %broadcast_in_dim.53), channel_id=1, replica_groups=mesh['gx'=8,'gy'=16,'gz'=8] {'gy','gz'}, dimensions={0} | all-to-all | bytes 131072 | tf_op jit(solution)/shard_map/all_to_all | solution.py:793
  141.7 8.9 %all_to_all.31.parts_ref = f32[8,1,128]{2,1,0:T(1,128)S(1)} all-to-all(f32[8,1,128]{2,1,0:T(1,128)S(1)} %broadcast_in_dim.54), channel_id=1, replica_groups=mesh['gx'=8,'gy'=16,'gz'=8] {'gx'}, dimensions={0} | all-to-all | bytes 8192 | tf_op jit(solution)/shard_map/all_to_all | solution.py:795
  150.6 1.0 shard_map.75
  (20 shorter events, 0.2 us)
Async XLA Ops:
  0.6 0.7 copy-start.2
  0.6 0.7 copy-start.4
  0.7 0.7 copy-start.3
  0.7 0.7 copy-start.5
  1.4 1.0 copy-start
  4.5 45.2 %all-to-all-start = ((f32[128,1,512]{2,1,0:T(1,128)}), f32[128,1,512]{2,1,0:T(1,128)S(1)}, u32[]{:S(2)}, u32[]{:S(2)}) async-start(f32[128,1,512]{2,1,0:T(1,128)} %broadcast_in_dim.21), calls=%async_computation | async-start | bytes 524288 | tf_op jit(solution)/shard_map/all_to_all | solution.py:787
  28.6 4.5 %collective-permute-start = (f32[8,640]{1,0:T(8,128)S(1)}, f32[8,640]{1,0:T(8,128)S(1)}, u32[]{:S(2)}, u32[]{:S(2)}) collective-permute-start(f32[8,640]{1,0:T(8,128)S(1)} %get-tuple-element.22.right_ref), channel_id=1, source_target_pairs={{0,128},{128,256},{256,384},{384,512},{512,640},{640,768},{768,896... | collective-permute-start | bytes 61448 | tf_op jit(solution)/shard_map/ppermute | solution.py:773
  31.8 4.8 %collective-permute-start.1 = (f32[8,640]{1,0:T(8,128)S(1)}, f32[8,640]{1,0:T(8,128)S(1)}, u32[]{:S(2)}, u32[]{:S(2)}) collective-permute-start(f32[8,640]{1,0:T(8,128)S(1)} %get-tuple-element.22.right_ref), channel_id=1, source_target_pairs={{128,0},{256,128},{384,256},{512,384},{640,512},{768,640},{896,768... | collective-permute-start | bytes 61448 | tf_op jit(solution)/shard_map/ppermute | solution.py:773
  36.6 6.7 %collective-permute-start.3 = (f32[24,384]{1,0:T(8,128)S(1)}, f32[24,384]{1,0:T(8,128)S(1)}, u32[]{:S(2)}, u32[]{:S(2)}) collective-permute-start(f32[24,384]{1,0:T(8,128)S(1)} %get-tuple-element.42), channel_id=1, source_target_pairs={{1,0},{2,1},{3,2},{4,3},{5,4},{6,5},{7,6},{9,8},{10,9},{11,10},{12... | collective-permute-start | bytes 110600 | tf_op jit(solution)/shard_map/ppermute | solution.py:773
  40.6 3.7 %collective-permute-start.2 = (f32[24,384]{1,0:T(8,128)S(1)}, f32[24,384]{1,0:T(8,128)S(1)}, u32[]{:S(2)}, u32[]{:S(2)}) collective-permute-start(f32[24,384]{1,0:T(8,128)S(1)} %get-tuple-element.43), channel_id=1, source_target_pairs={{0,1},{1,2},{2,3},{3,4},{4,5},{5,6},{6,7},{8,9},{9,10},{10,11},{11... | collective-permute-start | bytes 110600 | tf_op jit(solution)/shard_map/ppermute | solution.py:773
  43.3 14.1 %copy-start.1 = (f32[16,64,64]{2,1,0:T(8,128)S(1)}, f32[16,64,64]{2,1,0:T(8,128)}, u32[]{:S(2)}) copy-start(f32[16,64,64]{2,1,0:T(8,128)} %blocks_ref.3) | copy-start | bytes 786436
  44.4 13.3 %collective-permute-start.5 = (f32[24,1152]{1,0:T(8,128)S(1)}, f32[24,1152]{1,0:T(8,128)S(1)}, u32[]{:S(2)}, u32[]{:S(2)}) collective-permute-start(f32[24,1152]{1,0:T(8,128)S(1)} %concatenate.7.here_ref), channel_id=1, source_target_pairs={{8,0},{16,8},{24,16},{32,24},{40,32},{48,40},{56,48},{64,56},{72,6... | collective-permute-start | bytes 331784 | tf_op jit(solution)/shard_map/ppermute | solution.py:773
  45.7 12.0 %collective-permute-start.4 = (f32[24,1152]{1,0:T(8,128)S(1)}, f32[24,1152]{1,0:T(8,128)S(1)}, u32[]{:S(2)}, u32[]{:S(2)}) collective-permute-start(f32[24,1152]{1,0:T(8,128)S(1)} %concatenate.7.here_ref), channel_id=1, source_target_pairs={{0,8},{8,16},{16,24},{24,32},{32,40},{40,48},{48,56},{56,64},{64,7... | collective-permute-start | bytes 331784 | tf_op jit(solution)/shard_map/ppermute | solution.py:773
  50.4 15.4 %all-to-all-start.1 = ((f32[8,8,512]{2,1,0:T(8,128)}), f32[8,8,512]{2,1,0:T(8,128)S(1)}, u32[]{:S(2)}, u32[]{:S(2)}) async-start(f32[8,8,512]{2,1,0:T(8,128)} %broadcast_in_dim.22), calls=%async_computation.1 | async-start | bytes 262144 | tf_op jit(solution)/shard_map/all_to_all | solution.py:789
  70.0 34.4 %all-to-all-start.2 = ((f32[128,1,256]{2,1,0:T(1,128)}), f32[128,1,256]{2,1,0:T(1,128)S(1)}, u32[]{:S(2)}, u32[]{:S(2)}) async-start(f32[128,1,256]{2,1,0:T(1,128)} %broadcast_in_dim.50), calls=%async_computation.2 | async-start | bytes 262144 | tf_op jit(solution)/shard_map/all_to_all | solution.py:787
  88.4 20.2 %collective-permute-start.7 = (f32[3,64,128]{2,1,0:T(8,128)S(1)}, f32[3,64,128]{2,1,0:T(8,128)S(1)}, u32[]{:S(2)}, u32[]{:S(2)}) collective-permute-start(f32[3,64,128]{2,1,0:T(8,128)S(1)} %get-tuple-element.32), channel_id=1, source_target_pairs={{8,0},{16,8},{24,16},{32,24},{40,32},{48,40},{56,48},{64,56},{72,6... | collective-permute-start | bytes 294920 | tf_op jit(solution)/shard_map/ppermute | solution.py:773
  89.7 19.0 %collective-permute-start.6 = (f32[3,64,128]{2,1,0:T(8,128)S(1)}, f32[3,64,128]{2,1,0:T(8,128)S(1)}, u32[]{:S(2)}, u32[]{:S(2)}) collective-permute-start(f32[3,64,128]{2,1,0:T(8,128)S(1)} %get-tuple-element.32), channel_id=1, source_target_pairs={{0,8},{8,16},{16,24},{24,32},{32,40},{40,48},{48,56},{56,64},{64,7... | collective-permute-start | bytes 294920 | tf_op jit(solution)/shard_map/ppermute | solution.py:773
  105.1 10.4 %all-to-all-start.3 = ((f32[8,8,256]{2,1,0:T(8,128)}), f32[8,8,256]{2,1,0:T(8,128)S(1)}, u32[]{:S(2)}, u32[]{:S(2)}) async-start(f32[8,8,256]{2,1,0:T(8,128)} %broadcast_in_dim.51), calls=%async_computation.3 | async-start | bytes 131072 | tf_op jit(solution)/shard_map/all_to_all | solution.py:789

commit v6 on v5

--- a/solution.py
+++ b/solution.py
@@ -387,18 +387,27 @@
     return first, second, rest - second
 
 
-def cell_parts(own_ref, table, weights_ref, shift_ref):
+def cell_parts(wide_ref, table, weights_ref, shift_ref):
+    def own(columns):
+        return wide_ref[8:16, columns]
+
+    def beside(columns):
+        return jnp.concatenate([wide_ref[6:8, columns], jnp.zeros((4, 128), F32), wide_ref[16:18, columns]], axis=0)
+
     pieces = []
-    for pair in range(4):
-        start = 128 * pair if pair < 2 else 128 * pair + 128
-        values = own_ref[:, start : start + 128]
-        pieces += [values, roll(values, 64, 1)]
-    b = jnp.concatenate(pieces + [jnp.zeros((64, 128), F32)], axis=0).T[0:64]
-    turned = jnp.concatenate([own_ref[:, 256:384], jnp.zeros((120, 128), F32)], axis=0).T
+    for rows in (own, beside):
+        for pair in range(4):
+            start = 128 * pair if pair < 2 else 128 * pair + 128
+            values = rows(slice(start, start + 128))
+            pieces += [values, roll(values, 64, 1)]
+    b = jnp.concatenate(pieces, axis=0).T[0:64]
+    middle = slice(256, 384)
+    turned = jnp.concatenate([own(middle), beside(middle), jnp.zeros((112, 128), F32)], axis=0).T
     lane = iota((1, 128), 1)
     marks = jnp.zeros((1, 128), F32)
     for z in range(8):
         marks = jnp.where((lane >> 3) == z, roll(turned[z : z + 1], 8 * z, 1), marks)
+        marks = jnp.where((lane >> 3) == 8 + z, roll(turned[z : z + 1], 8 * z + 56, 1), marks)
     marks = marks.astype(jnp.int32)
     both = coefficients([marks], table)
     x0 = (RELAX / both[:64]) * b
@@ -418,7 +427,8 @@
     z_low = wz * along(jnp.where((sub & 3) == 0, every, 0.0))
     z_high = wz * along(jnp.where((sub & 3) == 3, every, 0.0))
     x, yi, z = (lane >> 1) & 3, lane & 1, lane >> 3
-    local = local + jnp.where(x > 0, roll(x_high, 2, 1), 0.0) + jnp.where(x < 3, roll(x_low, -2, 1), 0.0)
+    local = local + jnp.where(x > 0, roll(x_high, 2, 1), roll(x_high, -64, 1))
+    local = local + jnp.where(x < 3, roll(x_low, -2, 1), roll(x_low, -64, 1))
     local = local + jnp.where(yi == 1, roll(y_high, 1, 1), roll(y_low, -1, 1))
     local = local + jnp.where(z > 0, roll(z_high, 8, 1), 0.0) + jnp.where(z < 7, roll(z_low, -8, 1), 0.0)
     shifts = jnp.zeros((1, 128), F32)
@@ -431,18 +441,14 @@
             scale * jnp.where(yi == 1, y_high, 0.0),
             scale * jnp.where(yi == 0, y_low, 0.0),
             0.125 * shifts,
-            scale * jnp.where(x == 3, x_high, jnp.where(x == 0, x_low, 0.0)),
             scale * jnp.where(z == 7, z_high, jnp.where(z == 0, z_low, 0.0)),
-            jnp.zeros((2, 128), F32),
+            jnp.zeros((3, 128), F32),
         ],
         axis=0,
     )
 
 
-def front_kernel(
-    place_ref, weights_ref, shift_ref, right_ref, marks_ref, blocks_ref,
-    own_ref, table_ref, payload_ref,
-):
+def own_kernel(right_ref, marks_ref, own_ref):
     own_ref[:, 256:384] = jnp.zeros((8, 128), F32)
     for x in range(4):
         rows = slice(2 * x, 2 * x + 2)
@@ -450,17 +456,10 @@
         own_ref[rows, 0:256] = values[:, 0:256]
         own_ref[rows, 384:640] = values[:, 256:512]
         own_ref[rows, 256:264] = marks_ref[x].astype(F32)
-    diagonal = jnp.where(iota((64, 64), 0) == iota((64, 64), 1), 1.0, 0.0)
-    rows = []
-    for k in range(CLASSES):
-        block = blocks_ref[k]
-        diag = jnp.sum(block * diagonal, axis=0, keepdims=True)
-        rows.append(jnp.concatenate([diag, jnp.sum(block, axis=0, keepdims=True)], axis=1))
-    parts = split(jnp.concatenate(rows, axis=0))
-    table = jnp.concatenate(list(parts) + [jnp.zeros((80, 128), F32)], axis=0).T
-    table_ref[...] = table[:, 0:48].astype(jnp.bfloat16)
-
-    parts = cell_parts(own_ref, table_ref, weights_ref, shift_ref)
+
+
+def front_kernel(place_ref, weights_ref, shift_ref, wide_ref, table_ref, payload_ref):
+    parts = cell_parts(wide_ref, table_ref, weights_ref, shift_ref)
     shape = (128, 128)
     source, target = iota(shape, 0), iota(shape, 1)
     hit = (source < 64) & (((source >> 2) & 1) == (target >> 6)) & ((source >> 4) == ((target >> 4) & 3))
@@ -471,30 +470,27 @@
     row = jnp.where(own, cells[0:1], jnp.where(gy == gy0 + 1, cells[1:2], 0.0))
     payload_ref[:, 0:128] = row + jnp.where(gy == gy0 - 1, cells[2:3], 0.0)
     payload_ref[:, 128:256] = jnp.where(own, cells[3:4], 0.0)
-    payload_ref[:, 256:384] = jnp.where(own, roll(cells[4:5], 64, 1), 0.0)
-    high = jnp.where(own & (b == 3), roll(cells[5:6], 48, 1), 0.0)
-    payload_ref[:, 384:512] = jnp.where(own & (b == 0), roll(cells[5:6], -48, 1), high)
+    high = jnp.where(own & (b == 3), roll(cells[4:5], 48, 1), 0.0)
+    payload_ref[:, 256:384] = jnp.where(own & (b == 0), roll(cells[4:5], -48, 1), high)
 
 
 def join_parts(gathered_ref):
     lane, sub = iota((8, 128), 1), iota((8, 128), 0)
-    a, b = lane >> 6, (lane >> 4) & 3
+    b = (lane >> 4) & 3
     result = []
     for gx in range(8):
         value = gathered_ref[gx, :, 0:128]
-        if gx > 0:
-            value = value + jnp.where(a == 0, gathered_ref[gx - 1, :, 256:384], 0.0)
-        if gx < 7:
-            value = value + jnp.where(a == 1, gathered_ref[gx + 1, :, 256:384], 0.0)
-        z = gathered_ref[gx, :, 384:512]
+        z = gathered_ref[gx, :, 256:384]
         value = value + jnp.where((b == 0) & (sub > 0), roll(z, 1, 0), 0.0)
         value = value + jnp.where((b == 3) & (sub < 7), roll(z, -1, 0), 0.0)
         result.append(value)
     return result
 
 
-def pack_kernel(blocks_ref, packed_ref):
+def pack_kernel(blocks_ref, packed_ref, table_ref):
+    diagonal = jnp.where(iota((64, 64), 0) == iota((64, 64), 1), 1.0, 0.0)
     low = iota((64, 128), 1) < 64
+    rows = []
     for k in range(CLASSES):
         block = blocks_ref[k]
         first, second, third = split(jnp.concatenate([block, block], axis=1))
@@ -502,6 +498,11 @@
         packed_ref[at, 0:128] = first.astype(jnp.bfloat16)
         packed_ref[at, 128:256] = jnp.where(low, first, second).astype(jnp.bfloat16)
         packed_ref[at, 256:384] = jnp.where(low, second, third).astype(jnp.bfloat16)
+        diag = jnp.sum(block * diagonal, axis=0, keepdims=True)
+        rows.append(jnp.concatenate([diag, jnp.sum(block, axis=0, keepdims=True)], axis=1))
+    parts = split(jnp.concatenate(rows, axis=0))
+    table = jnp.concatenate(list(parts) + [jnp.zeros((80, 128), F32)], axis=0).T
+    table_ref[...] = table[:, 0:48].astype(jnp.bfloat16)
 
 
 def coefficient_kernel(place_ref, below_ref, here_ref, above_ref, table_ref, class_ref, inverse_ref, sums_ref):
@@ -582,17 +583,18 @@
         return jnp.where(lane < 64, roll(smooth_ref[2 + j], -28, 1), roll(smooth_ref[8 + j], 36, 1))
 
     blocks = [block(j) for j in range(-1, 7)]
-    for j in (0, 2, 4):
-        marks = [class_ref[j + i : j + i + 1, :] for i in (0, 1)]
-        chosen = dense(jnp.concatenate([blocks[j + 1], blocks[j + 2]], axis=1), marks, packed_ref)
-        for part in range(2):
-            at = j + part
-            view = Pack(smooth_ref[2 + at], smooth_ref[8 + at])
-            faces = coupling(groups(blocks[at]), view, groups(blocks[at + 2]), weights_ref)
-            for g in range(8):
-                image_ref[at, 8 * g : 8 * g + 8] = chosen[part][g] - faces[g]
     own = (lane & 63) >= 20
     own = own & ((lane & 63) < 44)
+    halves = [jnp.where(own, blocks[j + 1], roll(blocks[j + 4], 32, 1)) for j in range(3)]
+    marks = class_ref[...]
+    marks = jnp.where(own[0:8], marks, roll(jnp.concatenate([marks[3:8], marks[0:3]], axis=0), 32, 1))
+    chosen = dense(jnp.concatenate(halves, axis=1), [marks[j : j + 1] for j in range(3)], packed_ref)
+    for j in range(6):
+        view = Pack(smooth_ref[2 + j], smooth_ref[8 + j])
+        faces = coupling(groups(blocks[j]), view, groups(blocks[j + 2]), weights_ref)
+        for g in range(8):
+            value = chosen[j][g] if j < 3 else roll(chosen[j - 3][g], -32, 1)
+            image_ref[j, 8 * g : 8 * g + 8] = value - faces[g]
     for j in range(3):
         edge_ref[j] = jnp.where(own, image_ref[j], roll(image_ref[j + 3], 32, 1))
     restrict(image_ref, near_inverse_ref, sums_ref, weights_ref, all_ref, cells_ref)
@@ -737,11 +739,11 @@
 
 
 def front_call(*args):
-    return call(front_kernel, 3, [((8, 640), F32), ((128, 48), jnp.bfloat16), ((1, 512), F32)], [], *args)
+    return call(front_kernel, 3, [((1, 384), F32)], [], *args)[0]
 
 
 def pack_call(blocks):
-    return call(pack_kernel, 0, [((CLASSES * NODES, 384), jnp.bfloat16)], [], blocks)[0]
+    return call(pack_kernel, 0, [((CLASSES * NODES, 384), jnp.bfloat16), ((128, 48), jnp.bfloat16)], [], blocks)
 
 
 def coefficient_call(*args):
@@ -773,8 +775,7 @@
     return lax.ppermute(x, axis, pairs)
 
 
-def extend_xz(own):
-    wide = jnp.concatenate([shifted(own, "gx", 1), own, shifted(own, "gx", -1)], axis=0)
+def extend_z(wide):
     low = shifted(wide[:, 256:640], "gz", 1)
     high = shifted(wide[:, 0:384], "gz", -1)
     nothing = jnp.zeros((24, 112), F32)
@@ -797,10 +798,12 @@
 
 def per_device(right_side, element_class, class_blocks, class_shift, face_weights):
     place = jnp.stack([lax.axis_index(axis) for axis in AXES]).astype(jnp.int32)
-    own, table, row = front_call(place, face_weights, class_shift, right_side, element_class, class_blocks)
+    own = call(own_kernel, 0, [((8, 640), F32)], [], right_side, element_class)[0]
+    wide = jnp.concatenate([shifted(own, "gx", 1), own, shifted(own, "gx", -1)], axis=0)
+    packed, table = pack_call(class_blocks)
+    row = front_call(place, face_weights, class_shift, wide, table)
     gathered = gather_cells(row)
-    packed = pack_call(class_blocks)
-    here = extend_xz(own)
+    here = extend_z(wide)
     below, above = shifted(here, "gy", 1), shifted(here, "gy", -1)
     marks, near_inverse, sums = coefficient_call(place, below, here, above, table)
     local, inverse, keep = local_call(place, face_weights, below, here, above, table, packed)

time: 152 us -> 155 us (1.020)
  waiting for transfers between devices: 24.8 us -> 29.3 us
  starting transfers between devices: 74.6 us -> 70.4 us
  local copies, waits for them, and re-layouts: 4.75 us -> 7.46 us
    all_to_all x2, waiting for transfers between devices: 10.8 us -> 15.4 us  [gather_cells(): lax.all_to_all(jnp.broadcast_to(row[None], (128, 1, width)), ('gy', 'gz')...]
    all_to_all x2, starting transfers between devices: 42.4 us -> 40.3 us  [gather_cells(): lax.all_to_all(jnp.broadcast_to(row[None], (128, 1, width)), ('gy', 'gz')...]
    unnamed x14, local copies, waits for them, and re-layouts: 1.66 us -> 3.73 us
    ppermute x8, starting transfers between devices: 21.6 us -> 19.7 us  [shifted(): return lax.ppermute(x, axis, pairs)]
    pallas_call x8 -> x9, Pallas kernels: 14.2 us -> 14 us  [call(): pl.pallas_call(body, out_shape=shapes, in_specs=specs, out_specs=[VMEM] *...]
  transfers between devices with their start and end apart: 12 -> 12, of which waited for: 5 -> 6; matrix products, arithmetic and copies ran while one was open for 1% -> 1% of each run, Pallas kernels for 4% -> 4%
where the time goes in v6:
time: 155 us; the launch traced here: 154 us
  starting transfers between devices  70.4 us (45%)
  blocking collectives  31.7 us (20%)
  waiting for transfers between devices  29.3 us (19%)
  Pallas kernels  14 us (9%)
  local copies, waits for them, and re-layouts  7.46 us (5%)
    all_to_all x2, starting transfers between devices, gather_cells(): lax.all_to_all(jnp.broadcast_to(row[None], (128, 1, width)), ('gy', 'gz')...  40.3 us
    all_to_all x1, blocking collectives, gather_sum(): lax.all_to_all(jnp.broadcast_to(row[None], (128, 1, 128)), ('gy', 'gz'),...  22.8 us
    ppermute x8, starting transfers between devices, shifted(): return lax.ppermute(x, axis, pairs)  19.7 us
    all_to_all x2, waiting for transfers between devices, gather_cells(): lax.all_to_all(jnp.broadcast_to(row[None], (128, 1, width)), ('gy', 'gz')...  15.4 us
    pallas_call x9, Pallas kernels, call(): pl.pallas_call(body, out_shape=shapes, in_specs=specs, out_specs=[VMEM] *...  14 us
    all_to_all x2, starting transfers between devices, gather_cells(): lax.all_to_all(jnp.broadcast_to(plane[None], (8, 8, width)), 'gx', 0, 0,...  10.4 us
    all_to_all x2, waiting for transfers between devices, gather_cells(): lax.all_to_all(jnp.broadcast_to(plane[None], (8, 8, width)), 'gx', 0, 0,...  9.11 us
    all_to_all x1, blocking collectives, gather_sum(): lax.all_to_all(jnp.broadcast_to(part[None, None], (8, 1, 128)), 'gx', 0,...  8.89 us
  transfers between devices with their start and end apart: 12, of which 6 were waited for; matrix products, arithmetic and copies ran while one was open for 1% of the time, Pallas kernels for 4%

profile of v6, /device:TPU:1, one launch (start us, length us, event | category | flops | bytes accessed | tf_op | source)
XLA Modules:
  0.0 153.9 jit_solution(6931769146243012418)
XLA Ops:
  0.6 0.7 copy-done.2
  1.4 0.7 copy-done.4
  2.0 4.0 %collective-permute-start = (f32[8,640]{1,0:T(8,128)S(1)}, f32[8,640]{1,0:T(8,128)S(1)}, u32[]{:S(2)}, u32[]{:S(2)}) collective-permute-start(f32[8,640]{1,0:T(8,128)S(1)} %shard_map.68.right_ref), channel_id=1, source_target_pairs={{0,128},{128,256},{256,384},{384,512},{512,640},{640,768},{768,896... | collective-permute-start | bytes 61448 | tf_op jit(solution)/shard_map/ppermute | solution.py:775
  6.1 1.3 collective-permute-start.1
  7.4 0.1 pad_add_fusion.place_ref
  7.5 1.0 copy-done.1
  8.5 0.3 shard_map.69
  8.9 0.0 collective-permute-done
  8.9 1.8 %collective-permute-done.1 = f32[8,640]{1,0:T(8,128)S(1)} collective-permute-done((f32[8,640]{1,0:T(8,128)S(1)}, f32[8,640]{1,0:T(8,128)S(1)}, u32[]{:S(2)}, u32[]{:S(2)}) %collective-permute-start.1) | collective-permute-done | bytes 20512 | tf_op jit(solution)/shard_map/ppermute | solution.py:775
  10.6 0.0 copy-start.3
  10.6 0.0 copy-start.5
  10.6 0.7 copy-done.3
  11.3 0.0 copy-done.5
  11.3 1.1 shard_map.70
  12.5 0.8 broadcast_in_dim.21
  13.3 24.7 %all-to-all-start = ((f32[128,1,384]{2,1,0:T(1,128)}), f32[128,1,384]{2,1,0:T(1,128)S(1)}, u32[]{:S(2)}, u32[]{:S(2)}) async-start(f32[128,1,384]{2,1,0:T(1,128)} %broadcast_in_dim.21), calls=%async_computation | async-start | bytes 393216 | tf_op jit(solution)/shard_map/all_to_all | solution.py:788
  38.0 3.5 %collective-permute-start.2 = (f32[24,384]{1,0:T(8,128)S(1)}, f32[24,384]{1,0:T(8,128)S(1)}, u32[]{:S(2)}, u32[]{:S(2)}) collective-permute-start(f32[24,384]{1,0:T(8,128)S(1)} %get-tuple-element.41), channel_id=1, source_target_pairs={{0,1},{1,2},{2,3},{3,4},{4,5},{5,6},{6,7},{8,9},{9,10},{10,11},{11... | collective-permute-start | bytes 110600 | tf_op jit(solution)/shard_map/ppermute | solution.py:775
  41.5 1.9 %collective-permute-start.3 = (f32[24,384]{1,0:T(8,128)S(1)}, f32[24,384]{1,0:T(8,128)S(1)}, u32[]{:S(2)}, u32[]{:S(2)}) collective-permute-start(f32[24,384]{1,0:T(8,128)S(1)} %get-tuple-element.40), channel_id=1, source_target_pairs={{1,0},{2,1},{3,2},{4,3},{5,4},{6,5},{7,6},{9,8},{10,9},{11,10},{12... | collective-permute-start | bytes 110600 | tf_op jit(solution)/shard_map/ppermute | solution.py:775
  43.5 0.0 collective-permute-done.2
  43.5 0.6 copy-done.6
  44.1 0.1 slice.37
  44.2 3.0 %collective-permute-done.3 = f32[24,384]{1,0:T(8,128)S(1)} collective-permute-done((f32[24,384]{1,0:T(8,128)S(1)}, f32[24,384]{1,0:T(8,128)S(1)}, u32[]{:S(2)}, u32[]{:S(2)}) %collective-permute-start.3) | collective-permute-done | bytes 36896 | tf_op jit(solution)/shard_map/ppermute | solution.py:775
  47.2 0.7 slice-done.1
  47.9 0.1 concatenate.7.here_ref
  48.0 3.0 %collective-permute-start.4 = (f32[24,1152]{1,0:T(8,128)S(1)}, f32[24,1152]{1,0:T(8,128)S(1)}, u32[]{:S(2)}, u32[]{:S(2)}) collective-permute-start(f32[24,1152]{1,0:T(8,128)S(1)} %concatenate.7.here_ref), channel_id=1, source_target_pairs={{0,8},{8,16},{16,24},{24,32},{32,40},{40,48},{48,56},{56,64},{64,7... | collective-permute-start | bytes 331784 | tf_op jit(solution)/shard_map/ppermute | solution.py:775
  51.0 1.3 collective-permute-start.5
  52.3 3.7 %all-to-all-done = f32[128,1,384]{2,1,0:T(1,128)S(1)} async-done(((f32[128,1,384]{2,1,0:T(1,128)}), f32[128,1,384]{2,1,0:T(1,128)S(1)}, u32[]{:S(2)}, u32[]{:S(2)}) %all-to-all-start) | async-done | bytes 196640 | tf_op jit(solution)/shard_map/all_to_all | solution.py:788
  56.0 0.7 broadcast_in_dim.22
  56.6 7.0 %all-to-all-start.1 = ((f32[8,8,384]{2,1,0:T(8,128)}), f32[8,8,384]{2,1,0:T(8,128)S(1)}, u32[]{:S(2)}, u32[]{:S(2)}) async-start(f32[8,8,384]{2,1,0:T(8,128)} %broadcast_in_dim.22), calls=%async_computation.1 | async-start | bytes 196608 | tf_op jit(solution)/shard_map/all_to_all | solution.py:790
  63.7 0.0 collective-permute-done.4.below_ref
  63.7 0.8 shard_map.72
  64.5 2.9 %shard_map.71 = (f32[16,64,128]{2,1,0:T(8,128)S(1)}, f32[16,64,128]{2,1,0:T(8,128)S(1)}, f32[16,64,128]{2,1,0:T(8,128)S(1)}) custom-call(s32[3]{0:T(128)S(1)} %pad_add_fusion.place_ref, f32[3]{0:T(128)S(1)} %copy-done.3, f32[24,1152]{1,0:T(8,128)S(1)} %collective-permute-done.4.below_ref, f32[24,1152]{1,0:T(8,128)S(1)} %concatenate.7.here_ref, ...), custom_call_target="tpu_custom_call" | custom-call | flops 1409286144 | bytes 1000000 | tf_op jit(solution)/shard_map/pallas_call | solution.py:718
  67.4 3.7 %all-to-all-done.1.gathered_ref.shifts_ref = f32[8,8,384]{2,1,0:T(8,128)S(1)} async-done(((f32[8,8,384]{2,1,0:T(8,128)}), f32[8,8,384]{2,1,0:T(8,128)S(1)}, u32[]{:S(2)}, u32[]{:S(2)}) %all-to-all-start.1) | async-done | bytes 98336 | tf_op jit(solution)/shard_map/all_to_all | solution.py:790
  71.1 3.4 %shard_map.73 = (f32[6,64,128]{2,1,0:T(8,128)S(1)}, f32[3,64,128]{2,1,0:T(8,128)S(1)}, f32[8,512]{1,0:T(8,128)S(1)}, f32[8,512]{1,0:T(8,128)S(1)}, f32[1,256]{1,0:T(1,128)S(1)}) custom-call(s32[3]{0:T(128)S(1)} %pad_add_fusion.place_ref, f32[3]{0:T(128)S(1)} %copy-done.3, f32[8,8,384]{2,1,0:T(8,128)S(1)} %all-to-all-done.1.gathered_ref.shifts_ref, ...), custom_call_target="tpu_custom_call" | custom-call | flops 603979776 | bytes 1000000 | tf_op jit(solution)/shard_map/pallas_call | solution.py:718
  74.5 0.7 broadcast_in_dim.50
  75.3 15.7 %all-to-all-start.2 = ((f32[128,1,256]{2,1,0:T(1,128)}), f32[128,1,256]{2,1,0:T(1,128)S(1)}, u32[]{:S(2)}, u32[]{:S(2)}) async-start(f32[128,1,256]{2,1,0:T(1,128)} %broadcast_in_dim.50), calls=%async_computation.2 | async-start | bytes 262144 | tf_op jit(solution)/shard_map/all_to_all | solution.py:788
  90.9 3.3 %collective-permute-start.6 = (f32[3,64,128]{2,1,0:T(8,128)S(1)}, f32[3,64,128]{2,1,0:T(8,128)S(1)}, u32[]{:S(2)}, u32[]{:S(2)}) collective-permute-start(f32[3,64,128]{2,1,0:T(8,128)S(1)} %get-tuple-element.30), channel_id=1, source_target_pairs={{0,8},{8,16},{16,24},{24,32},{32,40},{40,48},{48,56},{56,64},{64,7... | collective-permute-start | bytes 294920 | tf_op jit(solution)/shard_map/ppermute | solution.py:775
  94.2 1.3 collective-permute-start.7
  95.5 11.8 %all-to-all-done.2 = f32[128,1,256]{2,1,0:T(1,128)S(1)} async-done(((f32[128,1,256]{2,1,0:T(1,128)}), f32[128,1,256]{2,1,0:T(1,128)S(1)}, u32[]{:S(2)}, u32[]{:S(2)}) %all-to-all-start.2) | async-done | bytes 131104 | tf_op jit(solution)/shard_map/all_to_all | solution.py:788
  107.3 0.6 broadcast_in_dim.51
  107.9 3.3 %all-to-all-start.3 = ((f32[8,8,256]{2,1,0:T(8,128)}), f32[8,8,256]{2,1,0:T(8,128)S(1)}, u32[]{:S(2)}, u32[]{:S(2)}) async-start(f32[8,8,256]{2,1,0:T(8,128)} %broadcast_in_dim.51), calls=%async_computation.3 | async-start | bytes 131072 | tf_op jit(solution)/shard_map/all_to_all | solution.py:790
  111.3 0.0 collective-permute-done.6.below_ref
  111.3 1.6 %shard_map.74.local_ref = f32[6,64,128]{2,1,0:T(8,128)S(1)} custom-call(f32[3]{0:T(128)S(1)} %copy-done.3, f32[6,64,128]{2,1,0:T(8,128)S(1)} %get-tuple-element.29.own_ref, f32[3,64,128]{2,1,0:T(8,128)S(1)} %collective-permute-done.6.below_ref, f32[3,64,128]{2,1,0:T(8,128)S(1)} %collective-permute-done.7.above_ref, ...), custom_call_target="tpu_custom_call" | custom-call | flops 603979776 | bytes 1000000 | tf_op jit(solution)/shard_map/pallas_call | solution.py:718
  112.9 5.4 %all-to-all-done.3.gathered_ref = f32[8,8,256]{2,1,0:T(8,128)S(1)} async-done(((f32[8,8,256]{2,1,0:T(8,128)}), f32[8,8,256]{2,1,0:T(8,128)S(1)}, u32[]{:S(2)}, u32[]{:S(2)}) %all-to-all-start.3) | async-done | bytes 65568 | tf_op jit(solution)/shard_map/all_to_all | solution.py:790
  118.4 2.8 %shard_map.75 = (f32[8,512]{1,0:T(8,128)S(1)}, f32[8,512]{1,0:T(8,128)S(1)}, f32[8,512]{1,0:T(8,128)S(1)}, f32[1,128]{1,0:T(1,128)S(1)}, f32[1,128]{1,0:T(1,128)S(1)}) custom-call(s32[3]{0:T(128)S(1)} %pad_add_fusion.place_ref, f32[3]{0:T(128)S(1)} %copy-done.3, f32[8,8,256]{2,1,0:T(8,128)S(1)} %all-to-all-done.3.gathered_ref, ...), custom_call_target="tpu_custom_call" | custom-call | flops 201326592 | bytes 1000000 | tf_op jit(solution)/shard_map/pallas_call | solution.py:718
  121.2 22.8 %all_to_all.30 = f32[128,1,128]{2,1,0:T(1,128)S(1)} all-to-all(f32[128,1,128]{2,1,0:T(1,128)S(1)} %broadcast_in_dim.53), channel_id=1, replica_groups=mesh['gx'=8,'gy'=16,'gz'=8] {'gy','gz'}, dimensions={0} | all-to-all | bytes 131072 | tf_op jit(solution)/shard_map/all_to_all | solution.py:794
  144.0 8.9 %all_to_all.31.parts_ref = f32[8,1,128]{2,1,0:T(1,128)S(1)} all-to-all(f32[8,1,128]{2,1,0:T(1,128)S(1)} %broadcast_in_dim.54), channel_id=1, replica_groups=mesh['gx'=8,'gy'=16,'gz'=8] {'gx'}, dimensions={0} | all-to-all | bytes 8192 | tf_op jit(solution)/shard_map/all_to_all | solution.py:796
  152.9 1.0 shard_map.76
  (24 shorter events, 0.2 us)
Async XLA Ops:
  0.6 0.7 copy-start.2
  1.3 0.7 copy-start.4
  2.0 6.8 %collective-permute-start = (f32[8,640]{1,0:T(8,128)S(1)}, f32[8,640]{1,0:T(8,128)S(1)}, u32[]{:S(2)}, u32[]{:S(2)}) collective-permute-start(f32[8,640]{1,0:T(8,128)S(1)} %shard_map.68.right_ref), channel_id=1, source_target_pairs={{0,128},{128,256},{256,384},{384,512},{512,640},{640,768},{768,896... | collective-permute-start | bytes 61448 | tf_op jit(solution)/shard_map/ppermute | solution.py:775
  6.1 4.5 %collective-permute-start.1 = (f32[8,640]{1,0:T(8,128)S(1)}, f32[8,640]{1,0:T(8,128)S(1)}, u32[]{:S(2)}, u32[]{:S(2)}) collective-permute-start(f32[8,640]{1,0:T(8,128)S(1)} %shard_map.68.right_ref), channel_id=1, source_target_pairs={{128,0},{256,128},{384,256},{512,384},{640,512},{768,640},{896,768... | collective-permute-start | bytes 61448 | tf_op jit(solution)/shard_map/ppermute | solution.py:775
  7.5 1.0 copy-start.1
  10.6 32.8 %copy-start = (f32[24,640]{1,0:T(8,128)}, f32[24,640]{1,0:T(8,128)S(1)}, u32[]{:S(2)}) copy-start(f32[24,640]{1,0:T(8,128)S(1)} %pad_maximum_fusion.wide_ref) | copy-start | bytes 184324
  10.6 0.7 copy-start.3
  10.6 0.7 copy-start.5
  13.3 42.7 %all-to-all-start = ((f32[128,1,384]{2,1,0:T(1,128)}), f32[128,1,384]{2,1,0:T(1,128)S(1)}, u32[]{:S(2)}, u32[]{:S(2)}) async-start(f32[128,1,384]{2,1,0:T(1,128)} %broadcast_in_dim.21), calls=%async_computation | async-start | bytes 393216 | tf_op jit(solution)/shard_map/all_to_all | solution.py:788
  38.0 5.5 %collective-permute-start.2 = (f32[24,384]{1,0:T(8,128)S(1)}, f32[24,384]{1,0:T(8,128)S(1)}, u32[]{:S(2)}, u32[]{:S(2)}) collective-permute-start(f32[24,384]{1,0:T(8,128)S(1)} %get-tuple-element.41), channel_id=1, source_target_pairs={{0,1},{1,2},{2,3},{3,4},{4,5},{5,6},{6,7},{8,9},{9,10},{10,11},{11... | collective-permute-start | bytes 110600 | tf_op jit(solution)/shard_map/ppermute | solution.py:775
  41.5 5.7 %collective-permute-start.3 = (f32[24,384]{1,0:T(8,128)S(1)}, f32[24,384]{1,0:T(8,128)S(1)}, u32[]{:S(2)}, u32[]{:S(2)}) collective-permute-start(f32[24,384]{1,0:T(8,128)S(1)} %get-tuple-element.40), channel_id=1, source_target_pairs={{1,0},{2,1},{3,2},{4,3},{5,4},{6,5},{7,6},{9,8},{10,9},{11,10},{12... | collective-permute-start | bytes 110600 | tf_op jit(solution)/shard_map/ppermute | solution.py:775
  43.5 0.6 copy-start.6
  47.2 0.7 slice-start.1
  47.2 0.7 slice-start
  48.0 15.7 %collective-permute-start.4 = (f32[24,1152]{1,0:T(8,128)S(1)}, f32[24,1152]{1,0:T(8,128)S(1)}, u32[]{:S(2)}, u32[]{:S(2)}) collective-permute-start(f32[24,1152]{1,0:T(8,128)S(1)} %concatenate.7.here_ref), channel_id=1, source_target_pairs={{0,8},{8,16},{16,24},{24,32},{32,40},{40,48},{48,56},{56,64},{64,7... | collective-permute-start | bytes 331784 | tf_op jit(solution)/shard_map/ppermute | solution.py:775
  51.0 12.7 %collective-permute-start.5 = (f32[24,1152]{1,0:T(8,128)S(1)}, f32[24,1152]{1,0:T(8,128)S(1)}, u32[]{:S(2)}, u32[]{:S(2)}) collective-permute-start(f32[24,1152]{1,0:T(8,128)S(1)} %concatenate.7.here_ref), channel_id=1, source_target_pairs={{8,0},{16,8},{24,16},{32,24},{40,32},{48,40},{56,48},{64,56},{72,6... | collective-permute-start | bytes 331784 | tf_op jit(solution)/shard_map/ppermute | solution.py:775
  56.6 14.5 %all-to-all-start.1 = ((f32[8,8,384]{2,1,0:T(8,128)}), f32[8,8,384]{2,1,0:T(8,128)S(1)}, u32[]{:S(2)}, u32[]{:S(2)}) async-start(f32[8,8,384]{2,1,0:T(8,128)} %broadcast_in_dim.22), calls=%async_computation.1 | async-start | bytes 196608 | tf_op jit(solution)/shard_map/all_to_all | solution.py:790
  75.3 32.0 %all-to-all-start.2 = ((f32[128,1,256]{2,1,0:T(1,128)}), f32[128,1,256]{2,1,0:T(1,128)S(1)}, u32[]{:S(2)}, u32[]{:S(2)}) async-start(f32[128,1,256]{2,1,0:T(1,128)} %broadcast_in_dim.50), calls=%async_computation.2 | async-start | bytes 262144 | tf_op jit(solution)/shard_map/all_to_all | solution.py:788
  90.9 20.4 %collective-permute-start.6 = (f32[3,64,128]{2,1,0:T(8,128)S(1)}, f32[3,64,128]{2,1,0:T(8,128)S(1)}, u32[]{:S(2)}, u32[]{:S(2)}) collective-permute-start(f32[3,64,128]{2,1,0:T(8,128)S(1)} %get-tuple-element.30), channel_id=1, source_target_pairs={{0,8},{8,16},{16,24},{24,32},{32,40},{40,48},{48,56},{56,64},{64,7... | collective-permute-start | bytes 294920 | tf_op jit(solution)/shard_map/ppermute | solution.py:775
  94.2 17.1 %collective-permute-start.7 = (f32[3,64,128]{2,1,0:T(8,128)S(1)}, f32[3,64,128]{2,1,0:T(8,128)S(1)}, u32[]{:S(2)}, u32[]{:S(2)}) collective-permute-start(f32[3,64,128]{2,1,0:T(8,128)S(1)} %get-tuple-element.30), channel_id=1, source_target_pairs={{8,0},{16,8},{24,16},{32,24},{40,32},{48,40},{56,48},{64,56},{72,6... | collective-permute-start | bytes 294920 | tf_op jit(solution)/shard_map/ppermute | solution.py:775
  107.9 10.4 %all-to-all-start.3 = ((f32[8,8,256]{2,1,0:T(8,128)}), f32[8,8,256]{2,1,0:T(8,128)S(1)}, u32[]{:S(2)}, u32[]{:S(2)}) async-start(f32[8,8,256]{2,1,0:T(8,128)} %broadcast_in_dim.51), calls=%async_computation.3 | async-start | bytes 131072 | tf_op jit(solution)/shard_map/all_to_all | solution.py:790

commit v7 on v5

--- a/solution.py
+++ b/solution.py
@@ -467,13 +467,18 @@
     cells = dot(parts, jnp.where(hit, 1.0, 0.0))
     lane = iota((1, 128), 1)
     b, gy, gy0 = (lane >> 4) & 3, lane & 15, place_ref[1]
-    own = gy == gy0
-    row = jnp.where(own, cells[0:1], jnp.where(gy == gy0 + 1, cells[1:2], 0.0))
-    payload_ref[:, 0:128] = row + jnp.where(gy == gy0 - 1, cells[2:3], 0.0)
-    payload_ref[:, 128:256] = jnp.where(own, cells[3:4], 0.0)
-    payload_ref[:, 256:384] = jnp.where(own, roll(cells[4:5], 64, 1), 0.0)
-    high = jnp.where(own & (b == 3), roll(cells[5:6], 48, 1), 0.0)
-    payload_ref[:, 384:512] = jnp.where(own & (b == 0), roll(cells[5:6], -48, 1), high)
+    row = jnp.where(gy == gy0, cells[0:1], jnp.where(gy == gy0 + 1, cells[1:2], 0.0))
+    row = row + jnp.where(gy == gy0 - 1, cells[2:3], 0.0)
+    row = row + jnp.where(gy == ((gy0 + 8) & 15), cells[3:4], 0.0)
+    row = row + jnp.where(gy == ((gy0 + 4) & 15), roll(cells[4:5], 64, 1), 0.0)
+    far = gy == ((gy0 + 12) & 15)
+    row = row + jnp.where(far & (b == 0), roll(cells[5:6], -48, 1), 0.0)
+    payload_ref[...] = row + jnp.where(far & (b == 3), roll(cells[5:6], 48, 1), 0.0)
+
+
+def rotate(values, step):
+    gy = iota(values.shape, 1) & 15
+    return jnp.where(gy + step < 16, roll(values, -step, 1), roll(values, 16 - step, 1))
 
 
 def join_parts(gathered_ref):
@@ -483,10 +488,10 @@
     for gx in range(8):
         value = gathered_ref[gx, :, 0:128]
         if gx > 0:
-            value = value + jnp.where(a == 0, gathered_ref[gx - 1, :, 256:384], 0.0)
+            value = value + jnp.where(a == 0, rotate(gathered_ref[gx - 1, :, 256:384], 4), 0.0)
         if gx < 7:
-            value = value + jnp.where(a == 1, gathered_ref[gx + 1, :, 256:384], 0.0)
-        z = gathered_ref[gx, :, 384:512]
+            value = value + jnp.where(a == 1, rotate(gathered_ref[gx + 1, :, 256:384], 4), 0.0)
+        z = rotate(gathered_ref[gx, :, 384:512], 12)
         value = value + jnp.where((b == 0) & (sub > 0), roll(z, 1, 0), 0.0)
         value = value + jnp.where((b == 3) & (sub < 7), roll(z, -1, 0), 0.0)
         result.append(value)
@@ -565,7 +570,7 @@
     image_ref, edge_ref, own_direction_ref, own_image_ref, payload_ref,
     smooth_ref, pad_ref, rows_ref, shift_ref, all_ref, cells_ref,
 ):
-    coarse = coarse_cycle(join_parts(gathered_ref), [gathered_ref[g, :, 128:256] for g in range(8)])
+    coarse = coarse_cycle(join_parts(gathered_ref), [rotate(gathered_ref[g, :, 128:256], 8) for g in range(8)])
     place_correction(coarse, place_ref, pad_ref, rows_ref, shift_ref)
     _, _, yi = lane_places((8, 128))
     for s in range(1, 15):
@@ -596,13 +601,15 @@
     for j in range(3):
         edge_ref[j] = jnp.where(own, image_ref[j], roll(image_ref[j + 3], 32, 1))
     restrict(image_ref, near_inverse_ref, sums_ref, weights_ref, all_ref, cells_ref)
-    payload_ref[:, 0:128] = payload(cells_ref[...], place_ref, 1.0 / NODES)
+    row = payload(cells_ref[...], place_ref, 1.0 / NODES)
     own_z = gather_own([(smooth_ref[z + 4], 56) for z in range(8)])
     own_rows(own_z, own_of_packed(image_ref), own_direction_ref, own_image_ref)
     direction = own_direction_ref[...]
     lane = iota((1, 128), 1)
     gamma, delta = total(own_right(right_ref) * direction), total(direction * own_image_ref[...])
-    payload_ref[:, 128:256] = jnp.where(lane == 0, gamma, jnp.where(lane == 1, delta, 0.0))
+    far = (lane & 15) == ((place_ref[1] + 8) & 15)
+    row = row + jnp.where(far & ((lane >> 4) == 0), gamma, 0.0)
+    payload_ref[...] = row + jnp.where(far & ((lane >> 4) == 1), delta, 0.0)
 
 
 def near_kernel(
@@ -636,7 +643,7 @@
     smooth_ref, pad_ref, rows_ref, shift_ref, turned_ref, image_ref, near_ref,
 ):
     coarse = coarse_cycle(
-        [gathered_ref[g, :, 0:128] for g in range(8)], [shifts_ref[g, :, 128:256] for g in range(8)]
+        [gathered_ref[g, :, 0:128] for g in range(8)], [rotate(shifts_ref[g, :, 128:256], 8) for g in range(8)]
     )
     place_correction(coarse, place_ref, pad_ref, rows_ref, shift_ref)
     lane = iota((8, 128), 1)
@@ -673,8 +680,11 @@
     for g in range(1, 8):
         sums = sums + gathered_ref[g, :, 128:256]
     sums = jnp.sum(sums, axis=0, keepdims=True)
-    known_ref[...] = sums
-    step = sums[:, 0:1] / sums[:, 1:2]
+    slot = iota((1, 128), 1) >> 4
+    gamma, delta = total(jnp.where(slot == 0, sums, 0.0)), total(jnp.where(slot == 1, sums, 0.0))
+    lane = iota((1, 128), 1)
+    known_ref[...] = jnp.where(lane == 0, gamma, jnp.where(lane == 1, delta, 0.0))
+    step = gamma / delta
     own_rows(own_y, own_v, smoothed_ref, turned_ref)
     smoothed = own_direction_ref[...] - step * smoothed_ref[...]
     smoothed_ref[...] = smoothed
@@ -729,7 +739,7 @@
 MARKS = ((8, 128), jnp.int32)
 OWN = ((8, 512), F32)
 CELLS = ((8, 128), F32)
-ROW, WIDE = ((1, 128), F32), ((1, 256), F32)
+ROW = ((1, 128), F32)
 COARSE_SCRATCH = [((10, 24, 128), F32), ((16, 128), F32), ((16, 128), F32)]
 SUM_SCRATCH = [((6, 8, 128), F32), ((24, 128), F32)]
 EDGE = ((3, NODES, 128), F32)
@@ -737,7 +747,7 @@
 
 
 def front_call(*args):
-    return call(front_kernel, 3, [((8, 640), F32), ((128, 48), jnp.bfloat16), ((1, 512), F32)], [], *args)
+    return call(front_kernel, 3, [((8, 640), F32), ((128, 48), jnp.bfloat16), ROW], [], *args)
 
 
 def pack_call(blocks):
@@ -755,7 +765,7 @@
 
 def first_call(*args):
     scratch = [FIELD] + COARSE_SCRATCH + SUM_SCRATCH
-    return call(first_kernel, 2, [BLOCKS, EDGE, OWN, OWN, WIDE], scratch, *args, flops=3 * PAIR_FLOPS)
+    return call(first_kernel, 2, [BLOCKS, EDGE, OWN, OWN, ROW], scratch, *args, flops=3 * PAIR_FLOPS)
 
 
 def near_call(*args):
@@ -782,11 +792,15 @@
     return jnp.concatenate(pieces + [low[:, 128:384], wide[:, 0:256], wide[:, 384:640], high[:, 0:256]], axis=1)
 
 
-def gather_cells(row):
-    width = row.shape[1]
-    parts = lax.all_to_all(jnp.broadcast_to(row[None], (128, 1, width)), ("gy", "gz"), 0, 0, tiled=True)
-    plane = parts.reshape(16, 8, width).sum(axis=0)
-    return lax.all_to_all(jnp.broadcast_to(plane[None], (8, 8, width)), "gx", 0, 0, tiled=True)
+def gather_cells(row, *offsets):
+    parts = lax.all_to_all(jnp.broadcast_to(row[None], (128, 1, 128)), ("gy", "gz"), 0, 0, tiled=True)
+    parts = parts.reshape(16, 8, 128)
+    offset = (iota(parts.shape, 2) - iota(parts.shape, 0)) & 15
+    near = (offset == 0) | (offset == 1) | (offset == 15)
+    keeps = [near] + [offset == value for value in offsets]
+    plane = jnp.concatenate([jnp.where(keep, parts, 0.0).sum(axis=0) for keep in keeps], axis=1)
+    shape = (8,) + plane.shape
+    return lax.all_to_all(jnp.broadcast_to(plane[None], shape), "gx", 0, 0, tiled=True)
 
 
 def gather_sum(row):
@@ -798,7 +812,7 @@
 def per_device(right_side, element_class, class_blocks, class_shift, face_weights):
     place = jnp.stack([lax.axis_index(axis) for axis in AXES]).astype(jnp.int32)
     own, table, row = front_call(place, face_weights, class_shift, right_side, element_class, class_blocks)
-    gathered = gather_cells(row)
+    gathered = gather_cells(row, 8, 4, 12)
     packed = pack_call(class_blocks)
     here = extend_xz(own)
     below, above = shifted(here, "gy", 1), shifted(here, "gy", -1)
@@ -807,7 +821,7 @@
     image, edge, direction, own_image, row = first_call(
         place, face_weights, gathered, local, inverse, keep, marks, near_inverse, sums, packed, own
     )
-    again = gather_cells(row)
+    again = gather_cells(row, 8)
     from_below, from_above = shifted(edge, "gy", 1), shifted(edge, "gy", -1)
     near = near_call(face_weights, image, from_below, from_above, marks, near_inverse, packed)
     residual, smoothed, applied, known, row = second_call(

time: 152 us -> 152 us (level)
    ppermute x8, starting transfers between devices: 21.6 us -> 19.9 us  [shifted(): return lax.ppermute(x, axis, pairs)]
where the time goes in v7:
time: 152 us; the launch traced here: 151 us
  starting transfers between devices  74.3 us (49%)
  blocking collectives  33.1 us (22%)
  waiting for transfers between devices  23.9 us (16%)
  Pallas kernels  14.3 us (9%)
  local copies, waits for them, and re-layouts  4.51 us (3%)
    all_to_all x2, starting transfers between devices, gather_cells(): lax.all_to_all(jnp.broadcast_to(row[None], (128, 1, 128)), ('gy', 'gz'),...  41.8 us
    all_to_all x1, blocking collectives, gather_sum(): lax.all_to_all(jnp.broadcast_to(row[None], (128, 1, 128)), ('gy', 'gz'),...  24.2 us
    ppermute x8, starting transfers between devices, shifted(): return lax.ppermute(x, axis, pairs)  19.9 us
    pallas_call x8, Pallas kernels, call(): pl.pallas_call(body, out_shape=shapes, in_specs=specs, out_specs=[VMEM] *...  14.3 us
    all_to_all x2, starting transfers between devices, gather_cells(): lax.all_to_all(jnp.broadcast_to(plane[None], shape), 'gx', 0, 0, tiled=True)  12.6 us
    all_to_all x2, waiting for transfers between devices, gather_cells(): lax.all_to_all(jnp.broadcast_to(row[None], (128, 1, 128)), ('gy', 'gz'),...  11.3 us
    all_to_all x2, waiting for transfers between devices, gather_cells(): lax.all_to_all(jnp.broadcast_to(plane[None], shape), 'gx', 0, 0, tiled=True)  9.07 us
    all_to_all x1, blocking collectives, gather_sum(): lax.all_to_all(jnp.broadcast_to(part[None, None], (8, 1, 128)), 'gx', 0,...  8.89 us
  transfers between devices with their start and end apart: 12, of which 5 were waited for; matrix products, arithmetic and copies ran while one was open for 1% of the time, Pallas kernels for 4%

profile of v7, /device:TPU:1, one launch (start us, length us, event | category | flops | bytes accessed | tf_op | source)
XLA Modules:
  0.0 151.3 jit_solution(2251279590977186474)
XLA Ops:
  0.6 0.0 copy-start.2
  0.6 0.0 copy-start.4
  0.7 0.0 copy-start.3
  0.7 0.1 pad_add_fusion.place_ref
  0.8 0.6 copy-done.2
  1.4 0.0 copy-done.3
  1.4 1.0 copy-done
  2.4 1.2 shard_map.68
  3.6 4.0 %collective-permute-start = (f32[8,640]{1,0:T(8,128)S(1)}, f32[8,640]{1,0:T(8,128)S(1)}, u32[]{:S(2)}, u32[]{:S(2)}) collective-permute-start(f32[8,640]{1,0:T(8,128)S(1)} %get-tuple-element.22.right_ref), channel_id=1, source_target_pairs={{0,128},{128,256},{256,384},{384,512},{512,640},{640,768},{768,896... | collective-permute-start | bytes 61448 | tf_op jit(solution)/shard_map/ppermute | solution.py:783
  7.7 1.3 collective-permute-start.1
  9.0 0.7 broadcast_in_dim.55
  9.7 23.5 %all-to-all-start = ((f32[128,1,128]{2,1,0:T(1,128)}), f32[128,1,128]{2,1,0:T(1,128)S(1)}, u32[]{:S(2)}, u32[]{:S(2)}) async-start(f32[128,1,128]{2,1,0:T(1,128)} %broadcast_in_dim.55), calls=%async_computation | async-start | bytes 131072 | tf_op jit(solution)/shard_map/all_to_all | solution.py:796
  33.2 0.0 collective-permute-done
  33.2 0.0 collective-permute-done.1
  33.3 3.5 %collective-permute-start.2 = (f32[24,384]{1,0:T(8,128)S(1)}, f32[24,384]{1,0:T(8,128)S(1)}, u32[]{:S(2)}, u32[]{:S(2)}) collective-permute-start(f32[24,384]{1,0:T(8,128)S(1)} %get-tuple-element.49), channel_id=1, source_target_pairs={{0,1},{1,2},{2,3},{3,4},{4,5},{5,6},{6,7},{8,9},{9,10},{10,11},{11... | collective-permute-start | bytes 110600 | tf_op jit(solution)/shard_map/ppermute | solution.py:783
  36.8 0.0 copy-start.1
  36.8 2.1 %collective-permute-start.3 = (f32[24,384]{1,0:T(8,128)S(1)}, f32[24,384]{1,0:T(8,128)S(1)}, u32[]{:S(2)}, u32[]{:S(2)}) collective-permute-start(f32[24,384]{1,0:T(8,128)S(1)} %get-tuple-element.48), channel_id=1, source_target_pairs={{1,0},{2,1},{3,2},{4,3},{5,4},{6,5},{7,6},{9,8},{10,9},{11,10},{12... | collective-permute-start | bytes 110600 | tf_op jit(solution)/shard_map/ppermute | solution.py:783
  38.9 0.0 collective-permute-done.2
  38.9 0.1 slice.37
  39.0 3.5 %collective-permute-done.3 = f32[24,384]{1,0:T(8,128)S(1)} collective-permute-done((f32[24,384]{1,0:T(8,128)S(1)}, f32[24,384]{1,0:T(8,128)S(1)}, u32[]{:S(2)}, u32[]{:S(2)}) %collective-permute-start.3) | collective-permute-done | bytes 36896 | tf_op jit(solution)/shard_map/ppermute | solution.py:783
  42.5 0.1 concatenate.14.here_ref
  42.6 3.1 %collective-permute-start.4 = (f32[24,1152]{1,0:T(8,128)S(1)}, f32[24,1152]{1,0:T(8,128)S(1)}, u32[]{:S(2)}, u32[]{:S(2)}) collective-permute-start(f32[24,1152]{1,0:T(8,128)S(1)} %concatenate.14.here_ref), channel_id=1, source_target_pairs={{0,8},{8,16},{16,24},{24,32},{32,40},{40,48},{48,56},{56,64},{64,7... | collective-permute-start | bytes 331784 | tf_op jit(solution)/shard_map/ppermute | solution.py:783
  45.7 1.3 collective-permute-start.5
  47.0 1.0 all-to-all-done
  48.1 0.7 broadcast_in_dim.57
  48.7 9.1 %all-to-all-start.1 = ((f32[8,8,512]{2,1,0:T(8,128)}), f32[8,8,512]{2,1,0:T(8,128)S(1)}, u32[]{:S(2)}, u32[]{:S(2)}) async-start(f32[8,8,512]{2,1,0:T(8,128)} %broadcast_in_dim.57), calls=%async_computation.1 | async-start | bytes 262144 | tf_op jit(solution)/shard_map/all_to_all | solution.py:803
  57.9 0.3 shard_map.69.packed_ref
  58.1 0.0 collective-permute-done.4.below_ref
  58.1 0.0 collective-permute-done.5.above_ref
  58.1 0.8 shard_map.71
  59.0 2.9 %shard_map.70 = (f32[16,64,128]{2,1,0:T(8,128)S(1)}, f32[16,64,128]{2,1,0:T(8,128)S(1)}, f32[16,64,128]{2,1,0:T(8,128)S(1)}) custom-call(s32[3]{0:T(128)S(1)} %pad_add_fusion.place_ref, f32[3]{0:T(128)S(1)} %copy-done.3, f32[24,1152]{1,0:T(8,128)S(1)} %collective-permute-done.4.below_ref, f32[24,1152]{1,0:T(8,128)S(1)} %concatenate.14.here_ref, ...), custom_call_target="tpu_custom_call" | custom-call | flops 1409286144 | bytes 1000000 | tf_op jit(solution)/shard_map/pallas_call | solution.py:726
  61.9 3.7 %all-to-all-done.1.gathered_ref.shifts_ref = f32[8,8,512]{2,1,0:T(8,128)S(1)} async-done(((f32[8,8,512]{2,1,0:T(8,128)}), f32[8,8,512]{2,1,0:T(8,128)S(1)}, u32[]{:S(2)}, u32[]{:S(2)}) %all-to-all-start.1) | async-done | bytes 131104 | tf_op jit(solution)/shard_map/all_to_all | solution.py:803
  65.6 3.6 %shard_map.72 = (f32[6,64,128]{2,1,0:T(8,128)S(1)}, f32[3,64,128]{2,1,0:T(8,128)S(1)}, f32[8,512]{1,0:T(8,128)S(1)}, f32[8,512]{1,0:T(8,128)S(1)}, f32[1,128]{1,0:T(1,128)S(1)}) custom-call(s32[3]{0:T(128)S(1)} %pad_add_fusion.place_ref, f32[3]{0:T(128)S(1)} %copy-done.3, f32[8,8,512]{2,1,0:T(8,128)S(1)} %all-to-all-done.1.gathered_ref.shifts_ref, ...), custom_call_target="tpu_custom_call" | custom-call | flops 603979776 | bytes 1000000 | tf_op jit(solution)/shard_map/pallas_call | solution.py:726
  69.2 0.7 broadcast_in_dim.60
  69.9 18.3 %all-to-all-start.2 = ((f32[128,1,128]{2,1,0:T(1,128)}), f32[128,1,128]{2,1,0:T(1,128)S(1)}, u32[]{:S(2)}, u32[]{:S(2)}) async-start(f32[128,1,128]{2,1,0:T(1,128)} %broadcast_in_dim.60), calls=%async_computation.2 | async-start | bytes 131072 | tf_op jit(solution)/shard_map/all_to_all | solution.py:796
  88.2 3.3 %collective-permute-start.6 = (f32[3,64,128]{2,1,0:T(8,128)S(1)}, f32[3,64,128]{2,1,0:T(8,128)S(1)}, u32[]{:S(2)}, u32[]{:S(2)}) collective-permute-start(f32[3,64,128]{2,1,0:T(8,128)S(1)} %get-tuple-element.32), channel_id=1, source_target_pairs={{0,8},{8,16},{16,24},{24,32},{32,40},{40,48},{48,56},{56,64},{64,7... | collective-permute-start | bytes 294920 | tf_op jit(solution)/shard_map/ppermute | solution.py:783
  91.5 1.3 collective-permute-start.7
  92.8 10.3 %all-to-all-done.2 = f32[128,1,128]{2,1,0:T(1,128)S(1)} async-done(((f32[128,1,128]{2,1,0:T(1,128)}), f32[128,1,128]{2,1,0:T(1,128)S(1)}, u32[]{:S(2)}, u32[]{:S(2)}) %all-to-all-start.2) | async-done | bytes 65568 | tf_op jit(solution)/shard_map/all_to_all | solution.py:796
  103.1 0.6 broadcast_in_dim.61
  103.7 3.5 %all-to-all-start.3 = ((f32[8,8,256]{2,1,0:T(8,128)}), f32[8,8,256]{2,1,0:T(8,128)S(1)}, u32[]{:S(2)}, u32[]{:S(2)}) async-start(f32[8,8,256]{2,1,0:T(8,128)} %broadcast_in_dim.61), calls=%async_computation.3 | async-start | bytes 131072 | tf_op jit(solution)/shard_map/all_to_all | solution.py:803
  107.2 0.0 collective-permute-done.6.below_ref
  107.3 0.0 collective-permute-done.7.above_ref
  107.3 1.6 %shard_map.73.local_ref = f32[6,64,128]{2,1,0:T(8,128)S(1)} custom-call(f32[3]{0:T(128)S(1)} %copy-done.3, f32[6,64,128]{2,1,0:T(8,128)S(1)} %get-tuple-element.31.own_ref, f32[3,64,128]{2,1,0:T(8,128)S(1)} %collective-permute-done.6.below_ref, f32[3,64,128]{2,1,0:T(8,128)S(1)} %collective-permute-done.7.above_ref, ...), custom_call_target="tpu_custom_call" | custom-call | flops 603979776 | bytes 1000000 | tf_op jit(solution)/shard_map/pallas_call | solution.py:726
  108.9 5.3 %all-to-all-done.3.gathered_ref = f32[8,8,256]{2,1,0:T(8,128)S(1)} async-done(((f32[8,8,256]{2,1,0:T(8,128)}), f32[8,8,256]{2,1,0:T(8,128)S(1)}, u32[]{:S(2)}, u32[]{:S(2)}) %all-to-all-start.3) | async-done | bytes 65568 | tf_op jit(solution)/shard_map/all_to_all | solution.py:803
  114.2 2.8 %shard_map.74 = (f32[8,512]{1,0:T(8,128)S(1)}, f32[8,512]{1,0:T(8,128)S(1)}, f32[8,512]{1,0:T(8,128)S(1)}, f32[1,128]{1,0:T(1,128)S(1)}, f32[1,128]{1,0:T(1,128)S(1)}) custom-call(s32[3]{0:T(128)S(1)} %pad_add_fusion.place_ref, f32[3]{0:T(128)S(1)} %copy-done.3, f32[8,8,256]{2,1,0:T(8,128)S(1)} %all-to-all-done.3.gathered_ref, ...), custom_call_target="tpu_custom_call" | custom-call | flops 201326592 | bytes 1000000 | tf_op jit(solution)/shard_map/pallas_call | solution.py:726
  117.1 24.2 %all_to_all.30 = f32[128,1,128]{2,1,0:T(1,128)S(1)} all-to-all(f32[128,1,128]{2,1,0:T(1,128)S(1)} %broadcast_in_dim.63), channel_id=1, replica_groups=mesh['gx'=8,'gy'=16,'gz'=8] {'gy','gz'}, dimensions={0} | all-to-all | bytes 131072 | tf_op jit(solution)/shard_map/all_to_all | solution.py:807
  141.3 8.9 %all_to_all.31.parts_ref = f32[8,1,128]{2,1,0:T(1,128)S(1)} all-to-all(f32[8,1,128]{2,1,0:T(1,128)S(1)} %broadcast_in_dim.64), channel_id=1, replica_groups=mesh['gx'=8,'gy'=16,'gz'=8] {'gx'}, dimensions={0} | all-to-all | bytes 8192 | tf_op jit(solution)/shard_map/all_to_all | solution.py:809
  150.2 1.0 shard_map.75
  (22 shorter events, 0.2 us)
Async XLA Ops:
  0.6 0.7 copy-start.2
  0.6 0.7 copy-start.4
  0.7 0.7 copy-start.3
  0.7 0.7 copy-start.5
  1.4 1.0 copy-start
  3.6 29.5 %collective-permute-start = (f32[8,640]{1,0:T(8,128)S(1)}, f32[8,640]{1,0:T(8,128)S(1)}, u32[]{:S(2)}, u32[]{:S(2)}) collective-permute-start(f32[8,640]{1,0:T(8,128)S(1)} %get-tuple-element.22.right_ref), channel_id=1, source_target_pairs={{0,128},{128,256},{256,384},{384,512},{512,640},{640,768},{768,896... | collective-permute-start | bytes 61448 | tf_op jit(solution)/shard_map/ppermute | solution.py:783
  7.7 25.5 %collective-permute-start.1 = (f32[8,640]{1,0:T(8,128)S(1)}, f32[8,640]{1,0:T(8,128)S(1)}, u32[]{:S(2)}, u32[]{:S(2)}) collective-permute-start(f32[8,640]{1,0:T(8,128)S(1)} %get-tuple-element.22.right_ref), channel_id=1, source_target_pairs={{128,0},{256,128},{384,256},{512,384},{640,512},{768,640},{896,768... | collective-permute-start | bytes 61448 | tf_op jit(solution)/shard_map/ppermute | solution.py:783
  9.7 38.4 %all-to-all-start = ((f32[128,1,128]{2,1,0:T(1,128)}), f32[128,1,128]{2,1,0:T(1,128)S(1)}, u32[]{:S(2)}, u32[]{:S(2)}) async-start(f32[128,1,128]{2,1,0:T(1,128)} %broadcast_in_dim.55), calls=%async_computation | async-start | bytes 131072 | tf_op jit(solution)/shard_map/all_to_all | solution.py:796
  33.3 5.6 %collective-permute-start.2 = (f32[24,384]{1,0:T(8,128)S(1)}, f32[24,384]{1,0:T(8,128)S(1)}, u32[]{:S(2)}, u32[]{:S(2)}) collective-permute-start(f32[24,384]{1,0:T(8,128)S(1)} %get-tuple-element.49), channel_id=1, source_target_pairs={{0,1},{1,2},{2,3},{3,4},{4,5},{5,6},{6,7},{8,9},{9,10},{10,11},{11... | collective-permute-start | bytes 110600 | tf_op jit(solution)/shard_map/ppermute | solution.py:783
  36.8 21.0 %copy-start.1 = (f32[16,64,64]{2,1,0:T(8,128)S(1)}, f32[16,64,64]{2,1,0:T(8,128)}, u32[]{:S(2)}) copy-start(f32[16,64,64]{2,1,0:T(8,128)} %blocks_ref.3) | copy-start | bytes 786436
  36.8 5.7 %collective-permute-start.3 = (f32[24,384]{1,0:T(8,128)S(1)}, f32[24,384]{1,0:T(8,128)S(1)}, u32[]{:S(2)}, u32[]{:S(2)}) collective-permute-start(f32[24,384]{1,0:T(8,128)S(1)} %get-tuple-element.48), channel_id=1, source_target_pairs={{1,0},{2,1},{3,2},{4,3},{5,4},{6,5},{7,6},{9,8},{10,9},{11,10},{12... | collective-permute-start | bytes 110600 | tf_op jit(solution)/shard_map/ppermute | solution.py:783
  42.6 15.5 %collective-permute-start.4 = (f32[24,1152]{1,0:T(8,128)S(1)}, f32[24,1152]{1,0:T(8,128)S(1)}, u32[]{:S(2)}, u32[]{:S(2)}) collective-permute-start(f32[24,1152]{1,0:T(8,128)S(1)} %concatenate.14.here_ref), channel_id=1, source_target_pairs={{0,8},{8,16},{16,24},{24,32},{32,40},{40,48},{48,56},{56,64},{64,7... | collective-permute-start | bytes 331784 | tf_op jit(solution)/shard_map/ppermute | solution.py:783
  45.7 12.4 %collective-permute-start.5 = (f32[24,1152]{1,0:T(8,128)S(1)}, f32[24,1152]{1,0:T(8,128)S(1)}, u32[]{:S(2)}, u32[]{:S(2)}) collective-permute-start(f32[24,1152]{1,0:T(8,128)S(1)} %concatenate.14.here_ref), channel_id=1, source_target_pairs={{8,0},{16,8},{24,16},{32,24},{40,32},{48,40},{56,48},{64,56},{72,6... | collective-permute-start | bytes 331784 | tf_op jit(solution)/shard_map/ppermute | solution.py:783
  48.7 16.9 %all-to-all-start.1 = ((f32[8,8,512]{2,1,0:T(8,128)}), f32[8,8,512]{2,1,0:T(8,128)S(1)}, u32[]{:S(2)}, u32[]{:S(2)}) async-start(f32[8,8,512]{2,1,0:T(8,128)} %broadcast_in_dim.57), calls=%async_computation.1 | async-start | bytes 262144 | tf_op jit(solution)/shard_map/all_to_all | solution.py:803
  69.9 33.2 %all-to-all-start.2 = ((f32[128,1,128]{2,1,0:T(1,128)}), f32[128,1,128]{2,1,0:T(1,128)S(1)}, u32[]{:S(2)}, u32[]{:S(2)}) async-start(f32[128,1,128]{2,1,0:T(1,128)} %broadcast_in_dim.60), calls=%async_computation.2 | async-start | bytes 131072 | tf_op jit(solution)/shard_map/all_to_all | solution.py:796
  88.2 19.1 %collective-permute-start.6 = (f32[3,64,128]{2,1,0:T(8,128)S(1)}, f32[3,64,128]{2,1,0:T(8,128)S(1)}, u32[]{:S(2)}, u32[]{:S(2)}) collective-permute-start(f32[3,64,128]{2,1,0:T(8,128)S(1)} %get-tuple-element.32), channel_id=1, source_target_pairs={{0,8},{8,16},{16,24},{24,32},{32,40},{40,48},{48,56},{56,64},{64,7... | collective-permute-start | bytes 294920 | tf_op jit(solution)/shard_map/ppermute | solution.py:783
  91.5 15.8 %collective-permute-start.7 = (f32[3,64,128]{2,1,0:T(8,128)S(1)}, f32[3,64,128]{2,1,0:T(8,128)S(1)}, u32[]{:S(2)}, u32[]{:S(2)}) collective-permute-start(f32[3,64,128]{2,1,0:T(8,128)S(1)} %get-tuple-element.32), channel_id=1, source_target_pairs={{8,0},{16,8},{24,16},{32,24},{40,32},{48,40},{56,48},{64,56},{72,6... | collective-permute-start | bytes 294920 | tf_op jit(solution)/shard_map/ppermute | solution.py:783
  103.7 10.5 %all-to-all-start.3 = ((f32[8,8,256]{2,1,0:T(8,128)}), f32[8,8,256]{2,1,0:T(8,128)S(1)}, u32[]{:S(2)}, u32[]{:S(2)}) async-start(f32[8,8,256]{2,1,0:T(8,128)} %broadcast_in_dim.61), calls=%async_computation.3 | async-start | bytes 131072 | tf_op jit(solution)/shard_map/all_to_all | solution.py:803

commit v8 on v7

--- a/solution.py
+++ b/solution.py
@@ -596,10 +596,12 @@
             faces = coupling(groups(blocks[at]), view, groups(blocks[at + 2]), weights_ref)
             for g in range(8):
                 image_ref[at, 8 * g : 8 * g + 8] = chosen[part][g] - faces[g]
-    own = (lane & 63) >= 20
-    own = own & ((lane & 63) < 44)
-    for j in range(3):
-        edge_ref[j] = jnp.where(own, image_ref[j], roll(image_ref[j + 3], 32, 1))
+    edge = jnp.zeros((64, 128), F32)
+    for i in range(10):
+        j, half = (i + 1) % 6, (i + 1) // 6
+        taken = (lane >= 12 * i) & (lane < 12 * i + 12)
+        edge = jnp.where(taken, roll(image_ref[j], 12 * i - 26 - 64 * half, 1), edge)
+    edge_ref[...] = edge
     restrict(image_ref, near_inverse_ref, sums_ref, weights_ref, all_ref, cells_ref)
     row = payload(cells_ref[...], place_ref, 1.0 / NODES)
     own_z = gather_own([(smooth_ref[z + 4], 56) for z in range(8)])
@@ -612,6 +614,17 @@
     payload_ref[...] = row + jnp.where(far & ((lane >> 4) == 1), delta, 0.0)
 
 
+def from_edge(edge_ref, j, first):
+    lane = iota((64, 128), 1)
+    result = jnp.zeros((64, 128), F32)
+    for half in range(2):
+        i, start = j - 1 + 6 * half, first + 64 * half
+        if 0 <= i < 10:
+            taken = (lane >= start) & (lane < start + 12)
+            result = jnp.where(taken, roll(edge_ref[...], start - 12 * i, 1), result)
+    return result
+
+
 def near_kernel(
     weights_ref, own_ref, below_ref, above_ref, class_ref, inverse_ref, packed_ref,
     smooth_ref,
@@ -619,8 +632,7 @@
 ):
     lane = iota((64, 128), 1) & 63
     for j in range(6):
-        below = roll(below_ref[j % 3], -24 if j < 3 else -56, 1)
-        above = roll(above_ref[j % 3], 24 if j < 3 else -8, 1)
+        below, above = from_edge(below_ref, j, 2), from_edge(above_ref, j, 50)
         image_ref[j] = jnp.where(lane < 20, below, jnp.where(lane < 44, own_ref[j], above))
         iterate_ref[j] = inverse_ref[j] * image_ref[j]
     for j in (0, 2, 4):
@@ -742,7 +754,7 @@
 ROW = ((1, 128), F32)
 COARSE_SCRATCH = [((10, 24, 128), F32), ((16, 128), F32), ((16, 128), F32)]
 SUM_SCRATCH = [((6, 8, 128), F32), ((24, 128), F32)]
-EDGE = ((3, NODES, 128), F32)
+EDGE = ((NODES, 128), F32)
 PAIR_FLOPS = 2 * 1024 * 384 * 256
 
 

time: 152 us -> 157 us (1.033)
  blocking collectives: 33.1 us -> 70.1 us
  starting transfers between devices: 74.3 us -> 55.4 us
  waiting for transfers between devices: 23.9 us -> 11.7 us
    all_to_all x0 -> x1, blocking collectives: none -> 33.1 us  [gather_cells(): lax.all_to_all(jnp.broadcast_to(row[None], (128, 1, 128)), ('gy', 'gz'),...]
    all_to_all x2 -> x1, starting transfers between devices: 41.8 us -> 23.5 us  [gather_cells(): lax.all_to_all(jnp.broadcast_to(row[None], (128, 1, 128)), ('gy', 'gz'),...]
    all_to_all x2 -> x1, waiting for transfers between devices: 11.3 us -> 0.96 us  [gather_cells(): lax.all_to_all(jnp.broadcast_to(row[None], (128, 1, 128)), ('gy', 'gz'),...]
    all_to_all x2, waiting for transfers between devices: 9.07 us -> 3.74 us  [gather_cells(): lax.all_to_all(jnp.broadcast_to(plane[None], shape), 'gx', 0, 0, tiled=True)]
    all_to_all x1, blocking collectives: 8.89 us -> 13.2 us  [gather_sum(): lax.all_to_all(jnp.broadcast_to(part[None, None], (8, 1, 128)), 'gx', 0,...]
    ppermute x8, waiting for transfers between devices: 3.55 us -> 7.01 us  [shifted(): return lax.ppermute(x, axis, pairs)]
  transfers between devices with their start and end apart: 12 -> 11, of which waited for: 5 -> 4; matrix products, arithmetic and copies ran while one was open for 1% -> 1% of each run, Pallas kernels for 4% -> 4%
where the time goes in v8:
time: 157 us
  blocking collectives  70.1 us (45%)
  starting transfers between devices  55.4 us (35%)
  Pallas kernels  14.3 us (9%)
  waiting for transfers between devices  11.7 us (7%)
  local copies, waits for them, and re-layouts  3.9 us (2%)
    all_to_all x1, blocking collectives, gather_cells(): lax.all_to_all(jnp.broadcast_to(row[None], (128, 1, 128)), ('gy', 'gz'),...  33.1 us
    all_to_all x1, blocking collectives, gather_sum(): lax.all_to_all(jnp.broadcast_to(row[None], (128, 1, 128)), ('gy', 'gz'),...  23.9 us
    all_to_all x1, starting transfers between devices, gather_cells(): lax.all_to_all(jnp.broadcast_to(row[None], (128, 1, 128)), ('gy', 'gz'),...  23.5 us
    ppermute x8, starting transfers between devices, shifted(): return lax.ppermute(x, axis, pairs)  19.4 us
    pallas_call x8, Pallas kernels, call(): pl.pallas_call(body, out_shape=shapes, in_specs=specs, out_specs=[VMEM] *...  14.3 us
    all_to_all x1, blocking collectives, gather_sum(): lax.all_to_all(jnp.broadcast_to(part[None, None], (8, 1, 128)), 'gx', 0,...  13.2 us
    all_to_all x2, starting transfers between devices, gather_cells(): lax.all_to_all(jnp.broadcast_to(plane[None], shape), 'gx', 0, 0, tiled=True)  12.4 us
    ppermute x8, waiting for transfers between devices, shifted(): return lax.ppermute(x, axis, pairs)  7.01 us
  transfers between devices with their start and end apart: 11, of which 4 were waited for; matrix products, arithmetic and copies ran while one was open for 1% of the time, Pallas kernels for 4%

profile of v8, /device:TPU:1, one launch (start us, length us, event | category | flops | bytes accessed | tf_op | source)
XLA Modules:
  0.0 156.6 jit_solution(12334742532968818262)
XLA Ops:
  0.6 0.0 copy-start.2
  0.6 0.0 copy-start.4
  0.7 0.0 copy-start.3
  0.7 0.0 copy-start.5
  0.7 0.1 pad_add_fusion.place_ref
  0.8 0.6 copy-done.2
  1.3 0.0 copy-done.4
  1.4 0.0 copy-done.3
  1.4 1.0 copy-done
  2.4 1.2 shard_map.68
  3.6 4.0 %collective-permute-start = (f32[8,640]{1,0:T(8,128)S(1)}, f32[8,640]{1,0:T(8,128)S(1)}, u32[]{:S(2)}, u32[]{:S(2)}) collective-permute-start(f32[8,640]{1,0:T(8,128)S(1)} %get-tuple-element.22.right_ref), channel_id=1, source_target_pairs={{0,128},{128,256},{256,384},{384,512},{512,640},{640,768},{768,896... | collective-permute-start | bytes 61448 | tf_op jit(solution)/shard_map/ppermute | solution.py:795
  7.7 1.3 collective-permute-start.1
  9.0 0.7 broadcast_in_dim.55
  9.7 23.5 %all-to-all-start = ((f32[128,1,128]{2,1,0:T(1,128)}), f32[128,1,128]{2,1,0:T(1,128)S(1)}, u32[]{:S(2)}, u32[]{:S(2)}) async-start(f32[128,1,128]{2,1,0:T(1,128)} %broadcast_in_dim.55), calls=%async_computation | async-start | bytes 131072 | tf_op jit(solution)/shard_map/all_to_all | solution.py:808
  33.2 0.0 collective-permute-done
  33.2 0.0 collective-permute-done.1
  33.3 3.5 %collective-permute-start.2 = (f32[24,384]{1,0:T(8,128)S(1)}, f32[24,384]{1,0:T(8,128)S(1)}, u32[]{:S(2)}, u32[]{:S(2)}) collective-permute-start(f32[24,384]{1,0:T(8,128)S(1)} %get-tuple-element.49), channel_id=1, source_target_pairs={{0,1},{1,2},{2,3},{3,4},{4,5},{5,6},{6,7},{8,9},{9,10},{10,11},{11... | collective-permute-start | bytes 110600 | tf_op jit(solution)/shard_map/ppermute | solution.py:795
  36.8 0.0 copy-start.1
  36.8 2.1 %collective-permute-start.3 = (f32[24,384]{1,0:T(8,128)S(1)}, f32[24,384]{1,0:T(8,128)S(1)}, u32[]{:S(2)}, u32[]{:S(2)}) collective-permute-start(f32[24,384]{1,0:T(8,128)S(1)} %get-tuple-element.48), channel_id=1, source_target_pairs={{1,0},{2,1},{3,2},{4,3},{5,4},{6,5},{7,6},{9,8},{10,9},{11,10},{12... | collective-permute-start | bytes 110600 | tf_op jit(solution)/shard_map/ppermute | solution.py:795
  38.9 0.0 collective-permute-done.2
  38.9 0.1 slice.37
  39.0 3.5 %collective-permute-done.3 = f32[24,384]{1,0:T(8,128)S(1)} collective-permute-done((f32[24,384]{1,0:T(8,128)S(1)}, f32[24,384]{1,0:T(8,128)S(1)}, u32[]{:S(2)}, u32[]{:S(2)}) %collective-permute-start.3) | collective-permute-done | bytes 36896 | tf_op jit(solution)/shard_map/ppermute | solution.py:795
  42.5 0.1 concatenate.14.here_ref
  42.6 3.1 %collective-permute-start.4 = (f32[24,1152]{1,0:T(8,128)S(1)}, f32[24,1152]{1,0:T(8,128)S(1)}, u32[]{:S(2)}, u32[]{:S(2)}) collective-permute-start(f32[24,1152]{1,0:T(8,128)S(1)} %concatenate.14.here_ref), channel_id=1, source_target_pairs={{0,8},{8,16},{16,24},{24,32},{32,40},{40,48},{48,56},{56,64},{64,7... | collective-permute-start | bytes 331784 | tf_op jit(solution)/shard_map/ppermute | solution.py:795
  45.7 1.3 collective-permute-start.5
  47.0 1.0 all-to-all-done
  48.0 0.7 broadcast_in_dim.57
  48.7 9.1 %all-to-all-start.1 = ((f32[8,8,512]{2,1,0:T(8,128)}), f32[8,8,512]{2,1,0:T(8,128)S(1)}, u32[]{:S(2)}, u32[]{:S(2)}) async-start(f32[8,8,512]{2,1,0:T(8,128)} %broadcast_in_dim.57), calls=%async_computation.1 | async-start | bytes 262144 | tf_op jit(solution)/shard_map/all_to_all | solution.py:815
  57.8 0.3 shard_map.69.packed_ref
  58.1 0.0 collective-permute-done.4.below_ref
  58.1 0.0 collective-permute-done.5.above_ref
  58.1 0.8 shard_map.71
  58.9 2.9 %shard_map.70 = (f32[16,64,128]{2,1,0:T(8,128)S(1)}, f32[16,64,128]{2,1,0:T(8,128)S(1)}, f32[16,64,128]{2,1,0:T(8,128)S(1)}) custom-call(s32[3]{0:T(128)S(1)} %pad_add_fusion.place_ref, f32[3]{0:T(128)S(1)} %copy-done.3, f32[24,1152]{1,0:T(8,128)S(1)} %collective-permute-done.4.below_ref, f32[24,1152]{1,0:T(8,128)S(1)} %concatenate.14.here_ref, ...), custom_call_target="tpu_custom_call" | custom-call | flops 1409286144 | bytes 1000000 | tf_op jit(solution)/shard_map/pallas_call | solution.py:738
  61.8 3.7 %all-to-all-done.1.gathered_ref.shifts_ref = f32[8,8,512]{2,1,0:T(8,128)S(1)} async-done(((f32[8,8,512]{2,1,0:T(8,128)}), f32[8,8,512]{2,1,0:T(8,128)S(1)}, u32[]{:S(2)}, u32[]{:S(2)}) %all-to-all-start.1) | async-done | bytes 131104 | tf_op jit(solution)/shard_map/all_to_all | solution.py:815
  65.6 3.6 %shard_map.72 = (f32[6,64,128]{2,1,0:T(8,128)S(1)}, f32[64,128]{1,0:T(8,128)S(1)}, f32[8,512]{1,0:T(8,128)S(1)}, f32[8,512]{1,0:T(8,128)S(1)}, f32[1,128]{1,0:T(1,128)S(1)}) custom-call(s32[3]{0:T(128)S(1)} %pad_add_fusion.place_ref, f32[3]{0:T(128)S(1)} %copy-done.3, f32[8,8,512]{2,1,0:T(8,128)S(1)} %all-to-all-done.1.gathered_ref.shifts_ref, ...), custom_call_target="tpu_custom_call" | custom-call | flops 603979776 | bytes 1000000 | tf_op jit(solution)/shard_map/pallas_call | solution.py:738
  69.2 33.1 %all_to_all.30 = f32[128,1,128]{2,1,0:T(1,128)S(1)} all-to-all(f32[128,1,128]{2,1,0:T(1,128)S(1)} %broadcast_in_dim.60), channel_id=1, replica_groups=mesh['gx'=8,'gy'=16,'gz'=8] {'gy','gz'}, dimensions={0} | all-to-all | bytes 131072 | tf_op jit(solution)/shard_map/all_to_all | solution.py:808
  102.3 0.6 broadcast_in_dim.61
  103.0 3.3 %all-to-all-start.3 = ((f32[8,8,256]{2,1,0:T(8,128)}), f32[8,8,256]{2,1,0:T(8,128)S(1)}, u32[]{:S(2)}, u32[]{:S(2)}) async-start(f32[8,8,256]{2,1,0:T(8,128)} %broadcast_in_dim.61), calls=%async_computation.3 | async-start | bytes 131072 | tf_op jit(solution)/shard_map/all_to_all | solution.py:815
  106.3 2.6 %collective-permute-start.6 = (f32[64,128]{1,0:T(8,128)S(1)}, f32[64,128]{1,0:T(8,128)S(1)}, u32[]{:S(2)}, u32[]{:S(2)}) collective-permute-start(f32[64,128]{1,0:T(8,128)S(1)} %get-tuple-element.32), channel_id=1, source_target_pairs={{0,8},{8,16},{16,24},{24,32},{32,40},{40,48},{48,56},{56,64},{64,7... | collective-permute-start | bytes 98312 | tf_op jit(solution)/shard_map/ppermute | solution.py:795
  108.9 1.5 collective-permute-start.7
  110.4 0.0 collective-permute-done.6.below_ref
  110.4 3.5 %collective-permute-done.7.above_ref = f32[64,128]{1,0:T(8,128)S(1)} collective-permute-done((f32[64,128]{1,0:T(8,128)S(1)}, f32[64,128]{1,0:T(8,128)S(1)}, u32[]{:S(2)}, u32[]{:S(2)}) %collective-permute-start.7) | collective-permute-done | bytes 32800 | tf_op jit(solution)/shard_map/ppermute | solution.py:795
  113.9 1.6 %shard_map.73.local_ref = f32[6,64,128]{2,1,0:T(8,128)S(1)} custom-call(f32[3]{0:T(128)S(1)} %copy-done.3, f32[6,64,128]{2,1,0:T(8,128)S(1)} %get-tuple-element.31.own_ref, f32[64,128]{1,0:T(8,128)S(1)} %collective-permute-done.6.below_ref, f32[64,128]{1,0:T(8,128)S(1)} %collective-permute-done.7.above_ref, s32[8,128]{1,0:T(8,128)S(1)} %get-tuple-element.27.class_ref, ...), custom_call_target="tpu_custom_call" | custom-call | flops 603979776 | bytes 1000000 | tf_op jit(solution)/shard_map/pallas_call | solution.py:738
  115.5 0.0 all-to-all-done.3.gathered_ref
  115.5 2.9 %shard_map.74 = (f32[8,512]{1,0:T(8,128)S(1)}, f32[8,512]{1,0:T(8,128)S(1)}, f32[8,512]{1,0:T(8,128)S(1)}, f32[1,128]{1,0:T(1,128)S(1)}, f32[1,128]{1,0:T(1,128)S(1)}) custom-call(s32[3]{0:T(128)S(1)} %pad_add_fusion.place_ref, f32[3]{0:T(128)S(1)} %copy-done.3, f32[8,8,256]{2,1,0:T(8,128)S(1)} %all-to-all-done.3.gathered_ref, ...), custom_call_target="tpu_custom_call" | custom-call | flops 201326592 | bytes 1000000 | tf_op jit(solution)/shard_map/pallas_call | solution.py:738
  118.4 23.9 %all_to_all.31 = f32[128,1,128]{2,1,0:T(1,128)S(1)} all-to-all(f32[128,1,128]{2,1,0:T(1,128)S(1)} %broadcast_in_dim.63), channel_id=1, replica_groups=mesh['gx'=8,'gy'=16,'gz'=8] {'gy','gz'}, dimensions={0} | all-to-all | bytes 131072 | tf_op jit(solution)/shard_map/all_to_all | solution.py:819
  142.4 13.2 %all_to_all.32.parts_ref = f32[8,1,128]{2,1,0:T(1,128)S(1)} all-to-all(f32[8,1,128]{2,1,0:T(1,128)S(1)} %broadcast_in_dim.64), channel_id=1, replica_groups=mesh['gx'=8,'gy'=16,'gz'=8] {'gx'}, dimensions={0} | all-to-all | bytes 8192 | tf_op jit(solution)/shard_map/all_to_all | solution.py:821
  155.5 1.0 shard_map.75
  (21 shorter events, 0.2 us)
Async XLA Ops:
  0.6 0.7 copy-start.2
  0.6 0.7 copy-start.4
  0.7 0.7 copy-start.3
  0.7 0.7 copy-start.5
  1.4 1.0 copy-start
  3.6 29.5 %collective-permute-start = (f32[8,640]{1,0:T(8,128)S(1)}, f32[8,640]{1,0:T(8,128)S(1)}, u32[]{:S(2)}, u32[]{:S(2)}) collective-permute-start(f32[8,640]{1,0:T(8,128)S(1)} %get-tuple-element.22.right_ref), channel_id=1, source_target_pairs={{0,128},{128,256},{256,384},{384,512},{512,640},{640,768},{768,896... | collective-permute-start | bytes 61448 | tf_op jit(solution)/shard_map/ppermute | solution.py:795
  7.7 25.5 %collective-permute-start.1 = (f32[8,640]{1,0:T(8,128)S(1)}, f32[8,640]{1,0:T(8,128)S(1)}, u32[]{:S(2)}, u32[]{:S(2)}) collective-permute-start(f32[8,640]{1,0:T(8,128)S(1)} %get-tuple-element.22.right_ref), channel_id=1, source_target_pairs={{128,0},{256,128},{384,256},{512,384},{640,512},{768,640},{896,768... | collective-permute-start | bytes 61448 | tf_op jit(solution)/shard_map/ppermute | solution.py:795
  9.7 38.3 %all-to-all-start = ((f32[128,1,128]{2,1,0:T(1,128)}), f32[128,1,128]{2,1,0:T(1,128)S(1)}, u32[]{:S(2)}, u32[]{:S(2)}) async-start(f32[128,1,128]{2,1,0:T(1,128)} %broadcast_in_dim.55), calls=%async_computation | async-start | bytes 131072 | tf_op jit(solution)/shard_map/all_to_all | solution.py:808
  33.3 5.6 %collective-permute-start.2 = (f32[24,384]{1,0:T(8,128)S(1)}, f32[24,384]{1,0:T(8,128)S(1)}, u32[]{:S(2)}, u32[]{:S(2)}) collective-permute-start(f32[24,384]{1,0:T(8,128)S(1)} %get-tuple-element.49), channel_id=1, source_target_pairs={{0,1},{1,2},{2,3},{3,4},{4,5},{5,6},{6,7},{8,9},{9,10},{10,11},{11... | collective-permute-start | bytes 110600 | tf_op jit(solution)/shard_map/ppermute | solution.py:795
  36.8 21.0 %copy-start.1 = (f32[16,64,64]{2,1,0:T(8,128)S(1)}, f32[16,64,64]{2,1,0:T(8,128)}, u32[]{:S(2)}) copy-start(f32[16,64,64]{2,1,0:T(8,128)} %blocks_ref.3) | copy-start | bytes 786436
  36.8 5.7 %collective-permute-start.3 = (f32[24,384]{1,0:T(8,128)S(1)}, f32[24,384]{1,0:T(8,128)S(1)}, u32[]{:S(2)}, u32[]{:S(2)}) collective-permute-start(f32[24,384]{1,0:T(8,128)S(1)} %get-tuple-element.48), channel_id=1, source_target_pairs={{1,0},{2,1},{3,2},{4,3},{5,4},{6,5},{7,6},{9,8},{10,9},{11,10},{12... | collective-permute-start | bytes 110600 | tf_op jit(solution)/shard_map/ppermute | solution.py:795
  42.6 15.5 %collective-permute-start.4 = (f32[24,1152]{1,0:T(8,128)S(1)}, f32[24,1152]{1,0:T(8,128)S(1)}, u32[]{:S(2)}, u32[]{:S(2)}) collective-permute-start(f32[24,1152]{1,0:T(8,128)S(1)} %concatenate.14.here_ref), channel_id=1, source_target_pairs={{0,8},{8,16},{16,24},{24,32},{32,40},{40,48},{48,56},{56,64},{64,7... | collective-permute-start | bytes 331784 | tf_op jit(solution)/shard_map/ppermute | solution.py:795
  45.7 12.4 %collective-permute-start.5 = (f32[24,1152]{1,0:T(8,128)S(1)}, f32[24,1152]{1,0:T(8,128)S(1)}, u32[]{:S(2)}, u32[]{:S(2)}) collective-permute-start(f32[24,1152]{1,0:T(8,128)S(1)} %concatenate.14.here_ref), channel_id=1, source_target_pairs={{8,0},{16,8},{24,16},{32,24},{40,32},{48,40},{56,48},{64,56},{72,6... | collective-permute-start | bytes 331784 | tf_op jit(solution)/shard_map/ppermute | solution.py:795
  48.7 16.9 %all-to-all-start.1 = ((f32[8,8,512]{2,1,0:T(8,128)}), f32[8,8,512]{2,1,0:T(8,128)S(1)}, u32[]{:S(2)}, u32[]{:S(2)}) async-start(f32[8,8,512]{2,1,0:T(8,128)} %broadcast_in_dim.57), calls=%async_computation.1 | async-start | bytes 262144 | tf_op jit(solution)/shard_map/all_to_all | solution.py:815
  103.0 12.6 %all-to-all-start.3 = ((f32[8,8,256]{2,1,0:T(8,128)}), f32[8,8,256]{2,1,0:T(8,128)S(1)}, u32[]{:S(2)}, u32[]{:S(2)}) async-start(f32[8,8,256]{2,1,0:T(8,128)} %broadcast_in_dim.61), calls=%async_computation.3 | async-start | bytes 131072 | tf_op jit(solution)/shard_map/all_to_all | solution.py:815
  106.3 4.1 %collective-permute-start.6 = (f32[64,128]{1,0:T(8,128)S(1)}, f32[64,128]{1,0:T(8,128)S(1)}, u32[]{:S(2)}, u32[]{:S(2)}) collective-permute-start(f32[64,128]{1,0:T(8,128)S(1)} %get-tuple-element.32), channel_id=1, source_target_pairs={{0,8},{8,16},{16,24},{24,32},{32,40},{40,48},{48,56},{56,64},{64,7... | collective-permute-start | bytes 98312 | tf_op jit(solution)/shard_map/ppermute | solution.py:795
  108.9 5.0 %collective-permute-start.7 = (f32[64,128]{1,0:T(8,128)S(1)}, f32[64,128]{1,0:T(8,128)S(1)}, u32[]{:S(2)}, u32[]{:S(2)}) collective-permute-start(f32[64,128]{1,0:T(8,128)S(1)} %get-tuple-element.32), channel_id=1, source_target_pairs={{8,0},{16,8},{24,16},{32,24},{40,32},{48,40},{56,48},{64,56},{72,6... | collective-permute-start | bytes 98312 | tf_op jit(solution)/shard_map/ppermute | solution.py:795
